TPU v7x, 128 devices: a whole 4x4x4 slice. The times are simulated.
128 devices in a mesh: ep: 8 (over y, core), dp: 16 (over z, x).
Axes of the slice: x: 4, y: 4, z: 4, core: 2. Of those that a mesh axis runs over, the one named last changes fastest.
Arguments:
- hidden_state: bfloat16 [16384, 2048], P(('dp', 'ep')), may hold values from -6 to 6
- out_grad: bfloat16 [16384, 2048], P(('dp', 'ep')), may hold values from -6 to 6
- norm_gain: bfloat16 [2048], replicated, may hold values from 0.5 to 1.5
- expert_ids: int32 [16384, 8], P(('dp', 'ep')), may hold values from 0 to 127, all different within a row; in each aligned block of 128 rows (0 to 127, 128 to 255, ...) at most 10 rows name the same one
- route_weight: bfloat16 [16384, 8], P(('dp', 'ep')), may hold values from 0.019897461 to 0.3984375
- w_gate: bfloat16 [128, 2048, 512], P(('ep', 'dp')), may hold values from -0.125 to 0.125
- w_up: bfloat16 [128, 2048, 512], P(('ep', 'dp')), may hold values from -0.125 to 0.125
- w_down: bfloat16 [128, 512, 2048], P(('ep', 'dp')), may hold values from -0.25 to 0.25
- queries: bfloat16 [16384, 2048], P('dp', 'ep'), may hold values from -6 to 6
- keys: bfloat16 [16384, 2048], P('dp', 'ep'), may hold values from -6 to 6
- values: bfloat16 [16384, 2048], P('dp', 'ep'), may hold values from -6 to 6
- attn_out: bfloat16 [16384, 2048], P('dp', 'ep'), may hold values from -4 to 4
- out_weight: bfloat16 [2048, 2048], P(None, 'ep'), may hold values from -0.125 to 0.125
- doc_start: int32 [16384], P('dp'), may hold values from 0 to 510, as said below
Outputs:
- gate_grad: bfloat16 [16384, 8], P(('dp', 'ep'))
- grad_gate_w: bfloat16 [128, 2048, 512], P(('ep', 'dp'))
- grad_up_w: bfloat16 [128, 2048, 512], P(('ep', 'dp'))
- grad_down_w: bfloat16 [128, 512, 2048], P(('ep', 'dp'))
- residual_grad: bfloat16 [16384, 2048], P(('dp', 'ep'))
- out_weight_grad: bfloat16 [2048, 2048], P('dp', 'ep')
- query_grad: bfloat16 [16384, 2048], P('dp', 'ep')
- key_grad: bfloat16 [16384, 2048], P('dp', 'ep')
- value_grad: bfloat16 [16384, 2048], P('dp', 'ep')
Inputs may be any that keep to these rules, and one draw needn't show every extreme that they name: `expert_ids`: each token names 8 different experts; among the 128 rows of one device (aligned blocks of rows) no expert is named more than 10 times, and in some block some expert exactly 10 times. doc_start of a token is at most its own position in its sequence and equals that of the token before it unless a new document begins there; every document after the first holds two or more tokens.
All inputs are finite; a program needn't handle non-finite values.
Results may differ from a plain program's by a relative error of at most 0.019.
Values may be sent and summed in bfloat16 or wider, within the bound.
A program may use at most 192 MiB of HBM per device.

v0:
```python
import jax
import jax.numpy as jnp
from jax import lax
from jax.sharding import PartitionSpec as P

HEAD_DIM = 128
SEQ = 512


EPS = 1e-06


def per_device(
    hidden_state,
    out_grad,
    norm_gain,
    expert_ids,
    route_weight,
    w_gate,
    w_up,
    w_down,
    queries,
    keys,
    values,
    attn_out,
    out_weight,
    doc_start,
):
    tok_rows, model_width = hidden_state.shape
    top_k = expert_ids.shape[1]
    ep_size = lax.axis_size("ep")
    dp_size = lax.axis_size("dp")
    expert_count = ep_size * dp_size
    slot_caps = 5 * tok_rows * top_k // (4 * expert_count)
    pair_count = tok_rows * top_k
    buffer_rows = expert_count * slot_caps
    hidden_f32 = hidden_state.astype(jnp.float32)
    inv_rms = lax.rsqrt(jnp.mean(hidden_f32 * hidden_f32, axis=1, keepdims=True) + EPS)
    unit_hidden = hidden_f32 * inv_rms
    gain_f32 = norm_gain.astype(jnp.float32)
    normed = (unit_hidden * gain_f32).astype(jnp.bfloat16)
    flat_ids = expert_ids.reshape(pair_count)
    one_hot = (flat_ids[:, None] == jnp.arange(expert_count, dtype=jnp.int32)[None, :]).astype(
        jnp.int32
    )
    earlier = jnp.sum((jnp.cumsum(one_hot, axis=0) - one_hot) * one_hot, axis=1)
    slot_place = flat_ids * slot_caps + earlier
    owner_tok = jnp.arange(pair_count, dtype=jnp.int32) // top_k
    send_rows = (
        jnp.zeros((buffer_rows, model_width), jnp.bfloat16).at[slot_place].set(normed[owner_tok])
    )
    send_grads = (
        jnp.zeros((buffer_rows, model_width), jnp.bfloat16).at[slot_place].set(out_grad[owner_tok])
    )
    send_weights = (
        jnp.zeros((buffer_rows,), jnp.bfloat16).at[slot_place].set(route_weight.reshape(pair_count))
    )
    arrived = (
        lax.all_to_all(
            send_rows.reshape(expert_count, slot_caps, model_width),
            ("ep", "dp"),
            split_axis=0,
            concat_axis=0,
            tiled=True,
        ),
        lax.all_to_all(
            send_grads.reshape(expert_count, slot_caps, model_width),
            ("ep", "dp"),
            split_axis=0,
            concat_axis=0,
            tiled=True,
        ),
        lax.all_to_all(
            send_weights.reshape(expert_count, slot_caps),
            ("ep", "dp"),
            split_axis=0,
            concat_axis=0,
            tiled=True,
        ),
    )
    group_len, head_cols = queries.shape
    head_count = head_cols // HEAD_DIM
    seq_count = group_len // SEQ

    def heads_view(array):
        return array.reshape(seq_count, SEQ, head_count, HEAD_DIM)

    query_rows = heads_view(queries)
    key_rows = heads_view(keys)
    value_rows = heads_view(values)
    positions = jnp.arange(SEQ, dtype=jnp.int32)
    begins = doc_start.reshape(seq_count, SEQ)
    visible = (positions[None, None, :] <= positions[None, :, None]) & (
        positions[None, None, :] >= begins[:, :, None]
    )
    score_scale = HEAD_DIM ** (-0.5)
    scores = (
        jnp.einsum("bqhd,bkhd->bhqk", query_rows, key_rows, preferred_element_type=jnp.float32)
        * score_scale
    )
    masked = jnp.where(visible[:, None], scores, -1e30)
    top_score = jnp.max(masked, axis=3, keepdims=True)
    weights = jnp.where(visible[:, None], jnp.exp(masked - top_score), 0.0)
    probs = weights / jnp.sum(weights, axis=3, keepdims=True)
    probs_bf16 = probs.astype(jnp.bfloat16)
    rows_in = arrived[0].reshape(buffer_rows, model_width)
    rows_grad = arrived[1].reshape(buffer_rows, model_width)
    rows_weight = arrived[2].reshape(buffer_rows, 1).astype(jnp.float32)
    gate_mat = w_gate[0]
    up_mat = w_up[0]
    down_mat = w_down[0]
    gate_pre = jnp.dot(rows_in, gate_mat, preferred_element_type=jnp.float32)
    up_proj = jnp.dot(rows_in, up_mat, preferred_element_type=jnp.float32)
    sigmoid_gate = jax.nn.sigmoid(gate_pre)
    act_bf16 = (gate_pre * sigmoid_gate * up_proj).astype(jnp.bfloat16)
    expert_out = jnp.dot(act_bf16, down_mat, preferred_element_type=jnp.float32)
    gate_score = (
        jnp.sum(rows_grad.astype(jnp.float32) * expert_out, axis=1) * model_width ** (-0.5)
    ).astype(jnp.bfloat16)
    scaled_grad = (rows_weight * rows_grad.astype(jnp.float32)).astype(jnp.bfloat16)
    contract_last = (((1,), (1,)), ((), ()))
    act_grad = lax.dot_general(
        scaled_grad, down_mat, contract_last, preferred_element_type=jnp.float32
    )
    pre_grad = (act_grad * up_proj * sigmoid_gate * (1.0 + gate_pre * (1.0 - sigmoid_gate))).astype(
        jnp.bfloat16
    )
    up_grad = (act_grad * gate_pre * sigmoid_gate).astype(jnp.bfloat16)
    row_grad = (
        lax.dot_general(pre_grad, gate_mat, contract_last, preferred_element_type=jnp.float32)
        + lax.dot_general(up_grad, up_mat, contract_last, preferred_element_type=jnp.float32)
    ).astype(jnp.bfloat16)
    came_back = (
        lax.all_to_all(
            row_grad.reshape(expert_count, slot_caps, model_width),
            ("ep", "dp"),
            split_axis=0,
            concat_axis=0,
            tiled=True,
        ),
        lax.all_to_all(
            gate_score.reshape(expert_count, slot_caps),
            ("ep", "dp"),
            split_axis=0,
            concat_axis=0,
            tiled=True,
        ),
    )
    contract_first = (((0,), (0,)), ((), ()))
    grad_scale = (tok_rows * top_k) ** (-0.5)
    grad_gate_w = (
        lax.dot_general(rows_in, pre_grad, contract_first, preferred_element_type=jnp.float32)
        * grad_scale
    ).astype(jnp.bfloat16)[None]
    grad_up_w = (
        lax.dot_general(rows_in, up_grad, contract_first, preferred_element_type=jnp.float32)
        * grad_scale
    ).astype(jnp.bfloat16)[None]
    grad_down_w = (
        lax.dot_general(act_bf16, scaled_grad, contract_first, preferred_element_type=jnp.float32)
        * grad_scale
    ).astype(jnp.bfloat16)[None]
    back_rows = (
        came_back[0]
        .reshape(buffer_rows, model_width)[slot_place]
        .reshape(tok_rows, top_k, model_width)
    )
    normed_grad = jnp.sum(back_rows.astype(jnp.float32), axis=1)
    gate_grad = came_back[1].reshape(buffer_rows)[slot_place].reshape(tok_rows, top_k)
    scaled_norm = normed_grad * gain_f32
    residual_f32 = out_grad.astype(jnp.float32) + inv_rms * (
        scaled_norm - unit_hidden * jnp.mean(scaled_norm * unit_hidden, axis=1, keepdims=True)
    )
    residual_grad = residual_f32.astype(jnp.bfloat16)
    group_rows = lax.all_gather(residual_grad, "ep", axis=0, tiled=True)
    attn_grad = jnp.dot(group_rows, out_weight, preferred_element_type=jnp.float32).astype(
        jnp.bfloat16
    )
    weight_total = lax.psum_scatter(
        lax.dot_general(
            group_rows, attn_out, contract_first, preferred_element_type=jnp.float32
        ).astype(jnp.bfloat16),
        "dp",
        scatter_dimension=0,
        tiled=True,
    ).astype(jnp.float32)
    out_weight_grad = (weight_total * (group_len * dp_size) ** (-0.5)).astype(jnp.bfloat16)
    grad_heads = heads_view(attn_grad)
    delta = jnp.swapaxes(
        jnp.sum(grad_heads.astype(jnp.float32) * heads_view(attn_out).astype(jnp.float32), axis=3),
        1,
        2,
    )
    prob_grad = jnp.einsum(
        "bqhd,bkhd->bhqk", grad_heads, value_rows, preferred_element_type=jnp.float32
    )
    score_grad = (probs * (prob_grad - delta[:, :, :, None])).astype(jnp.bfloat16)
    query_grad = (
        (
            jnp.einsum("bhqk,bkhd->bqhd", score_grad, key_rows, preferred_element_type=jnp.float32)
            * score_scale
        )
        .astype(jnp.bfloat16)
        .reshape(group_len, head_cols)
    )
    key_grad = (
        (
            jnp.einsum(
                "bhqk,bqhd->bkhd", score_grad, query_rows, preferred_element_type=jnp.float32
            )
            * score_scale
        )
        .astype(jnp.bfloat16)
        .reshape(group_len, head_cols)
    )
    value_grad = (
        jnp.einsum("bhqk,bqhd->bkhd", probs_bf16, grad_heads, preferred_element_type=jnp.float32)
        .astype(jnp.bfloat16)
        .reshape(group_len, head_cols)
    )
    return (
        gate_grad,
        grad_gate_w,
        grad_up_w,
        grad_down_w,
        residual_grad,
        out_weight_grad,
        query_grad,
        key_grad,
        value_grad,
    )


def solution(mesh):
    in_specs = (
        P(("dp", "ep"), None),
        P(("dp", "ep"), None),
        P(),
        P(("dp", "ep"), None),
        P(("dp", "ep"), None),
        P(("ep", "dp"), None, None),
        P(("ep", "dp"), None, None),
        P(("ep", "dp"), None, None),
        P("dp", "ep"),
        P("dp", "ep"),
        P("dp", "ep"),
        P("dp", "ep"),
        P(None, "ep"),
        P("dp"),
    )
    out_specs = (
        P(("dp", "ep"), None),
        P(("ep", "dp"), None, None),
        P(("ep", "dp"), None, None),
        P(("ep", "dp"), None, None),
        P(("dp", "ep"), None),
        P("dp", "ep"),
        P("dp", "ep"),
        P("dp", "ep"),
        P("dp", "ep"),
    )
    return jax.shard_map(
        per_device, mesh=mesh, in_specs=in_specs, out_specs=out_specs, check_vma=False
    )
```

profile of v0, /device:TPU:1, one launch (start us, length us, event | category | flops | bytes accessed | tf_op | source)
XLA Modules:
  0.0 653.2 jit_solution(4592148170669482275)
XLA Ops:
  7.2 0.9 copy.54
  11.0 7.6 %scatter_custom_fusion.2 = bf16[1280]{0:T(1024)(128)(2,1)S(1)} fusion(s32[1024]{0:T(1024)S(1)} %bitcast.88, bf16[1024]{0:T(1024)(128)(2,1)S(1)} %reshape.316, bf16[]{:T(256)} %constant.19.clone.1), kind=kCustom, calls=%fused_computation.106 | custom fusion | bytes 2562 | tf_op jit(solution)/shard_map/scatter | solution.py:56
  19.4 11.8 %all-to-all-start.3 = ((bf16[128,1,10]{2,1,0:T(2,128)(2,1)}), bf16[128,1,10]{2,1,0:T(2,128)(2,1)S(1)}, u32[]{:S(2)}, u32[]{:S(2)}) async-start(bf16[128,1,10]{2,1,0:T(2,128)(2,1)} %all_to_all.25), calls=%async_computation.3 | async-start | bytes 131072 | tf_op jit(solution)/shard_map/all_to_all | solution.py:73
  31.3 23.4 %scatter_custom_fusion = bf16[1280,2048]{1,0:T(8,128)(2,1)} fusion(s32[1024]{0:T(1024)S(1)} %bitcast.89, bf16[128,2048]{1,0:T(8,128)(2,1)} %param.15, s32[1024]{0:T(1024)S(1)} %broadcast_clamp_fusion.1, bf16[]{:T(256)} %constant.19.clone.1), kind=kCustom, calls=%fused_computation.17 | custom fusion | bytes 5243392 | tf_op jit(solution)/shard_map/scatter | solution.py:53
  54.6 9.5 %reshape.244 = bf16[128,10,2048]{2,1,0:T(8,128)(2,1)} reshape(bf16[1280,2048]{1,0:T(8,128)(2,1)} %scatter_custom_fusion) | data formatting | bytes 10485760 | tf_op jit(solution)/shard_map/reshape | solution.py:67
  64.2 10.9 %all-to-all-start = ((bf16[128,10,2048]{2,1,0:T(8,128)(2,1)}), bf16[128,10,2048]{2,1,0:T(8,128)(2,1)}, u32[]{:S(2)}, u32[]{:S(2)}) async-start(bf16[128,10,2048]{2,1,0:T(8,128)(2,1)} %reshape.244), calls=%async_computation | async-start | bytes 16777216 | tf_op jit(solution)/shard_map/all_to_all | solution.py:66
  75.5 23.3 %scatter_custom_fusion.1 = bf16[1280,2048]{1,0:T(8,128)(2,1)} fusion(s32[1024]{0:T(1024)S(1)} %bitcast.90, bf16[128,2048]{1,0:T(8,128)(2,1)S(1)} %fusion.42, s32[1024]{0:T(1024)S(1)} %broadcast_clamp_fusion.1, bf16[]{:T(256)} %constant.19.clone.1), kind=kCustom, calls=%fused_computation.15 | custom fusion | bytes 5242882 | tf_op jit(solution)/shard_map/scatter | solution.py:50
  98.9 9.5 %reshape.245 = bf16[128,10,2048]{2,1,0:T(8,128)(2,1)} reshape(bf16[1280,2048]{1,0:T(8,128)(2,1)} %scatter_custom_fusion.1) | data formatting | bytes 10485760 | tf_op jit(solution)/shard_map/reshape | solution.py:60
  108.4 66.6 %all-to-all-done = bf16[128,10,2048]{2,1,0:T(8,128)(2,1)} async-done(((bf16[128,10,2048]{2,1,0:T(8,128)(2,1)}), bf16[128,10,2048]{2,1,0:T(8,128)(2,1)}, u32[]{:S(2)}, u32[]{:S(2)}) %all-to-all-start) | async-done | bytes 5242912 | tf_op jit(solution)/shard_map/all_to_all | solution.py:66
  175.0 17.6 %all-to-all-start.1 = ((bf16[128,10,2048]{2,1,0:T(8,128)(2,1)}), bf16[128,10,2048]{2,1,0:T(8,128)(2,1)}, u32[]{:S(2)}, u32[]{:S(2)}) async-start(bf16[128,10,2048]{2,1,0:T(8,128)(2,1)} %reshape.245), calls=%async_computation.1 | async-start | bytes 16777216 | tf_op jit(solution)/shard_map/all_to_all | solution.py:59
  192.7 8.2 %multiply_convert_fusion = bf16[128,10,2048]{2,1,0:T(8,128)(2,1)} fusion(f32[128,10]{1,0:T(8,128)S(1)} %bitcast.86, bf16[128,10,2048]{2,1,0:T(8,128)(2,1)} %all-to-all-done), kind=kLoop, calls=%fused_computation.8 | loop fusion | flops 7864320 | bytes 10490880 | tf_op jit(solution)/shard_map/convert_element_type | solution.py:120
  200.8 9.8 %convert_element_type.157 = bf16[1280,2048]{1,0:T(8,128)(2,1)} reshape(bf16[128,10,2048]{2,1,0:T(8,128)(2,1)} %multiply_convert_fusion) | data formatting | bytes 10485760 | tf_op jit(solution)/shard_map/convert_element_type | solution.py:120
  210.7 81.6 %all-to-all-done.1 = bf16[128,10,2048]{2,1,0:T(8,128)(2,1)} async-done(((bf16[128,10,2048]{2,1,0:T(8,128)(2,1)}), bf16[128,10,2048]{2,1,0:T(8,128)(2,1)}, u32[]{:S(2)}, u32[]{:S(2)}) %all-to-all-start.1) | async-done | bytes 5242912 | tf_op jit(solution)/shard_map/all_to_all | solution.py:59
  292.3 9.8 %reshape.246 = bf16[1280,2048]{1,0:T(8,128)(2,1)} reshape(bf16[128,10,2048]{2,1,0:T(8,128)(2,1)} %all-to-all-done.1) | data formatting | bytes 10485760 | tf_op jit(solution)/shard_map/reshape | solution.py:106
  302.2 5.6 fusion.17
  307.8 2.9 fusion.21
  310.7 5.3 multiply_convert_fusion.11
  316.0 3.0 fusion.19
  319.0 5.1 add_convert_fusion
  324.1 9.5 %reshape.250 = bf16[128,10,2048]{2,1,0:T(8,128)(2,1)} reshape(bf16[1280,2048]{1,0:T(8,128)(2,1)} %add_convert_fusion) | data formatting | bytes 10485760 | tf_op jit(solution)/shard_map/reshape | solution.py:135
  333.6 19.0 %all-to-all-start.4 = ((bf16[128,10,2048]{2,1,0:T(8,128)(2,1)}), bf16[128,10,2048]{2,1,0:T(8,128)(2,1)}, u32[]{:S(2)}, u32[]{:S(2)}) async-start(bf16[128,10,2048]{2,1,0:T(8,128)(2,1)} %reshape.250), calls=%async_computation.4 | async-start | bytes 16777216 | tf_op jit(solution)/shard_map/all_to_all | solution.py:134
  352.7 99.7 %all-to-all-done.4 = bf16[128,10,2048]{2,1,0:T(8,128)(2,1)} async-done(((bf16[128,10,2048]{2,1,0:T(8,128)(2,1)}), bf16[128,10,2048]{2,1,0:T(8,128)(2,1)}, u32[]{:S(2)}, u32[]{:S(2)}) %all-to-all-start.4) | async-done | bytes 5242912 | tf_op jit(solution)/shard_map/all_to_all | solution.py:134
  452.4 9.8 %reshape.251 = bf16[1280,2048]{1,0:T(8,128)(2,1)} reshape(bf16[128,10,2048]{2,1,0:T(8,128)(2,1)} %all-to-all-done.4) | data formatting | bytes 10485760 | tf_op jit(solution)/shard_map/reshape | solution.py:165
  462.2 12.0 %gather_fusion.1 = bf16[1024,2048]{1,0:T(8,128)(2,1)} fusion(bf16[1280,2048]{1,0:T(8,128)(2,1)} %reshape.251, s32[1024]{0:T(1024)S(1)} %broadcast_clamp_fusion), kind=kCustom, calls=%fused_computation.3 | custom fusion | bytes 8392704 | tf_op jit(solution)/shard_map/gather | solution.py:164
  474.2 5.1 convert_reduce_fusion
  479.7 1.2 fusion.47
  481.0 1.2 reshape.253
  482.7 2.0 reshape.255
  485.9 4.3 fusion.64
  490.5 11.7 %reshape.259 = f32[1280,2048]{1,0:T(8,128)} reshape(bf16[128,10,2048]{2,1,0:T(8,128)(2,1)} %all-to-all-done) | data formatting | bytes 15728640 | tf_op jit(solution)/shard_map/convert_element_type | solution.py:118
  502.3 8.0 %multiply_reduce_fusion = f32[1280]{0:T(1024)S(1)} fusion(f32[1280,2048]{1,0:T(8,128)} %reshape.259, bf16[1280,512]{1,0:T(8,128)(2,1)} %get-tuple-element.29, bf16[1,512,2048]{2,1,0:T(8,128)(2,1)} %param.21), kind=kOutput, calls=%fused_computation.11 | convolution fusion | flops 2689596160 | bytes 13898752 | tf_op jit(solution)/shard_map/dot_general | solution.py:116
  511.1 19.0 %all-to-all-start.2 = ((bf16[128,1,10]{2,1,0:T(2,128)(2,1)}), bf16[128,1,10]{2,1,0:T(2,128)(2,1)S(1)}, u32[]{:S(2)}, u32[]{:S(2)}) async-start(bf16[128,1,10]{2,1,0:T(2,128)(2,1)} %convert_element_type.191), calls=%async_computation.2 | async-start | bytes 131072 | tf_op jit(solution)/shard_map/all_to_all | solution.py:141
  530.2 7.2 %fusion.9 = bf16[1,2048,512]{2,1,0:T(8,128)(2,1)} fusion(bf16[1280,2048]{1,0:T(8,128)(2,1)} %reshape.246, bf16[1280,512]{1,0:T(8,128)(2,1)} %copy-done.13), kind=kOutput, calls=%fused_computation.27 | convolution fusion | flops 2686451712 | bytes 8650752 | tf_op jit(solution)/shard_map/dot_general | solution.py:156
  537.4 8.3 %fusion.10 = bf16[1,512,2048]{2,1,0:T(8,128)(2,1)} fusion(bf16[1280,512]{1,0:T(8,128)(2,1)S(1)} %copy-done.5, f32[1280,2048]{1,0:T(8,128)} %reshape.259, f32[1280]{0:T(1024)S(1)} %reshape.261), kind=kOutput, calls=%fused_computation.28 | convolution fusion | flops 2691694592 | bytes 13898752 | tf_op jit(solution)/shard_map/dot_general | solution.py:160
  545.7 6.7 %fusion.8 = bf16[1,2048,512]{2,1,0:T(8,128)(2,1)} fusion(bf16[1280,2048]{1,0:T(8,128)(2,1)} %reshape.246, bf16[1280,512]{1,0:T(8,128)(2,1)S(1)} %copy-done.15), kind=kOutput, calls=%fused_computation.26 | convolution fusion | flops 2686451712 | bytes 8650752 | tf_op jit(solution)/shard_map/dot_general | solution.py:152
  552.7 6.8 %gather_fusion = bf16[1024]{0:T(1024)(128)(2,1)S(1)} fusion(bf16[1280]{0:T(1024)(128)(2,1)S(1)} %reshape.247, s32[1024]{0:T(1024)S(1)} %broadcast_clamp_fusion), kind=kCustom, calls=%fused_computation.2 | custom fusion | bytes 8192 | tf_op jit(solution)/shard_map/gather | solution.py:169
  560.3 4.5 convolution_convert_fusion.1
  564.8 1.2 reshape.254
  566.0 1.1 copy.72
  567.1 4.5 convolution_convert_fusion
  571.6 3.2 fusion.39
  574.8 1.1 copy.74
  575.9 1.2 multiply_reduce_fusion.1
  577.3 3.2 multiply_convert_fusion.3
  581.8 1.0 fusion.38
  584.2 1.2 copy_bitcast_fusion
  585.4 59.4 %reduce-scatter.2.cloned.1.call-done = bf16[128,256]{1,0:T(8,128)(2,1)} async-done(((bf16[2048,256]{1,0:T(8,128)(2,1)}), bf16[128,256]{1,0:T(8,128)(2,1)}) %reduce-scatter.2.cloned.1.call-update) | async-done | bytes 65552 | tf_op jit(solution)/shard_map/reduce_scatter | solution.py:179
  644.7 1.5 multiply_convert_fusion.14
  (90 shorter events, 11.5 us)
Async XLA Ops:
  7.2 300.6 %copy-start = (bf16[1,2048,512]{2,1,0:T(8,128)(2,1)S(1)}, bf16[1,2048,512]{2,1,0:T(8,128)(2,1)}, u32[]{:S(2)}) copy-start(bf16[1,2048,512]{2,1,0:T(8,128)(2,1)} %param.19) | copy-start | bytes 6291460
  19.4 44.8 %all-to-all-start.3 = ((bf16[128,1,10]{2,1,0:T(2,128)(2,1)}), bf16[128,1,10]{2,1,0:T(2,128)(2,1)S(1)}, u32[]{:S(2)}, u32[]{:S(2)}) async-start(bf16[128,1,10]{2,1,0:T(2,128)(2,1)} %all_to_all.25), calls=%async_computation.3 | async-start | bytes 131072 | tf_op jit(solution)/shard_map/all_to_all | solution.py:73
  64.2 10.9 %copy-start.9 = (bf16[2048]{0:T(1024)(128)(2,1)S(1)}, bf16[2048]{0:T(1024)(128)(2,1)}, u32[]{:S(2)}) copy-start(bf16[2048]{0:T(1024)(128)(2,1)} %param.16) | copy-start | bytes 12292
  64.2 10.9 %copy-start.2 = (bf16[128,2048]{1,0:T(8,128)(2,1)S(1)}, bf16[128,2048]{1,0:T(8,128)(2,1)}, u32[]{:S(2)}) copy-start(bf16[128,2048]{1,0:T(8,128)(2,1)} %param.14) | copy-start | bytes 1572868
  64.2 110.8 %all-to-all-start = ((bf16[128,10,2048]{2,1,0:T(8,128)(2,1)}), bf16[128,10,2048]{2,1,0:T(8,128)(2,1)}, u32[]{:S(2)}, u32[]{:S(2)}) async-start(bf16[128,10,2048]{2,1,0:T(8,128)(2,1)} %reshape.244), calls=%async_computation | async-start | bytes 16777216 | tf_op jit(solution)/shard_map/all_to_all | solution.py:66
  175.0 117.4 %all-to-all-start.1 = ((bf16[128,10,2048]{2,1,0:T(8,128)(2,1)}), bf16[128,10,2048]{2,1,0:T(8,128)(2,1)}, u32[]{:S(2)}, u32[]{:S(2)}) async-start(bf16[128,10,2048]{2,1,0:T(8,128)(2,1)} %reshape.245), calls=%async_computation.1 | async-start | bytes 16777216 | tf_op jit(solution)/shard_map/all_to_all | solution.py:59
  302.2 5.6 copy-start.3
  302.2 8.5 %slice-start = ((s8[5242880]{0:T(1024)(128)(4,1)}), s8[4194304]{0:T(1024)(128)(4,1)S(1)}, s32[]{:S(2)}) async-start(s8[5242880]{0:T(1024)(128)(4,1)} %bitcast.79), calls=%async_computation.8 | async-start | bytes 8388608
  307.8 2.9 slice-start.1
  307.8 2.9 copy-start.12
  316.0 3.0 copy-start.14
  316.0 3.0 copy-start.13
  316.0 3.0 copy-start.11
  333.6 118.7 %all-to-all-start.4 = ((bf16[128,10,2048]{2,1,0:T(8,128)(2,1)}), bf16[128,10,2048]{2,1,0:T(8,128)(2,1)}, u32[]{:S(2)}, u32[]{:S(2)}) async-start(bf16[128,10,2048]{2,1,0:T(8,128)(2,1)} %reshape.250), calls=%async_computation.4 | async-start | bytes 16777216 | tf_op jit(solution)/shard_map/all_to_all | solution.py:134
  352.7 207.6 %all-gather.2.cloned.1.call-start = ((), (), s32[]{:S(2)}) async-start(), calls=%async_computation.6 | async-start | bytes 4718592 | tf_op jit(solution)/shard_map/all_gather | solution.py:175
  474.2 5.5 copy-start.6
  474.2 6.7 %copy-start.8 = (bf16[1024,256]{1,0:T(8,128)(2,1)S(1)}, bf16[1024,256]{1,0:T(8,128)(2,1)}, u32[]{:S(2)}) copy-start(bf16[1024,256]{1,0:T(8,128)(2,1)} %param.22) | copy-start | bytes 1572868
  479.3 2.9 copy-start.10
  479.3 2.9 copy-start.7
  511.1 41.3 %all-to-all-start.2 = ((bf16[128,1,10]{2,1,0:T(2,128)(2,1)}), bf16[128,1,10]{2,1,0:T(2,128)(2,1)S(1)}, u32[]{:S(2)}, u32[]{:S(2)}) async-start(bf16[128,1,10]{2,1,0:T(2,128)(2,1)} %convert_element_type.191), calls=%async_computation.2 | async-start | bytes 131072 | tf_op jit(solution)/shard_map/all_to_all | solution.py:141
  530.1 114.6 %reduce-scatter.2.cloned.1.call-start = ((), (), s32[]{:S(2)}) async-start(), calls=%async_computation.7 | async-start | bytes 1114112 | tf_op jit(solution)/shard_map/reduce_scatter | solution.py:179
  530.1 7.2 %copy-start.5 = (bf16[1280,512]{1,0:T(8,128)(2,1)S(1)}, bf16[1280,512]{1,0:T(8,128)(2,1)}, u32[]{:S(2)}) copy-start(bf16[1280,512]{1,0:T(8,128)(2,1)} %get-tuple-element.29) | copy-start | bytes 3932164
  537.4 8.3 %copy-start.15 = (bf16[1280,512]{1,0:T(8,128)(2,1)S(1)}, bf16[1280,512]{1,0:T(8,128)(2,1)}, u32[]{:S(2)}) copy-start(bf16[1280,512]{1,0:T(8,128)(2,1)} %copy-done.14) | copy-start | bytes 3932164
  580.5 3.7 copy-start.4
  580.5 65.7 %copy-start.1 = (bf16[1,2048,512]{2,1,0:T(8,128)(2,1)S(1)}, bf16[1,2048,512]{2,1,0:T(8,128)(2,1)}, u32[]{:S(2)}) copy-start(bf16[1,2048,512]{2,1,0:T(8,128)(2,1)} %param.19) | copy-start | bytes 6291460
Sparse Core Ops, SparseCore 0:
  481.0 42.8 all-gather.1
  571.8 72.9 reduce-scatter.1
where the time goes:
time: 661 us; the launch traced here: 653 us
  waiting for transfers between devices  307 us (46%)
  local copies, waits for them, and re-layouts  159 us (24%)
  starting transfers between devices  78.5 us (12%)
  matrix products  69.9 us (11%)
  other arithmetic  24.4 us (4%)
  between operations  14.7 us (2%)
    all_to_all x1, waiting for transfers between devices, per_device(): lax.all_to_all(row_grad.reshape(expert_count, slot_caps, model_width), ('...  99.7 us
    all_to_all x1, waiting for transfers between devices, per_device(): lax.all_to_all(send_rows.reshape(expert_count, slot_caps, model_width), (...  81.6 us
    all_to_all x1, waiting for transfers between devices, per_device(): lax.all_to_all(send_grads.reshape(expert_count, slot_caps, model_width),...  66.6 us
    reduce_scatter x1, waiting for transfers between devices, per_device(): lax.psum_scatter(lax.dot_general(group_rows, attn_out, contract_first, pr...  59.4 us
    scatter x2, local copies, waits for them, and re-layouts, per_device(): jnp.zeros((buffer_rows, model_width), jnp.bfloat16).at[slot_place]  46.7 us
    all_to_all x1, starting transfers between devices, per_device(): lax.all_to_all(row_grad.reshape(expert_count, slot_caps, model_width), ('...  19 us
    all_to_all x1, starting transfers between devices, per_device(): lax.all_to_all(gate_score.reshape(expert_count, slot_caps), ('ep', 'dp'),...  19 us
    all_to_all x1, starting transfers between devices, per_device(): lax.all_to_all(send_rows.reshape(expert_count, slot_caps, model_width), (...  17.6 us
  transfers between devices with their start and end apart: 7, of which 4 were waited for; matrix products, arithmetic and copies ran while one was open for 24% of the time, Pallas kernels for 0%

commit v1 on v0

v1 whole, which is shorter than its diff:
```python
import functools

import jax
import jax.numpy as jnp
import numpy as np
from jax import lax
from jax.experimental import pallas as pl
from jax.experimental.pallas import tpu as pltpu
from jax.sharding import PartitionSpec as P

HEAD_DIM = 128
SEQ = 512
EPS = 1e-06
LANES = 128
CHUNKS = 16
F32 = jnp.float32
BF16 = jnp.bfloat16
LAST = (((1,), (1,)), ((), ()))
FIRST = (((0,), (0,)), ((), ()))
PACK_EXTRA = 8
VMEM_LIMIT = 56 * 1024 * 1024


def swap_matrix():
    index = np.arange(256)
    matrix = np.zeros((256, 256), np.float32)
    matrix[(index % 16) * 16 + index // 16, index] = 1.0
    return jnp.asarray(matrix, BF16)


def call(kernel, out_shape, flops=0, moved=0, **kwargs):
    return pl.pallas_call(
        kernel,
        out_shape=out_shape,
        compiler_params=pltpu.CompilerParams(vmem_limit_bytes=VMEM_LIMIT),
        cost_estimate=pl.CostEstimate(flops=flops, bytes_accessed=moved, transcendentals=0),
        **kwargs,
    )


def whole(shape):
    return pl.BlockSpec(shape, lambda *_: (0,) * len(shape))


def tiles_to_rows(get_tiles, swap, out_ref, groups):
    for group in range(groups):
        pair = jnp.concatenate([get_tiles(2 * group), get_tiles(2 * group + 1)], axis=1)
        turned = jnp.dot(swap, pair, preferred_element_type=F32).astype(BF16)
        for chunk in range(CHUNKS):
            cols = slice(chunk * LANES, (chunk + 1) * LANES)
            rows = turned[chunk * 16 : (chunk + 1) * 16]
            out_ref[group * 32 : group * 32 + 16, cols] = rows[:, :LANES]
            out_ref[group * 32 + 16 : group * 32 + 32, cols] = rows[:, LANES:]


def slots_kernel(caps, ids_ref, weight_ref, table_ref, scale_ref, slot_ref):
    tokens, top_k = ids_ref.shape
    experts = LANES
    lane = lax.broadcasted_iota(jnp.int32, (tokens, experts), 1)
    row = lax.broadcasted_iota(jnp.int32, (tokens, experts), 0)
    ids = ids_ref[...]
    weight = weight_ref[...].astype(F32)
    chosen = jnp.zeros((tokens, experts), F32)
    weights = jnp.zeros((tokens, experts), F32)
    for k in range(top_k):
        hit = ids[:, k : k + 1] == lane
        chosen = jnp.where(hit, 1.0, chosen)
        weights = jnp.where(hit, weight[:, k : k + 1], weights)
    lower = jnp.where(lane < row, 1.0, 0.0).astype(BF16)
    counts = jnp.dot(lower, chosen.astype(BF16), preferred_element_type=F32)
    table = jnp.zeros((16, experts), F32)
    scales = jnp.zeros((16, experts), F32)
    sub = lax.broadcasted_iota(jnp.int32, (16, experts), 0)
    from_end = (row - tokens).astype(F32)
    for place in range(caps):
        mask = (chosen > 0.5) & (jnp.abs(counts - place) < 0.5)
        token = jnp.sum(jnp.where(mask, from_end, 0.0), axis=0, keepdims=True) + tokens
        scale = jnp.sum(jnp.where(mask, weights, 0.0), axis=0, keepdims=True)
        table = jnp.where(sub == place, token, table)
        scales = jnp.where(sub == place, scale, scales)
    table_ref[...] = table.astype(jnp.int32)
    scale_ref[...] = scales
    slot = jnp.zeros((tokens, experts), F32)
    for k in range(top_k):
        place = jnp.sum(jnp.where(ids[:, k : k + 1] == lane, counts, 0.0), axis=1, keepdims=True)
        slot = jnp.where(lane == k, place, slot)
    slot_ref[...] = slot.astype(jnp.int32)


def pack_rows_kernel(caps, table_ref, hidden_ref, gain_ref, out_ref, normed):
    tokens = hidden_ref.shape[0]
    step = pl.program_id(0)

    @pl.when(step == 0)
    def _():
        gain = gain_ref[...].astype(F32)[None]
        for start in range(0, tokens, 16):
            hidden = hidden_ref[start : start + 16].astype(F32)
            mean = jnp.sum(
                jnp.sum(hidden * hidden, axis=2, keepdims=True), axis=1, keepdims=True
            ) * (1.0 / (CHUNKS * LANES))
            normed[start : start + 16] = (hidden * lax.rsqrt(mean + EPS) * gain).astype(BF16)
        normed[tokens] = jnp.zeros((CHUNKS, LANES), BF16)

    def fill(dest, carry):
        for place in range(caps):
            out_ref[dest * caps + place] = normed[table_ref[place, step * 16 + dest]]
        return carry

    lax.fori_loop(0, 16, fill, 0)


def pack_grads_kernel(caps, table_ref, scale_ref, grad_ref, out_ref):
    tokens = grad_ref.shape[0]
    step = pl.program_id(0)

    def fill(dest, carry):
        for place in range(caps):
            token = jnp.minimum(table_ref[place, step * 16 + dest], tokens - 1)
            scale = scale_ref[place, step * 16 + dest]
            out_ref[dest * caps + place] = (grad_ref[token].astype(F32) * scale).astype(BF16)
        return carry

    lax.fori_loop(0, 16, fill, 0)


def expert_up_kernel(tile_ref, swap_ref, gate_w_ref, up_w_ref, row_ref, act_ref, da_ref, db_ref):
    rows = row_ref.shape[0]
    tiles_to_rows(
        lambda i: tile_ref[i * 256 : (i + 1) * 256], swap_ref[...], row_ref, rows // 32
    )
    gate = jnp.dot(row_ref[...], gate_w_ref[0], preferred_element_type=F32)
    up = jnp.dot(row_ref[...], up_w_ref[0], preferred_element_type=F32)
    sig = 1.0 / (1.0 + jnp.exp(-gate))
    silu = gate * sig
    act_ref[...] = (silu * up).astype(BF16)
    da_ref[...] = (up * sig * (1.0 + gate * (1.0 - sig))).astype(BF16)
    db_ref[...] = silu.astype(BF16)


def expert_down_kernel(
    caps,
    tile_ref,
    swap_ref,
    gather_ref,
    spread_ref,
    gate_w_ref,
    up_w_ref,
    down_w_ref,
    act_ref,
    da_ref,
    db_ref,
    grad_ref,
    pre_ref,
    upg_ref,
    back_ref,
    rowg,
):
    rows = grad_ref.shape[0]
    swap = swap_ref[...]
    tiles_to_rows(lambda i: tile_ref[i * 256 : (i + 1) * 256], swap, grad_ref, rows // 32)
    act_grad = lax.dot_general(grad_ref[...], down_w_ref[0], LAST, preferred_element_type=F32)
    pre = (act_grad * da_ref[...].astype(F32)).astype(BF16)
    upg = (act_grad * db_ref[...].astype(F32)).astype(BF16)
    pre_ref[...] = pre
    upg_ref[...] = upg
    score = jnp.sum(act_grad * act_ref[...].astype(F32), axis=1, keepdims=True)
    placed = jnp.dot(
        gather_ref[...],
        (score * spread_ref[...].astype(F32)).astype(BF16),
        preferred_element_type=F32,
    ).astype(BF16)
    rowg[...] = (
        lax.dot_general(pre, gate_w_ref[0], LAST, preferred_element_type=F32)
        + lax.dot_general(upg, up_w_ref[0], LAST, preferred_element_type=F32)
    ).astype(BF16)
    for group in range(rows // 32):
        halves = []
        for half in range(2):
            at = group * 32 + half * 16
            halves.append(
                jnp.concatenate(
                    [
                        rowg[at : at + 16, chunk * LANES : (chunk + 1) * LANES]
                        for chunk in range(CHUNKS)
                    ],
                    axis=0,
                )
            )
        turned = jnp.dot(
            swap, jnp.concatenate(halves, axis=1), preferred_element_type=F32
        ).astype(BF16)
        for half in range(2):
            for inner in range(16):
                row = group * 32 + half * 16 + inner
                place = (row % caps) * 16
                back_ref[row // caps, place : place + 16, :] = turned[
                    inner * 16 : (inner + 1) * 16, half * LANES : (half + 1) * LANES
                ]
    for source in range(rows // caps):
        back_ref[source, caps * 16 : caps * 16 + PACK_EXTRA, :] = jnp.broadcast_to(
            placed[source : source + 1], (PACK_EXTRA, LANES)
        )


def combine_kernel(
    ids_ref, slot_ref, back_ref, hidden_ref, grad_ref, gain_ref, swap_ref, out_ref, total, tiles
):
    tokens = hidden_ref.shape[0]
    top_k = ids_ref.shape[1]

    def gather(token, carry):
        acc = jnp.zeros((CHUNKS, LANES), F32)
        for k in range(top_k):
            at = pl.multiple_of(slot_ref[token, k] * 16, 16)
            acc = acc + back_ref[ids_ref[token, k], pl.ds(at, 16), :].astype(F32)
        total[token] = acc
        return carry

    lax.fori_loop(0, tokens, gather, 0, unroll=2)
    gain = gain_ref[...].astype(F32)[None]
    share = 1.0 / (CHUNKS * LANES)

    def mean(value):
        return (
            jnp.sum(jnp.sum(value, axis=2, keepdims=True), axis=1, keepdims=True) * share
        )

    for start in range(0, tokens, 16):
        hidden = hidden_ref[start : start + 16].astype(F32)
        inv_rms = lax.rsqrt(mean(hidden * hidden) + EPS)
        unit = hidden * inv_rms
        scaled = total[start : start + 16] * gain
        residual = grad_ref[start : start + 16].astype(F32) + inv_rms * (
            scaled - unit * mean(scaled * unit)
        )
        tiles[start * 16 : start * 16 + 256] = residual.astype(BF16).reshape(256, LANES)
    tiles_to_rows(
        lambda i: tiles[i * 256 : (i + 1) * 256], swap_ref[...], out_ref, tokens // 32
    )


def gate_kernel(ids_ref, slot_ref, weight_ref, score_ref, out_ref):
    tokens, top_k = ids_ref.shape
    lane = lax.broadcasted_iota(jnp.int32, (tokens, LANES), 1)
    ids = ids_ref[...]
    slot = slot_ref[...]
    found = jnp.zeros((tokens, LANES), F32)
    for k in range(top_k):
        hit = jnp.where(ids[:, k : k + 1] == lane, 1.0, 0.0).astype(BF16)
        mine = jnp.dot(hit, score_ref[...], preferred_element_type=F32)
        value = jnp.sum(jnp.where(slot[:, k : k + 1] == lane, mine, 0.0), axis=1, keepdims=True)
        found = jnp.where(lane == k, value, found)
    scale = (CHUNKS * LANES) ** (-0.5)
    out_ref[...] = (found[:, :top_k] * scale / weight_ref[...].astype(F32)).astype(BF16)


def probs_kernel(query_ref, key_ref, begin_ref, out_ref):
    scores = lax.dot_general(
        query_ref[...], key_ref[...], LAST, preferred_element_type=F32
    ) * HEAD_DIM ** (-0.5)
    here = lax.broadcasted_iota(jnp.int32, (SEQ, SEQ), 0)
    there = lax.broadcasted_iota(jnp.int32, (SEQ, SEQ), 1)
    visible = (there <= here) & (there >= begin_ref[...])
    masked = jnp.where(visible, scores, -1e30)
    top = jnp.max(masked, axis=1, keepdims=True)
    weights = jnp.where(visible, jnp.exp(masked - top), 0.0)
    out_ref[0, 0] = (weights / jnp.sum(weights, axis=1, keepdims=True)).astype(BF16)


def attention_kernel(
    probs_ref, query_ref, key_ref, value_ref, attn_ref, grad_ref, dq_ref, dk_ref, dv_ref
):
    probs = probs_ref[0, 0]
    grad = grad_ref[...]
    delta = jnp.sum(grad.astype(F32) * attn_ref[...].astype(F32), axis=1, keepdims=True)
    prob_grad = lax.dot_general(grad, value_ref[...], LAST, preferred_element_type=F32)
    score_grad = (probs.astype(F32) * (prob_grad - delta)).astype(BF16)
    scale = HEAD_DIM ** (-0.5)
    dq_ref[...] = (
        jnp.dot(score_grad, key_ref[...], preferred_element_type=F32) * scale
    ).astype(BF16)
    dk_ref[...] = (
        lax.dot_general(score_grad, query_ref[...], FIRST, preferred_element_type=F32) * scale
    ).astype(BF16)
    dv_ref[...] = lax.dot_general(probs, grad, FIRST, preferred_element_type=F32).astype(BF16)


def per_device(
    hidden_state,
    out_grad,
    norm_gain,
    expert_ids,
    route_weight,
    w_gate,
    w_up,
    w_down,
    queries,
    keys,
    values,
    attn_out,
    out_weight,
    doc_start,
):
    tokens, width = hidden_state.shape
    top_k = expert_ids.shape[1]
    ff = w_gate.shape[2]
    dp_size = lax.axis_size("dp")
    experts = lax.axis_size("ep") * dp_size
    caps = 5 * tokens * top_k // (4 * experts)
    rows = experts * caps
    both = ("ep", "dp")
    swap = swap_matrix()
    hidden3 = hidden_state.reshape(tokens, CHUNKS, LANES)
    grad3 = out_grad.reshape(tokens, CHUNKS, LANES)
    gain2 = norm_gain.reshape(CHUNKS, LANES)

    table, scales, slots = call(
        functools.partial(slots_kernel, caps),
        (
            jax.ShapeDtypeStruct((16, LANES), jnp.int32),
            jax.ShapeDtypeStruct((16, LANES), F32),
            jax.ShapeDtypeStruct((tokens, LANES), jnp.int32),
        ),
        moved=300000,
    )(expert_ids, route_weight)

    step_rows = 16 * caps
    steps = rows // step_rows
    tile_block = pl.BlockSpec((step_rows, CHUNKS, LANES), lambda i, *_: (i, 0, 0))
    send_rows = call(
        functools.partial(pack_rows_kernel, caps),
        jax.ShapeDtypeStruct((rows, CHUNKS, LANES), BF16),
        moved=12000000,
        grid_spec=pltpu.PrefetchScalarGridSpec(
            num_scalar_prefetch=1,
            grid=(steps,),
            in_specs=[whole((tokens, CHUNKS, LANES)), whole((CHUNKS, LANES))],
            out_specs=tile_block,
            scratch_shapes=[pltpu.VMEM((tokens + 1, CHUNKS, LANES), BF16)],
        ),
    )(table, hidden3, gain2)
    send_grads = call(
        functools.partial(pack_grads_kernel, caps),
        jax.ShapeDtypeStruct((rows, CHUNKS, LANES), BF16),
        moved=12000000,
        grid_spec=pltpu.PrefetchScalarGridSpec(
            num_scalar_prefetch=2,
            grid=(steps,),
            in_specs=[whole((tokens, CHUNKS, LANES))],
            out_specs=tile_block,
        ),
    )(table, scales, grad3)

    def exchange(array):
        return lax.all_to_all(array, both, split_axis=0, concat_axis=0, tiled=True)

    got_rows = exchange(send_rows.reshape(experts, caps * 16, LANES)).reshape(rows * 16, LANES)
    got_grads = exchange(send_grads.reshape(experts, caps * 16, LANES)).reshape(rows * 16, LANES)

    group_len, head_cols = queries.shape
    head_count = head_cols // HEAD_DIM
    seq_count = group_len // SEQ
    head_block = pl.BlockSpec((SEQ, HEAD_DIM), lambda s, h: (s, h))
    probs_block = pl.BlockSpec((1, 1, SEQ, SEQ), lambda s, h: (s, h, 0, 0))
    probs = call(
        probs_kernel,
        jax.ShapeDtypeStruct((seq_count, head_count, SEQ, SEQ), BF16),
        flops=10**10,
        moved=5000000,
        grid=(seq_count, head_count),
        in_specs=[head_block, head_block, pl.BlockSpec((SEQ, 1), lambda s, h: (s, 0))],
        out_specs=probs_block,
    )(queries, keys, doc_start.reshape(group_len, 1))

    flat_tiles = pl.BlockSpec((step_rows * 16, LANES), lambda i: (i, 0))
    wide = pl.BlockSpec((step_rows, width), lambda i: (i, 0))
    narrow = pl.BlockSpec((step_rows, ff), lambda i: (i, 0))
    w_in = whole((1, width, ff))
    w_out = whole((1, ff, width))
    narrow_shape = jax.ShapeDtypeStruct((rows, ff), BF16)
    wide_shape = jax.ShapeDtypeStruct((rows, width), BF16)
    rows_in, act, act_da, act_db = call(
        expert_up_kernel,
        (wide_shape, narrow_shape, narrow_shape, narrow_shape),
        flops=4 * rows * width * ff,
        moved=18000000,
        grid=(steps,),
        in_specs=[flat_tiles, whole((256, 256)), w_in, w_in],
        out_specs=(wide, narrow, narrow, narrow),
    )(got_rows, swap, w_gate, w_up)
    index = np.arange(step_rows)
    gather = jnp.asarray(index[None, :] // caps == np.arange(16)[:, None], BF16)
    spread = jnp.asarray(index[:, None] % caps == np.arange(LANES)[None, :], BF16)
    block_rows = caps * 16 + PACK_EXTRA
    scaled_grad, pre_grad, up_grad, send_back = call(
        functools.partial(expert_down_kernel, caps),
        (
            wide_shape,
            narrow_shape,
            narrow_shape,
            jax.ShapeDtypeStruct((experts, block_rows, LANES), BF16),
        ),
        flops=6 * rows * width * ff,
        moved=25000000,
        grid=(steps,),
        in_specs=[
            flat_tiles,
            whole((256, 256)),
            whole((16, step_rows)),
            whole((step_rows, LANES)),
            w_in,
            w_in,
            w_out,
            narrow,
            narrow,
            narrow,
        ],
        out_specs=(
            wide,
            narrow,
            narrow,
            pl.BlockSpec((16, block_rows, LANES), lambda i: (i, 0, 0)),
        ),
        scratch_shapes=[pltpu.VMEM((step_rows, width), BF16)],
    )(got_grads, swap, gather, spread, w_gate, w_up, w_down, act, act_da, act_db)
    back = exchange(send_back)
    grad_scale = (tokens * top_k) ** (-0.5)

    def weight_grad(left, right):
        product = lax.dot_general(left, right, FIRST, preferred_element_type=F32)
        return (product * grad_scale).astype(BF16)[None]

    grad_gate_w = weight_grad(rows_in, pre_grad)
    grad_up_w = weight_grad(rows_in, up_grad)
    grad_down_w = weight_grad(act, scaled_grad)

    residual_grad = call(
        combine_kernel,
        jax.ShapeDtypeStruct((tokens, width), BF16),
        moved=8000000,
        grid_spec=pltpu.PrefetchScalarGridSpec(
            num_scalar_prefetch=2,
            grid=(1,),
            in_specs=[
                whole((experts, block_rows, LANES)),
                whole((tokens, CHUNKS, LANES)),
                whole((tokens, CHUNKS, LANES)),
                whole((CHUNKS, LANES)),
                whole((256, 256)),
            ],
            out_specs=whole((tokens, width)),
            scratch_shapes=[
                pltpu.VMEM((tokens, CHUNKS, LANES), F32),
                pltpu.VMEM((tokens * CHUNKS, LANES), BF16),
            ],
        ),
    )(expert_ids, slots, back, hidden3, grad3, gain2, swap)
    gate_grad = call(gate_kernel, jax.ShapeDtypeStruct((tokens, top_k), BF16), moved=200000)(
        expert_ids, slots, route_weight, back[:, caps * 16, :]
    )

    group_rows = lax.all_gather(residual_grad, "ep", axis=0, tiled=True)
    partial_w = lax.dot_general(
        group_rows, attn_out, FIRST, preferred_element_type=F32
    ).astype(BF16)
    pieces = lax.all_to_all(
        partial_w.reshape(dp_size, width // dp_size, head_cols),
        "dp",
        split_axis=0,
        concat_axis=0,
        tiled=True,
    )
    out_weight_grad = (
        jnp.sum(pieces.astype(F32), axis=0) * (group_len * dp_size) ** (-0.5)
    ).astype(BF16)
    attn_grad = jnp.dot(group_rows, out_weight, preferred_element_type=F32).astype(BF16)
    head_shape = jax.ShapeDtypeStruct((group_len, head_cols), BF16)
    query_grad, key_grad, value_grad = call(
        attention_kernel,
        (head_shape, head_shape, head_shape),
        flops=4 * 8 * SEQ * SEQ * HEAD_DIM,
        moved=6000000,
        grid=(seq_count, head_count),
        in_specs=[probs_block] + [head_block] * 5,
        out_specs=(head_block, head_block, head_block),
    )(probs, queries, keys, values, attn_out, attn_grad)
    return (
        gate_grad,
        grad_gate_w,
        grad_up_w,
        grad_down_w,
        residual_grad,
        out_weight_grad,
        query_grad,
        key_grad,
        value_grad,
    )


def solution(mesh):
    tokens = P(("dp", "ep"), None)
    expert = P(("ep", "dp"), None, None)
    heads = P("dp", "ep")
    return jax.shard_map(
        per_device,
        mesh=mesh,
        in_specs=(
            tokens,
            tokens,
            P(),
            tokens,
            tokens,
            expert,
            expert,
            expert,
            heads,
            heads,
            heads,
            heads,
            P(None, "ep"),
            P("dp"),
        ),
        out_specs=(tokens, expert, expert, expert, tokens, heads, heads, heads, heads),
        check_vma=False,
    )
```

time: 661 us -> 347 us (0.52)
  waiting for transfers between devices: 307 us -> 115 us
  local copies, waits for them, and re-layouts: 159 us -> 9.81 us
  Pallas kernels: 0 us -> 82 us
  blocking collectives: 0 us -> 72.4 us
  starting transfers between devices: 78.5 us -> 24.8 us
  matrix products: 69.9 us -> 26.3 us
  other arithmetic: 24.4 us -> 0.78 us
    all_to_all x5 -> x3, waiting for transfers between devices: 248 us -> 104 us  [the longest x2 104 us: exchange(): return lax.all_to_all(array, both, split_axis=0, concat_axis=0, tiled=True)]
    pallas_call x0 -> x9, Pallas kernels: none -> 82 us  [the longest x1 28.2 us: per_device(): call(functools.partial(expert_down_kernel, caps), (wide_shape, narrow_sha...]
    all_to_all x0 -> x1, blocking collectives: none -> 72.4 us  [exchange(): return lax.all_to_all(array, both, split_axis=0, concat_axis=0, tiled=True)]
    reduce_scatter x1 -> x0, waiting for transfers between devices: 59.4 us -> none  [per_device(): lax.psum_scatter(lax.dot_general(group_rows, attn_out, contract_first, pr...]
    scatter x3 -> x0, local copies, waits for them, and re-layouts: 54.3 us -> none  [the longest x2 46.7 us: per_device(): jnp.zeros((buffer_rows, model_width), jnp.bfloat16).at[slot_place]]
    reshape x14 -> x1, local copies, waits for them, and re-layouts: 55.3 us -> 1.03 us  [per_device(): doc_start.reshape(group_len, 1)]
    all_to_all x5 -> x3, starting transfers between devices: 78.4 us -> 24.7 us  [the longest x2 18.1 us: exchange(): return lax.all_to_all(array, both, split_axis=0, concat_axis=0, tiled=True)]
    dot_general x16 -> x5, matrix products: 69.9 us -> 26.3 us  [the longest x3 17.6 us: weight_grad(): product = lax.dot_general(left, right, FIRST, preferred_element_type=F32)]
  transfers between devices with their start and end apart: 7 -> 4, of which waited for: 4 -> 3; matrix products, arithmetic and copies ran while one was open for 24% -> 8% of each run, Pallas kernels for 0% -> 10%
where the time goes in v1:
time: 347 us; the launch traced here: 345 us
  waiting for transfers between devices  115 us (33%)
  Pallas kernels  82 us (24%)
  blocking collectives  72.4 us (21%)
  matrix products  26.3 us (8%)
  starting transfers between devices  24.8 us (7%)
  between operations  14.1 us (4%)
  local copies, waits for them, and re-layouts  9.81 us (3%)
    all_to_all x2, waiting for transfers between devices, exchange(): return lax.all_to_all(array, both, split_axis=0, concat_axis=0, tiled=True)  104 us
    all_to_all x1, blocking collectives, exchange(): return lax.all_to_all(array, both, split_axis=0, concat_axis=0, tiled=True)  72.4 us
    pallas_call x1, Pallas kernels, per_device(): call(functools.partial(expert_down_kernel, caps), (wide_shape, narrow_sha...  28.2 us
    all_to_all x2, starting transfers between devices, exchange(): return lax.all_to_all(array, both, split_axis=0, concat_axis=0, tiled=True)  18.1 us
    dot_general x3, matrix products, weight_grad(): product = lax.dot_general(left, right, FIRST, preferred_element_type=F32)  17.6 us
    pallas_call x1, Pallas kernels, per_device(): call(expert_up_kernel, (wide_shape, narrow_shape, narrow_shape, narrow_sh...  12.5 us
    all_gather x1, waiting for transfers between devices, per_device(): group_rows = lax.all_gather(residual_grad, 'ep', axis=0, tiled=True)  11.4 us
    pallas_call x1, Pallas kernels, per_device(): call(combine_kernel, jax.ShapeDtypeStruct((tokens, width), BF16), moved=8...  10.4 us
  transfers between devices with their start and end apart: 4, of which 3 were waited for; matrix products, arithmetic and copies ran while one was open for 8% of the time, Pallas kernels for 10%

profile of v1, /device:TPU:1, one launch (start us, length us, event | category | flops | bytes accessed | tf_op | source)
XLA Modules:
  0.0 345.5 jit_solution(14097372938535878433)
XLA Ops:
  7.2 0.0 copy-start
  7.2 1.5 copy.34.ids_ref
  8.7 1.4 copy.33.weight_ref
  10.1 1.9 copy.41
  12.0 2.2 shard_map.232
  14.2 7.1 %shard_map.234 = bf16[1280,16,128]{2,1,0:T(8,128)(2,1)} custom-call(s32[16,128]{1,0:T(8,128)} %get-tuple-element.24.table_ref, bf16[128,16,128]{2,1,0:T(8,128)(2,1)} %bitcast.32, bf16[16,128]{1,0:T(8,128)(2,1)} %bitcast.39), custom_call_target="tpu_custom_call" | custom-call | bytes 12000000 | tf_op jit(solution)/shard_map/pallas_call | solution.py:331
  21.3 0.0 copy-start.2
  21.3 11.9 %all-to-all-start.1 = ((bf16[128,160,128]{2,1,0:T(8,128)(2,1)}), bf16[128,160,128]{2,1,0:T(8,128)(2,1)}, u32[]{:S(2)}, u32[]{:S(2)}) async-start(bf16[128,160,128]{2,1,0:T(8,128)(2,1)} %bitcast.31), calls=%async_computation.1 | async-start | bytes 10485760 | tf_op jit(solution)/shard_map/all_to_all | solution.py:356
  33.2 0.0 copy-done.2
  33.2 0.9 copy.40
  34.1 7.8 %shard_map.233 = bf16[1280,16,128]{2,1,0:T(8,128)(2,1)} custom-call(s32[16,128]{1,0:T(8,128)} %get-tuple-element.24.table_ref, f32[16,128]{1,0:T(8,128)} %get-tuple-element.25.scale_ref, bf16[128,16,128]{2,1,0:T(8,128)(2,1)} %bitcast.34), custom_call_target="tpu_custom_call" | custom-call | bytes 12000000 | tf_op jit(solution)/shard_map/pallas_call | solution.py:343
  41.9 53.8 %all-to-all-done.1 = bf16[128,160,128]{2,1,0:T(8,128)(2,1)} async-done(((bf16[128,160,128]{2,1,0:T(8,128)(2,1)}), bf16[128,160,128]{2,1,0:T(8,128)(2,1)}, u32[]{:S(2)}, u32[]{:S(2)}) %all-to-all-start.1) | async-done | bytes 5242912 | tf_op jit(solution)/shard_map/all_to_all | solution.py:356
  95.8 6.2 %all-to-all-start = ((bf16[128,160,128]{2,1,0:T(8,128)(2,1)}), bf16[128,160,128]{2,1,0:T(8,128)(2,1)}, u32[]{:S(2)}, u32[]{:S(2)}) async-start(bf16[128,160,128]{2,1,0:T(8,128)(2,1)} %bitcast.30), calls=%async_computation | async-start | bytes 10485760 | tf_op jit(solution)/shard_map/all_to_all | solution.py:356
  101.9 0.0 all-gather.2.cloned.1.call-start
  102.0 12.5 %shard_map.235 = (bf16[1280,2048]{1,0:T(8,128)(2,1)}, bf16[1280,512]{1,0:T(8,128)(2,1)}, bf16[1280,512]{1,0:T(8,128)(2,1)}, bf16[1280,512]{1,0:T(8,128)(2,1)}) custom-call(bf16[20480,128]{1,0:T(8,128)(2,1)} %bitcast.4.tile_ref, bf16[256,256]{1,0:T(8,128)(2,1)} %constant.5.clone.swap_ref, bf16[1,2048,512]{2,1,0:T(8,128)(2,1)} %gate_w_ref.3, ...), custom_call_target="tpu_custom_call" | custom-call | flops 5368709120 | bytes 18000000 | tf_op jit(solution)/shard_map/pallas_call | solution.py:383
  114.5 50.0 %all-to-all-done = bf16[128,160,128]{2,1,0:T(8,128)(2,1)} async-done(((bf16[128,160,128]{2,1,0:T(8,128)(2,1)}), bf16[128,160,128]{2,1,0:T(8,128)(2,1)}, u32[]{:S(2)}, u32[]{:S(2)}) %all-to-all-start) | async-done | bytes 5242912 | tf_op jit(solution)/shard_map/all_to_all | solution.py:356
  164.5 28.2 %shard_map.236 = (bf16[1280,2048]{1,0:T(8,128)(2,1)}, bf16[1280,512]{1,0:T(8,128)(2,1)}, bf16[1280,512]{1,0:T(8,128)(2,1)}, bf16[128,168,128]{2,1,0:T(8,128)(2,1)}) custom-call(bf16[20480,128]{1,0:T(8,128)(2,1)} %bitcast.1.tile_ref, bf16[256,256]{1,0:T(8,128)(2,1)} %constant.5.clone.swap_ref, bf16[16,160]{1,0:T(8,128)(2,1)} %constant.14.clone.gather_ref, ...), custom_call_target="tpu_custom_call" | custom-call | flops 8053063680 | bytes 25000000 | tf_op jit(solution)/shard_map/pallas_call | solution.py:396
  192.7 72.4 %all_to_all.20.back_ref = bf16[128,168,128]{2,1,0:T(8,128)(2,1)} all-to-all(bf16[128,168,128]{2,1,0:T(8,128)(2,1)} %get-tuple-element.29), channel_id=1, replica_groups=mesh['ep'=8,'dp'=16] {'ep','dp'}, dimensions={0} | all-to-all | bytes 11010048 | tf_op jit(solution)/shard_map/all_to_all | solution.py:356
  265.1 0.0 copy-start.3
  265.1 10.4 %shard_map.238 = bf16[128,2048]{1,0:T(8,128)(2,1)} custom-call(s32[128,8]{1,0:T(8,128)} %copy.34.ids_ref, s32[128,128]{1,0:T(8,128)} %get-tuple-element.23.slot_ref, bf16[128,168,128]{2,1,0:T(8,128)(2,1)} %all_to_all.20.back_ref, bf16[128,16,128]{2,1,0:T(8,128)(2,1)} %bitcast.33, bf16[128,16,128]{2,1,0:T(8,128)(2,1)} %bitcast.35, bf16[16,128]{1,0:T(8,128)(2,1)} %bitcast.40, ...), custom_call_target="tpu_custom_call" | custom-call | bytes 8000000 | tf_op jit(solution)/shard_map/pallas_call | solution.py:438
  275.5 0.0 slice-start
  275.5 0.0 all-gather.2.cloned.1.call-update
  275.5 0.0 copy-done.3
  275.5 1.0 copy.37.begin_ref
  276.6 5.2 %shard_map.239.probs_ref = bf16[2,2,512,512]{3,2,1,0:T(8,128)(2,1)} custom-call(bf16[1024,256]{1,0:T(8,128)(2,1)} %query_ref.3, bf16[1024,256]{1,0:T(8,128)(2,1)} %key_ref.3, s32[1024,1]{1,0:T(8,128)} %copy.37.begin_ref), custom_call_target="tpu_custom_call" | custom-call | flops 10000000000 | bytes 5000000 | tf_op jit(solution)/shard_map/pallas_call | solution.py:366
  281.7 0.0 slice-done
  281.7 0.0 slice-done.1
  281.7 0.0 copy-done.6
  281.8 0.0 copy-start.5
  281.8 4.1 %fusion = bf16[1,2048,512]{2,1,0:T(8,128)(2,1)} fusion(bf16[1280,2048]{1,0:T(8,128)(2,1)S(1)} %bitcast.43, bf16[1280,512]{1,0:T(8,128)(2,1)S(1)} %copy-done.6), kind=kOutput, calls=%fused_computation.3 | convolution fusion | flops 2686451712 | bytes 8650752 | tf_op jit(solution)/shard_map/dot_general | solution.py:431
  285.9 0.0 copy-done.5
  285.9 6.9 %fusion.1 = bf16[1,2048,512]{2,1,0:T(8,128)(2,1)} fusion(bf16[1280,2048]{1,0:T(8,128)(2,1)} %get-tuple-element.30, bf16[1280,512]{1,0:T(8,128)(2,1)S(1)} %copy-done.5), kind=kOutput, calls=%fused_computation.4 | convolution fusion | flops 2686451712 | bytes 8650752 | tf_op jit(solution)/shard_map/dot_general | solution.py:431
  292.8 11.4 %all-gather.2.cloned.1.call-done = bf16[1024,2048]{1,0:T(8,128)(2,1)} async-done(((bf16[128,2048]{1,0:T(8,128)(2,1)}), bf16[1024,2048]{1,0:T(8,128)(2,1)}) %all-gather.2.cloned.1.call-update) | async-done | bytes 4194320 | tf_op jit(solution)/shard_map/all_gather | solution.py:463
  304.2 0.0 copy-done.1
  304.2 4.5 %convolution_convert_fusion = bf16[2048,256]{1,0:T(8,128)(2,1)} fusion(bf16[1024,2048]{1,0:T(8,128)(2,1)} %all-gather.2.cloned.1.call-done, bf16[1024,256]{1,0:T(8,128)(2,1)S(1)} %copy-done.1), kind=kOutput, calls=%fused_computation.6 | convolution fusion | flops 1074266112 | bytes 5767168 | tf_op jit(solution)/shard_map/dot_general | solution.py:464
  308.7 6.7 %all-to-all-start.3 = ((bf16[16,128,256]{2,1,0:T(8,128)(2,1)}), bf16[16,128,256]{2,1,0:T(8,128)(2,1)S(1)}, u32[]{:S(2)}, u32[]{:S(2)}) async-start(bf16[16,128,256]{2,1,0:T(8,128)(2,1)} %bitcast.8), calls=%async_computation.3 | async-start | bytes 2097152 | tf_op jit(solution)/shard_map/all_to_all | solution.py:467
  315.4 0.0 copy-done.4
  315.4 6.6 %fusion.2 = bf16[1,512,2048]{2,1,0:T(8,128)(2,1)} fusion(bf16[1280,512]{1,0:T(8,128)(2,1)S(1)} %copy-done.4, bf16[1280,2048]{1,0:T(8,128)(2,1)} %get-tuple-element.33), kind=kOutput, calls=%fused_computation.5 | convolution fusion | flops 2686451712 | bytes 8650752 | tf_op jit(solution)/shard_map/dot_general | solution.py:431
  322.0 1.0 slice.4
  323.0 0.6 copy.43
  323.6 2.8 shard_map.237
  326.3 1.4 copy.38
  327.7 0.0 copy-done
  327.7 4.2 %convolution_convert_fusion.1.grad_ref = bf16[1024,256]{1,0:T(8,128)(2,1)} fusion(bf16[1024,2048]{1,0:T(8,128)(2,1)} %all-gather.2.cloned.1.call-done, bf16[2048,256]{1,0:T(8,128)(2,1)S(1)} %copy-done), kind=kOutput, calls=%fused_computation.8 | convolution fusion | flops 1074003968 | bytes 5767168 | tf_op jit(solution)/shard_map/dot_general | solution.py:477
  332.0 5.8 %shard_map.240 = (bf16[1024,256]{1,0:T(8,128)(2,1)}, bf16[1024,256]{1,0:T(8,128)(2,1)}, bf16[1024,256]{1,0:T(8,128)(2,1)}) custom-call(bf16[2,2,512,512]{3,2,1,0:T(8,128)(2,1)} %shard_map.239.probs_ref, bf16[1024,256]{1,0:T(8,128)(2,1)} %query_ref.3, bf16[1024,256]{1,0:T(8,128)(2,1)} %key_ref.3, bf16[1024,256]{1,0:T(8,128)(2,1)} %value_ref.1, ...), custom_call_target="tpu_custom_call" | custom-call | flops 1073741824 | bytes 6000000 | tf_op jit(solution)/shard_map/pallas_call | solution.py:479
  337.8 0.0 all-to-all-done.3
  337.8 0.1 convert_reduce_fusion
  338.0 0.6 multiply_convert_fusion.3
  (5 shorter events, 0.0 us)
Async XLA Ops:
  7.2 320.6 %copy-start = (bf16[2048,256]{1,0:T(8,128)(2,1)S(1)}, bf16[2048,256]{1,0:T(8,128)(2,1)}, u32[]{:S(2)}) copy-start(bf16[2048,256]{1,0:T(8,128)(2,1)} %param.29) | copy-start | bytes 3145732
  21.3 11.9 %copy-start.2 = (bf16[128,2048]{1,0:T(8,128)(2,1)S(1)}, bf16[128,2048]{1,0:T(8,128)(2,1)}, u32[]{:S(2)}) copy-start(bf16[128,2048]{1,0:T(8,128)(2,1)} %param.18) | copy-start | bytes 1572868
  21.3 74.4 %all-to-all-start.1 = ((bf16[128,160,128]{2,1,0:T(8,128)(2,1)}), bf16[128,160,128]{2,1,0:T(8,128)(2,1)}, u32[]{:S(2)}, u32[]{:S(2)}) async-start(bf16[128,160,128]{2,1,0:T(8,128)(2,1)} %bitcast.31), calls=%async_computation.1 | async-start | bytes 10485760 | tf_op jit(solution)/shard_map/all_to_all | solution.py:356
  95.8 68.7 %all-to-all-start = ((bf16[128,160,128]{2,1,0:T(8,128)(2,1)}), bf16[128,160,128]{2,1,0:T(8,128)(2,1)}, u32[]{:S(2)}, u32[]{:S(2)}) async-start(bf16[128,160,128]{2,1,0:T(8,128)(2,1)} %bitcast.30), calls=%async_computation | async-start | bytes 10485760 | tf_op jit(solution)/shard_map/all_to_all | solution.py:356
  101.9 202.2 %all-gather.2.cloned.1.call-start = ((), (), s32[]{:S(2)}) async-start(), calls=%async_computation.4 | async-start | bytes 4718592 | tf_op jit(solution)/shard_map/all_gather | solution.py:463
  265.1 10.5 %copy-start.3 = (s32[1024]{0:T(1024)S(1)}, s32[1024]{0:T(1024)}, u32[]{:S(2)}) copy-start(s32[1024]{0:T(1024)} %param.30) | copy-start | bytes 12292
  275.5 6.2 %slice-start = ((s8[5242880]{0:T(1024)(128)(4,1)}), s8[1048576]{0:T(1024)(128)(4,1)S(1)}, s32[]{:S(2)}) async-start(s8[5242880]{0:T(1024)(128)(4,1)} %bitcast.42), calls=%async_computation.5 | async-start | bytes 2097152
  276.6 5.2 %slice-start.1 = ((s8[5242880]{0:T(1024)(128)(4,1)}), s8[4194304]{0:T(1024)(128)(4,1)S(1)}, s32[]{:S(2)}) async-start(s8[5242880]{0:T(1024)(128)(4,1)} %bitcast.42), calls=%async_computation.6 | async-start | bytes 8388608
  276.6 5.2 %copy-start.6 = (bf16[1280,512]{1,0:T(8,128)(2,1)S(1)}, bf16[1280,512]{1,0:T(8,128)(2,1)}, u32[]{:S(2)}) copy-start(bf16[1280,512]{1,0:T(8,128)(2,1)} %get-tuple-element.31) | copy-start | bytes 3932164
  281.8 4.1 %copy-start.5 = (bf16[1280,512]{1,0:T(8,128)(2,1)S(1)}, bf16[1280,512]{1,0:T(8,128)(2,1)}, u32[]{:S(2)}) copy-start(bf16[1280,512]{1,0:T(8,128)(2,1)} %get-tuple-element.32) | copy-start | bytes 3932164
  285.9 18.3 %copy-start.1 = (bf16[1024,256]{1,0:T(8,128)(2,1)S(1)}, bf16[1024,256]{1,0:T(8,128)(2,1)}, u32[]{:S(2)}) copy-start(bf16[1024,256]{1,0:T(8,128)(2,1)} %attn_ref.1) | copy-start | bytes 1572868
  292.8 22.6 %copy-start.4 = (bf16[1280,512]{1,0:T(8,128)(2,1)S(1)}, bf16[1280,512]{1,0:T(8,128)(2,1)}, u32[]{:S(2)}) copy-start(bf16[1280,512]{1,0:T(8,128)(2,1)} %get-tuple-element.26.act_ref) | copy-start | bytes 3932164
  308.7 29.2 %all-to-all-start.3 = ((bf16[16,128,256]{2,1,0:T(8,128)(2,1)}), bf16[16,128,256]{2,1,0:T(8,128)(2,1)S(1)}, u32[]{:S(2)}, u32[]{:S(2)}) async-start(bf16[16,128,256]{2,1,0:T(8,128)(2,1)} %bitcast.8), calls=%async_computation.3 | async-start | bytes 2097152 | tf_op jit(solution)/shard_map/all_to_all | solution.py:467
Sparse Core Ops, SparseCore 0:
  275.7 28.4 all-gather.1

commit v2 on v1

--- a/solution.py
+++ b/solution.py
@@ -18,6 +18,8 @@
 LAST = (((1,), (1,)), ((), ()))
 FIRST = (((0,), (0,)), ((), ()))
 PACK_EXTRA = 8
+DESTS = 32
+SOURCES = 32
 VMEM_LIMIT = 56 * 1024 * 1024
 
 
@@ -54,42 +56,44 @@
 
 
 def slots_kernel(caps, ids_ref, weight_ref, table_ref, scale_ref, slot_ref):
-    tokens, top_k = ids_ref.shape
+    top_k, tokens = ids_ref.shape
     experts = LANES
-    lane = lax.broadcasted_iota(jnp.int32, (tokens, experts), 1)
-    row = lax.broadcasted_iota(jnp.int32, (tokens, experts), 0)
+    lane = lax.broadcasted_iota(jnp.int32, (experts, tokens), 1)
+    row = lax.broadcasted_iota(jnp.int32, (experts, tokens), 0)
     ids = ids_ref[...]
     weight = weight_ref[...].astype(F32)
-    chosen = jnp.zeros((tokens, experts), F32)
-    weights = jnp.zeros((tokens, experts), F32)
+    chosen = jnp.zeros((experts, tokens), F32)
+    weights = jnp.zeros((experts, tokens), F32)
     for k in range(top_k):
-        hit = ids[:, k : k + 1] == lane
+        hit = ids[k : k + 1] == row
         chosen = jnp.where(hit, 1.0, chosen)
-        weights = jnp.where(hit, weight[:, k : k + 1], weights)
-    lower = jnp.where(lane < row, 1.0, 0.0).astype(BF16)
-    counts = jnp.dot(lower, chosen.astype(BF16), preferred_element_type=F32)
-    table = jnp.zeros((16, experts), F32)
-    scales = jnp.zeros((16, experts), F32)
-    sub = lax.broadcasted_iota(jnp.int32, (16, experts), 0)
-    from_end = (row - tokens).astype(F32)
+        weights = jnp.where(hit, weight[k : k + 1], weights)
+    upper = jnp.where(row < lane, 1.0, 0.0).astype(BF16)
+    counts = jnp.dot(chosen.astype(BF16), upper, preferred_element_type=F32)
+    table = jnp.zeros((experts, LANES), F32)
+    scales = jnp.zeros((experts, LANES), F32)
+    from_end = (lane - tokens).astype(F32)
     for place in range(caps):
         mask = (chosen > 0.5) & (jnp.abs(counts - place) < 0.5)
-        token = jnp.sum(jnp.where(mask, from_end, 0.0), axis=0, keepdims=True) + tokens
-        scale = jnp.sum(jnp.where(mask, weights, 0.0), axis=0, keepdims=True)
-        table = jnp.where(sub == place, token, table)
-        scales = jnp.where(sub == place, scale, scales)
+        token = jnp.sum(jnp.where(mask, from_end, 0.0), axis=1, keepdims=True) + tokens
+        scale = jnp.sum(jnp.where(mask, weights, 0.0), axis=1, keepdims=True)
+        table = jnp.where(lane == place, token, table)
+        scales = jnp.where(lane == place, scale, scales)
     table_ref[...] = table.astype(jnp.int32)
     scale_ref[...] = scales
-    slot = jnp.zeros((tokens, experts), F32)
-    for k in range(top_k):
-        place = jnp.sum(jnp.where(ids[:, k : k + 1] == lane, counts, 0.0), axis=1, keepdims=True)
-        slot = jnp.where(lane == k, place, slot)
-    slot_ref[...] = slot.astype(jnp.int32)
-
-
-def pack_rows_kernel(caps, table_ref, hidden_ref, gain_ref, out_ref, normed):
+    slot_ref[...] = jnp.concatenate(
+        [
+            jnp.sum(jnp.where(ids[k : k + 1] == row, counts, 0.0), axis=0, keepdims=True)
+            for k in range(top_k)
+        ],
+        axis=0,
+    ).astype(jnp.int32)
+
+
+def pack_rows_kernel(table_ref, hidden_ref, gain_ref, out_ref, normed):
     tokens = hidden_ref.shape[0]
     step = pl.program_id(0)
+    caps = out_ref.shape[0] // DESTS
 
     @pl.when(step == 0)
     def _():
@@ -104,24 +108,26 @@
 
     def fill(dest, carry):
         for place in range(caps):
-            out_ref[dest * caps + place] = normed[table_ref[place, step * 16 + dest]]
+            out_ref[dest * caps + place] = normed[table_ref[step * DESTS + dest, place]]
         return carry
 
-    lax.fori_loop(0, 16, fill, 0)
-
-
-def pack_grads_kernel(caps, table_ref, scale_ref, grad_ref, out_ref):
+    lax.fori_loop(0, DESTS, fill, 0, unroll=2)
+
+
+def pack_grads_kernel(table_ref, scale_ref, grad_ref, out_ref):
     tokens = grad_ref.shape[0]
     step = pl.program_id(0)
+    caps = out_ref.shape[0] // DESTS
 
     def fill(dest, carry):
         for place in range(caps):
-            token = jnp.minimum(table_ref[place, step * 16 + dest], tokens - 1)
-            scale = scale_ref[place, step * 16 + dest]
+            at = step * DESTS + dest
+            token = jnp.minimum(table_ref[at, place], tokens - 1)
+            scale = scale_ref[at, place]
             out_ref[dest * caps + place] = (grad_ref[token].astype(F32) * scale).astype(BF16)
         return carry
 
-    lax.fori_loop(0, 16, fill, 0)
+    lax.fori_loop(0, DESTS, fill, 0, unroll=2)
 
 
 def expert_up_kernel(tile_ref, swap_ref, gate_w_ref, up_w_ref, row_ref, act_ref, da_ref, db_ref):
@@ -176,8 +182,8 @@
     ).astype(BF16)
     for group in range(rows // 32):
         halves = []
-        for half in range(2):
-            at = group * 32 + half * 16
+        for side in range(2):
+            at = group * 32 + side * 16
             halves.append(
                 jnp.concatenate(
                     [
@@ -190,12 +196,12 @@
         turned = jnp.dot(
             swap, jnp.concatenate(halves, axis=1), preferred_element_type=F32
         ).astype(BF16)
-        for half in range(2):
+        for side in range(2):
             for inner in range(16):
-                row = group * 32 + half * 16 + inner
+                row = group * 32 + side * 16 + inner
                 place = (row % caps) * 16
                 back_ref[row // caps, place : place + 16, :] = turned[
-                    inner * 16 : (inner + 1) * 16, half * LANES : (half + 1) * LANES
+                    inner * 16 : (inner + 1) * 16, side * LANES : (side + 1) * LANES
                 ]
     for source in range(rows // caps):
         back_ref[source, caps * 16 : caps * 16 + PACK_EXTRA, :] = jnp.broadcast_to(
@@ -206,18 +212,17 @@
 def combine_kernel(
     ids_ref, slot_ref, back_ref, hidden_ref, grad_ref, gain_ref, swap_ref, out_ref, total, tiles
 ):
-    tokens = hidden_ref.shape[0]
-    top_k = ids_ref.shape[1]
+    top_k, tokens = ids_ref.shape
 
     def gather(token, carry):
         acc = jnp.zeros((CHUNKS, LANES), F32)
         for k in range(top_k):
-            at = pl.multiple_of(slot_ref[token, k] * 16, 16)
-            acc = acc + back_ref[ids_ref[token, k], pl.ds(at, 16), :].astype(F32)
+            at = pl.multiple_of(slot_ref[k, token] * 16, 16)
+            acc = acc + back_ref[ids_ref[k, token], pl.ds(at, 16), :].astype(F32)
         total[token] = acc
         return carry
 
-    lax.fori_loop(0, tokens, gather, 0, unroll=2)
+    lax.fori_loop(0, tokens, gather, 0, unroll=4)
     gain = gain_ref[...].astype(F32)[None]
     share = 1.0 / (CHUNKS * LANES)
 
@@ -241,18 +246,20 @@
 
 
 def gate_kernel(ids_ref, slot_ref, weight_ref, score_ref, out_ref):
-    tokens, top_k = ids_ref.shape
-    lane = lax.broadcasted_iota(jnp.int32, (tokens, LANES), 1)
+    top_k, tokens = ids_ref.shape
+    row = lax.broadcasted_iota(jnp.int32, (LANES, tokens), 0)
     ids = ids_ref[...]
     slot = slot_ref[...]
-    found = jnp.zeros((tokens, LANES), F32)
+    found = []
     for k in range(top_k):
-        hit = jnp.where(ids[:, k : k + 1] == lane, 1.0, 0.0).astype(BF16)
-        mine = jnp.dot(hit, score_ref[...], preferred_element_type=F32)
-        value = jnp.sum(jnp.where(slot[:, k : k + 1] == lane, mine, 0.0), axis=1, keepdims=True)
-        found = jnp.where(lane == k, value, found)
+        hit = jnp.where(ids[k : k + 1] == row, 1.0, 0.0).astype(BF16)
+        mine = lax.dot_general(score_ref[...], hit, FIRST, preferred_element_type=F32)
+        found.append(
+            jnp.sum(jnp.where(slot[k : k + 1] == row, mine, 0.0), axis=0, keepdims=True)
+        )
     scale = (CHUNKS * LANES) ** (-0.5)
-    out_ref[...] = (found[:, :top_k] * scale / weight_ref[...].astype(F32)).astype(BF16)
+    value = jnp.concatenate(found, axis=0) * scale / weight_ref[...].astype(F32)
+    out_ref[...] = value.astype(BF16)
 
 
 def probs_kernel(query_ref, key_ref, begin_ref, out_ref):
@@ -315,48 +322,40 @@
     grad3 = out_grad.reshape(tokens, CHUNKS, LANES)
     gain2 = norm_gain.reshape(CHUNKS, LANES)
 
+    ids_t, weight_t = expert_ids.T, route_weight.T
     table, scales, slots = call(
         functools.partial(slots_kernel, caps),
         (
-            jax.ShapeDtypeStruct((16, LANES), jnp.int32),
-            jax.ShapeDtypeStruct((16, LANES), F32),
-            jax.ShapeDtypeStruct((tokens, LANES), jnp.int32),
+            jax.ShapeDtypeStruct((experts, LANES), jnp.int32),
+            jax.ShapeDtypeStruct((experts, LANES), F32),
+            jax.ShapeDtypeStruct((top_k, tokens), jnp.int32),
         ),
         moved=300000,
-    )(expert_ids, route_weight)
-
-    step_rows = 16 * caps
-    steps = rows // step_rows
-    tile_block = pl.BlockSpec((step_rows, CHUNKS, LANES), lambda i, *_: (i, 0, 0))
-    send_rows = call(
-        functools.partial(pack_rows_kernel, caps),
-        jax.ShapeDtypeStruct((rows, CHUNKS, LANES), BF16),
-        moved=12000000,
-        grid_spec=pltpu.PrefetchScalarGridSpec(
-            num_scalar_prefetch=1,
-            grid=(steps,),
-            in_specs=[whole((tokens, CHUNKS, LANES)), whole((CHUNKS, LANES))],
-            out_specs=tile_block,
-            scratch_shapes=[pltpu.VMEM((tokens + 1, CHUNKS, LANES), BF16)],
-        ),
-    )(table, hidden3, gain2)
-    send_grads = call(
-        functools.partial(pack_grads_kernel, caps),
-        jax.ShapeDtypeStruct((rows, CHUNKS, LANES), BF16),
-        moved=12000000,
-        grid_spec=pltpu.PrefetchScalarGridSpec(
-            num_scalar_prefetch=2,
-            grid=(steps,),
-            in_specs=[whole((tokens, CHUNKS, LANES))],
-            out_specs=tile_block,
-        ),
-    )(table, scales, grad3)
+    )(ids_t, weight_t)
+
+    pack_block = pl.BlockSpec((DESTS * caps, CHUNKS, LANES), lambda i, *_: (i, 0, 0))
 
     def exchange(array):
         return lax.all_to_all(array, both, split_axis=0, concat_axis=0, tiled=True)
 
-    got_rows = exchange(send_rows.reshape(experts, caps * 16, LANES)).reshape(rows * 16, LANES)
-    got_grads = exchange(send_grads.reshape(experts, caps * 16, LANES)).reshape(rows * 16, LANES)
+    def send(kernel, scalars, arrays, scratch):
+        packed = call(
+            kernel,
+            jax.ShapeDtypeStruct((rows, CHUNKS, LANES), BF16),
+            moved=6000000,
+            grid_spec=pltpu.PrefetchScalarGridSpec(
+                num_scalar_prefetch=len(scalars),
+                grid=(experts // DESTS,),
+                in_specs=[whole(a.shape) for a in arrays],
+                out_specs=pack_block,
+                scratch_shapes=scratch,
+            ),
+        )(*scalars, *arrays)
+        return exchange(packed.reshape(experts, caps * 16, LANES)).reshape(rows * 16, LANES)
+
+    table_scratch = [pltpu.VMEM((tokens + 1, CHUNKS, LANES), BF16)]
+    got_rows = send(pack_rows_kernel, [table], [hidden3, gain2], table_scratch)
+    got_grads = send(pack_grads_kernel, [table, scales], [grad3], [])
 
     group_len, head_cols = queries.shape
     head_count = head_cols // HEAD_DIM
@@ -373,6 +372,9 @@
         out_specs=probs_block,
     )(queries, keys, doc_start.reshape(group_len, 1))
 
+    got_rows, probs = lax.optimization_barrier((got_rows, probs))
+    step_rows = SOURCES * caps
+    steps = rows // step_rows
     flat_tiles = pl.BlockSpec((step_rows * 16, LANES), lambda i: (i, 0))
     wide = pl.BlockSpec((step_rows, width), lambda i: (i, 0))
     narrow = pl.BlockSpec((step_rows, ff), lambda i: (i, 0))
@@ -390,7 +392,7 @@
         out_specs=(wide, narrow, narrow, narrow),
     )(got_rows, swap, w_gate, w_up)
     index = np.arange(step_rows)
-    gather = jnp.asarray(index[None, :] // caps == np.arange(16)[:, None], BF16)
+    gather = jnp.asarray(index[None, :] // caps == np.arange(SOURCES)[:, None], BF16)
     spread = jnp.asarray(index[:, None] % caps == np.arange(LANES)[None, :], BF16)
     block_rows = caps * 16 + PACK_EXTRA
     scaled_grad, pre_grad, up_grad, send_back = call(
@@ -407,7 +409,7 @@
         in_specs=[
             flat_tiles,
             whole((256, 256)),
-            whole((16, step_rows)),
+            whole((SOURCES, step_rows)),
             whole((step_rows, LANES)),
             w_in,
             w_in,
@@ -420,7 +422,7 @@
             wide,
             narrow,
             narrow,
-            pl.BlockSpec((16, block_rows, LANES), lambda i: (i, 0, 0)),
+            pl.BlockSpec((SOURCES, block_rows, LANES), lambda i: (i, 0, 0)),
         ),
         scratch_shapes=[pltpu.VMEM((step_rows, width), BF16)],
     )(got_grads, swap, gather, spread, w_gate, w_up, w_down, act, act_da, act_db)
@@ -435,6 +437,9 @@
     grad_up_w = weight_grad(rows_in, up_grad)
     grad_down_w = weight_grad(act, scaled_grad)
 
+    back, grad_gate_w, grad_up_w, grad_down_w = lax.optimization_barrier(
+        (back, grad_gate_w, grad_up_w, grad_down_w)
+    )
     residual_grad = call(
         combine_kernel,
         jax.ShapeDtypeStruct((tokens, width), BF16),
@@ -443,7 +448,7 @@
             num_scalar_prefetch=2,
             grid=(1,),
             in_specs=[
-                whole((experts, block_rows, LANES)),
+                whole(back.shape),
                 whole((tokens, CHUNKS, LANES)),
                 whole((tokens, CHUNKS, LANES)),
                 whole((CHUNKS, LANES)),
@@ -455,12 +460,13 @@
                 pltpu.VMEM((tokens * CHUNKS, LANES), BF16),
             ],
         ),
-    )(expert_ids, slots, back, hidden3, grad3, gain2, swap)
-    gate_grad = call(gate_kernel, jax.ShapeDtypeStruct((tokens, top_k), BF16), moved=200000)(
-        expert_ids, slots, route_weight, back[:, caps * 16, :]
-    )
+    )(ids_t, slots, back, hidden3, grad3, gain2, swap)
+    gate_grad = call(gate_kernel, jax.ShapeDtypeStruct((top_k, tokens), BF16), moved=200000)(
+        ids_t, slots, weight_t, back[:, caps * 16, :]
+    ).T
 
     group_rows = lax.all_gather(residual_grad, "ep", axis=0, tiled=True)
+    group_rows, gate_grad = lax.optimization_barrier((group_rows, gate_grad))
     partial_w = lax.dot_general(
         group_rows, attn_out, FIRST, preferred_element_type=F32
     ).astype(BF16)

time: 347 us -> 327 us (0.942)
  blocking collectives: 72.4 us -> 0 us
  waiting for transfers between devices: 115 us -> 176 us
  Pallas kernels: 82 us -> 67.9 us
  starting transfers between devices: 24.8 us -> 31.2 us
    all_to_all x1 -> x0, blocking collectives: 72.4 us -> none  [exchange(): return lax.all_to_all(array, both, split_axis=0, concat_axis=0, tiled=True)]
    all_to_all x2 -> x3, waiting for transfers between devices: 104 us -> 146 us  [exchange(): return lax.all_to_all(array, both, split_axis=0, concat_axis=0, tiled=True)]
    all_gather x1, waiting for transfers between devices: 11.4 us -> 24 us  [per_device(): group_rows = lax.all_gather(residual_grad, 'ep', axis=0, tiled=True)]
    pallas_call x1, Pallas kernels: 28.2 us -> 18.6 us  [per_device(): call(functools.partial(expert_down_kernel, caps), (wide_shape, narrow_sha...]
    all_to_all x1, waiting for transfers between devices: 0.01 us -> 6.38 us  [per_device(): lax.all_to_all(partial_w.reshape(dp_size, width // dp_size, head_cols), '...]
    all_to_all x2 -> x3, starting transfers between devices: 18.1 us -> 24.3 us  [exchange(): return lax.all_to_all(array, both, split_axis=0, concat_axis=0, tiled=True)]
    unnamed x24 -> x20, local copies, waits for them, and re-layouts: 7.8 us -> 2.98 us
    optimization_barrier x0 -> x1, local copies, waits for them, and re-layouts: none -> 4.07 us  [per_device(): lax.optimization_barrier((back, grad_gate_w, grad_up_w, grad_down_w))]
  transfers between devices with their start and end apart: 4 -> 5, of which waited for: 3 -> 5; matrix products, arithmetic and copies ran while one was open for 8% -> 9% of each run, Pallas kernels for 10% -> 10%
where the time goes in v2:
time: 327 us; the launch traced here: 325 us
  waiting for transfers between devices  176 us (54%)
  Pallas kernels  67.9 us (21%)
  starting transfers between devices  31.2 us (10%)
  matrix products  26.5 us (8%)
  between operations  14.2 us (4%)
  local copies, waits for them, and re-layouts  8.69 us (3%)
    all_to_all x3, waiting for transfers between devices, exchange(): return lax.all_to_all(array, both, split_axis=0, concat_axis=0, tiled=True)  146 us
    all_to_all x3, starting transfers between devices, exchange(): return lax.all_to_all(array, both, split_axis=0, concat_axis=0, tiled=True)  24.3 us
    all_gather x1, waiting for transfers between devices, per_device(): group_rows = lax.all_gather(residual_grad, 'ep', axis=0, tiled=True)  24 us
    pallas_call x1, Pallas kernels, per_device(): call(functools.partial(expert_down_kernel, caps), (wide_shape, narrow_sha...  18.6 us
    dot_general x3, matrix products, weight_grad(): product = lax.dot_general(left, right, FIRST, preferred_element_type=F32)  17.8 us
    pallas_call x2, Pallas kernels, send(): call(kernel, jax.ShapeDtypeStruct((rows, CHUNKS, LANES), BF16), moved=600...  14.8 us
    pallas_call x1, Pallas kernels, per_device(): call(expert_up_kernel, (wide_shape, narrow_shape, narrow_shape, narrow_sh...  11.7 us
    pallas_call x1, Pallas kernels, per_device(): call(combine_kernel, jax.ShapeDtypeStruct((tokens, width), BF16), moved=8...  8.5 us
  transfers between devices with their start and end apart: 5, of which 5 were waited for; matrix products, arithmetic and copies ran while one was open for 9% of the time, Pallas kernels for 10%

profile of v2, /device:TPU:1, one launch (start us, length us, event | category | flops | bytes accessed | tf_op | source)
XLA Modules:
  0.0 325.3 jit_solution(14581155588988694133)
XLA Ops:
  7.2 0.0 copy-start
  7.2 2.0 copy.34
  9.2 1.9 shard_map.232
  11.2 6.6 %shard_map.234 = bf16[1280,16,128]{2,1,0:T(8,128)(2,1)} custom-call(s32[128,128]{1,0:T(8,128)} %get-tuple-element.32.table_ref, bf16[128,16,128]{2,1,0:T(8,128)(2,1)} %bitcast.34, bf16[16,128]{1,0:T(8,128)(2,1)} %bitcast.43), custom_call_target="tpu_custom_call" | custom-call | bytes 6000000 | tf_op jit(solution)/shard_map/pallas_call | solution.py:342
  17.8 0.0 copy-start.2
  17.8 11.9 %all-to-all-start.1 = ((bf16[128,160,128]{2,1,0:T(8,128)(2,1)}), bf16[128,160,128]{2,1,0:T(8,128)(2,1)}, u32[]{:S(2)}, u32[]{:S(2)}) async-start(bf16[128,160,128]{2,1,0:T(8,128)(2,1)} %bitcast.33), calls=%async_computation.1 | async-start | bytes 10485760 | tf_op jit(solution)/shard_map/all_to_all | solution.py:339
  29.7 0.0 copy-done.2
  29.7 0.9 copy.33
  30.6 8.2 %shard_map.233 = bf16[1280,16,128]{2,1,0:T(8,128)(2,1)} custom-call(s32[128,128]{1,0:T(8,128)} %get-tuple-element.32.table_ref, f32[128,128]{1,0:T(8,128)} %get-tuple-element.33.scale_ref, bf16[128,16,128]{2,1,0:T(8,128)(2,1)} %bitcast.36), custom_call_target="tpu_custom_call" | custom-call | bytes 6000000 | tf_op jit(solution)/shard_map/pallas_call | solution.py:342
  38.8 53.4 %all-to-all-done.1 = bf16[128,160,128]{2,1,0:T(8,128)(2,1)} async-done(((bf16[128,160,128]{2,1,0:T(8,128)(2,1)}), bf16[128,160,128]{2,1,0:T(8,128)(2,1)}, u32[]{:S(2)}, u32[]{:S(2)}) %all-to-all-start.1) | async-done | bytes 5242912 | tf_op jit(solution)/shard_map/all_to_all | solution.py:339
  92.2 0.0 copy-start.3
  92.2 6.2 %all-to-all-start = ((bf16[128,160,128]{2,1,0:T(8,128)(2,1)}), bf16[128,160,128]{2,1,0:T(8,128)(2,1)}, u32[]{:S(2)}, u32[]{:S(2)}) async-start(bf16[128,160,128]{2,1,0:T(8,128)(2,1)} %bitcast.32), calls=%async_computation | async-start | bytes 10485760 | tf_op jit(solution)/shard_map/all_to_all | solution.py:339
  98.4 0.0 copy-done.3
  98.4 1.0 copy.31.begin_ref
  99.5 4.9 %shard_map.235.probs_ref = bf16[2,2,512,512]{3,2,1,0:T(8,128)(2,1)} custom-call(bf16[1024,256]{1,0:T(8,128)(2,1)} %query_ref.3, bf16[1024,256]{1,0:T(8,128)(2,1)} %key_ref.3, s32[1024,1]{1,0:T(8,128)} %copy.31.begin_ref), custom_call_target="tpu_custom_call" | custom-call | flops 10000000000 | bytes 5000000 | tf_op jit(solution)/shard_map/pallas_call | solution.py:365
  104.4 11.7 %shard_map.236 = (bf16[1280,2048]{1,0:T(8,128)(2,1)}, bf16[1280,512]{1,0:T(8,128)(2,1)}, bf16[1280,512]{1,0:T(8,128)(2,1)}, bf16[1280,512]{1,0:T(8,128)(2,1)}) custom-call(bf16[20480,128]{1,0:T(8,128)(2,1)} %bitcast.6.tile_ref, bf16[256,256]{1,0:T(8,128)(2,1)} %constant.5.clone.swap_ref, bf16[1,2048,512]{2,1,0:T(8,128)(2,1)} %gate_w_ref.3, ...), custom_call_target="tpu_custom_call" | custom-call | flops 5368709120 | bytes 18000000 | tf_op jit(solution)/shard_map/pallas_call | solution.py:385
  116.1 44.8 %all-to-all-done = bf16[128,160,128]{2,1,0:T(8,128)(2,1)} async-done(((bf16[128,160,128]{2,1,0:T(8,128)(2,1)}), bf16[128,160,128]{2,1,0:T(8,128)(2,1)}, u32[]{:S(2)}, u32[]{:S(2)}) %all-to-all-start) | async-done | bytes 5242912 | tf_op jit(solution)/shard_map/all_to_all | solution.py:339
  160.9 18.6 %shard_map.237 = (bf16[1280,2048]{1,0:T(8,128)(2,1)}, bf16[1280,512]{1,0:T(8,128)(2,1)}, bf16[1280,512]{1,0:T(8,128)(2,1)}, bf16[128,168,128]{2,1,0:T(8,128)(2,1)}) custom-call(bf16[20480,128]{1,0:T(8,128)(2,1)} %bitcast.3.tile_ref, bf16[256,256]{1,0:T(8,128)(2,1)} %constant.5.clone.swap_ref, bf16[32,320]{1,0:T(8,128)(2,1)} %constant.14.clone.gather_ref, ...), custom_call_target="tpu_custom_call" | custom-call | flops 8053063680 | bytes 25000000 | tf_op jit(solution)/shard_map/pallas_call | solution.py:398
  179.5 0.0 copy-start.4
  179.5 6.2 %all-to-all-start.2 = ((bf16[128,168,128]{2,1,0:T(8,128)(2,1)}), bf16[128,168,128]{2,1,0:T(8,128)(2,1)}, u32[]{:S(2)}, u32[]{:S(2)}) async-start(bf16[128,168,128]{2,1,0:T(8,128)(2,1)} %get-tuple-element.38), calls=%async_computation.2 | async-start | bytes 11010048 | tf_op jit(solution)/shard_map/all_to_all | solution.py:339
  185.7 0.2 all-gather.2.cloned.1.call-start
  185.9 0.0 copy-done.4
  185.9 0.0 copy-start.6
  185.9 0.0 slice-start
  186.0 6.7 %fusion.2 = bf16[1,512,2048]{2,1,0:T(8,128)(2,1)} fusion(bf16[1280,512]{1,0:T(8,128)(2,1)S(1)} %copy-done.4, bf16[1280,2048]{1,0:T(8,128)(2,1)} %get-tuple-element.42), kind=kOutput, calls=%fused_computation.5 | convolution fusion | flops 2686451712 | bytes 8650752 | tf_op jit(solution)/shard_map/dot_general | solution.py:433
  192.7 0.0 copy-done.6
  192.7 6.9 %fusion = bf16[1,2048,512]{2,1,0:T(8,128)(2,1)} fusion(bf16[1280,2048]{1,0:T(8,128)(2,1)} %get-tuple-element.39, bf16[1280,512]{1,0:T(8,128)(2,1)S(1)} %copy-done.6), kind=kOutput, calls=%fused_computation.3 | convolution fusion | flops 2686451712 | bytes 8650752 | tf_op jit(solution)/shard_map/dot_general | solution.py:433
  199.6 0.0 slice-done
  199.6 0.0 slice-done.1
  199.6 0.0 copy-done.5
  199.6 4.1 %fusion.1 = bf16[1,2048,512]{2,1,0:T(8,128)(2,1)} fusion(bf16[1280,2048]{1,0:T(8,128)(2,1)S(1)} %bitcast.50, bf16[1280,512]{1,0:T(8,128)(2,1)S(1)} %copy-done.5), kind=kOutput, calls=%fused_computation.4 | convolution fusion | flops 2686451712 | bytes 8650752 | tf_op jit(solution)/shard_map/dot_general | solution.py:433
  203.8 47.3 %all-to-all-done.2.back_ref = bf16[128,168,128]{2,1,0:T(8,128)(2,1)} async-done(((bf16[128,168,128]{2,1,0:T(8,128)(2,1)}), bf16[128,168,128]{2,1,0:T(8,128)(2,1)}, u32[]{:S(2)}, u32[]{:S(2)}) %all-to-all-start.2) | async-done | bytes 5505056 | tf_op jit(solution)/shard_map/all_to_all | solution.py:339
  251.0 8.5 %shard_map.238 = bf16[128,2048]{1,0:T(8,128)(2,1)} custom-call(s32[8,128]{1,0:T(8,128)} %bitcast.41, s32[8,128]{1,0:T(8,128)} %get-tuple-element.31.slot_ref, bf16[128,168,128]{2,1,0:T(8,128)(2,1)} %all-to-all-done.2.back_ref, bf16[128,16,128]{2,1,0:T(8,128)(2,1)} %bitcast.35, bf16[128,16,128]{2,1,0:T(8,128)(2,1)} %bitcast.37, bf16[16,128]{1,0:T(8,128)(2,1)} %bitcast.44, ...), custom_call_target="tpu_custom_call" | custom-call | bytes 8000000 | tf_op jit(solution)/shard_map/pallas_call | solution.py:443
  259.5 0.0 all-gather.2.cloned.1.call-update
  259.6 0.0 copy-start.1
  259.6 4.1 %copy.32 = bf16[128,168,128]{2,0,1:T(8,128)(2,1)S(1)} copy(bf16[128,168,128]{2,1,0:T(8,128)(2,1)} %all-to-all-done.2.back_ref) | data formatting | bytes 11010048 | tf_op jit(solution)/shard_map/optimization_barrier | solution.py:440
  263.6 0.6 slice_bitcast_fusion.score_ref
  264.3 1.6 shard_map.239
  265.9 24.0 %all-gather.2.cloned.1.call-done = bf16[1024,2048]{1,0:T(8,128)(2,1)} async-done(((bf16[128,2048]{1,0:T(8,128)(2,1)}), bf16[1024,2048]{1,0:T(8,128)(2,1)}) %all-gather.2.cloned.1.call-update) | async-done | bytes 4194320 | tf_op jit(solution)/shard_map/all_gather | solution.py:468
  289.9 0.0 copy-done.1
  290.0 4.5 %convolution_convert_fusion = bf16[2048,256]{1,0:T(8,128)(2,1)} fusion(bf16[1024,2048]{1,0:T(8,128)(2,1)} %all-gather.2.cloned.1.call-done, bf16[1024,256]{1,0:T(8,128)(2,1)S(1)} %copy-done.1), kind=kOutput, calls=%fused_computation.6 | convolution fusion | flops 1074266112 | bytes 5767168 | tf_op jit(solution)/shard_map/dot_general | solution.py:470
  294.5 6.7 %all-to-all-start.3 = ((bf16[16,128,256]{2,1,0:T(8,128)(2,1)}), bf16[16,128,256]{2,1,0:T(8,128)(2,1)S(1)}, u32[]{:S(2)}, u32[]{:S(2)}) async-start(bf16[16,128,256]{2,1,0:T(8,128)(2,1)} %bitcast.13), calls=%async_computation.3 | async-start | bytes 2097152 | tf_op jit(solution)/shard_map/all_to_all | solution.py:473
  301.1 0.0 copy-done
  301.2 4.2 %convolution_convert_fusion.1.grad_ref = bf16[1024,256]{1,0:T(8,128)(2,1)} fusion(bf16[1024,2048]{1,0:T(8,128)(2,1)} %all-gather.2.cloned.1.call-done, bf16[2048,256]{1,0:T(8,128)(2,1)S(1)} %copy-done), kind=kOutput, calls=%fused_computation.8 | convolution fusion | flops 1074003968 | bytes 5767168 | tf_op jit(solution)/shard_map/dot_general | solution.py:483
  305.4 5.8 %shard_map.240 = (bf16[1024,256]{1,0:T(8,128)(2,1)}, bf16[1024,256]{1,0:T(8,128)(2,1)}, bf16[1024,256]{1,0:T(8,128)(2,1)}) custom-call(bf16[2,2,512,512]{3,2,1,0:T(8,128)(2,1)} %shard_map.235.probs_ref, bf16[1024,256]{1,0:T(8,128)(2,1)} %query_ref.3, bf16[1024,256]{1,0:T(8,128)(2,1)} %key_ref.3, bf16[1024,256]{1,0:T(8,128)(2,1)} %value_ref.1, ...), custom_call_target="tpu_custom_call" | custom-call | flops 1073741824 | bytes 6000000 | tf_op jit(solution)/shard_map/pallas_call | solution.py:485
  311.2 6.4 %all-to-all-done.3 = bf16[16,128,256]{2,1,0:T(8,128)(2,1)S(1)} async-done(((bf16[16,128,256]{2,1,0:T(8,128)(2,1)}), bf16[16,128,256]{2,1,0:T(8,128)(2,1)S(1)}, u32[]{:S(2)}, u32[]{:S(2)}) %all-to-all-start.3) | async-done | bytes 1048608 | tf_op jit(solution)/shard_map/all_to_all | solution.py:473
  317.6 0.1 convert_reduce_fusion
  317.8 0.6 multiply_convert_fusion.3
  (3 shorter events, 0.0 us)
Async XLA Ops:
  7.2 294.0 %copy-start = (bf16[2048,256]{1,0:T(8,128)(2,1)S(1)}, bf16[2048,256]{1,0:T(8,128)(2,1)}, u32[]{:S(2)}) copy-start(bf16[2048,256]{1,0:T(8,128)(2,1)} %param.29) | copy-start | bytes 3145732
  17.8 11.9 %copy-start.2 = (bf16[128,2048]{1,0:T(8,128)(2,1)S(1)}, bf16[128,2048]{1,0:T(8,128)(2,1)}, u32[]{:S(2)}) copy-start(bf16[128,2048]{1,0:T(8,128)(2,1)} %param.18) | copy-start | bytes 1572868
  17.8 74.4 %all-to-all-start.1 = ((bf16[128,160,128]{2,1,0:T(8,128)(2,1)}), bf16[128,160,128]{2,1,0:T(8,128)(2,1)}, u32[]{:S(2)}, u32[]{:S(2)}) async-start(bf16[128,160,128]{2,1,0:T(8,128)(2,1)} %bitcast.33), calls=%async_computation.1 | async-start | bytes 10485760 | tf_op jit(solution)/shard_map/all_to_all | solution.py:339
  92.2 6.2 %copy-start.3 = (s32[1024]{0:T(1024)S(1)}, s32[1024]{0:T(1024)}, u32[]{:S(2)}) copy-start(s32[1024]{0:T(1024)} %param.30) | copy-start | bytes 12292
  92.2 68.7 %all-to-all-start = ((bf16[128,160,128]{2,1,0:T(8,128)(2,1)}), bf16[128,160,128]{2,1,0:T(8,128)(2,1)}, u32[]{:S(2)}, u32[]{:S(2)}) async-start(bf16[128,160,128]{2,1,0:T(8,128)(2,1)} %bitcast.32), calls=%async_computation | async-start | bytes 10485760 | tf_op jit(solution)/shard_map/all_to_all | solution.py:339
  179.5 6.4 %copy-start.4 = (bf16[1280,512]{1,0:T(8,128)(2,1)S(1)}, bf16[1280,512]{1,0:T(8,128)(2,1)}, u32[]{:S(2)}) copy-start(bf16[1280,512]{1,0:T(8,128)(2,1)} %get-tuple-element.35.act_ref) | copy-start | bytes 3932164
  179.5 71.5 %all-to-all-start.2 = ((bf16[128,168,128]{2,1,0:T(8,128)(2,1)}), bf16[128,168,128]{2,1,0:T(8,128)(2,1)}, u32[]{:S(2)}, u32[]{:S(2)}) async-start(bf16[128,168,128]{2,1,0:T(8,128)(2,1)} %get-tuple-element.38), calls=%async_computation.2 | async-start | bytes 11010048 | tf_op jit(solution)/shard_map/all_to_all | solution.py:339
  185.7 104.3 %all-gather.2.cloned.1.call-start = ((), (), s32[]{:S(2)}) async-start(), calls=%async_computation.4 | async-start | bytes 4718592 | tf_op jit(solution)/shard_map/all_gather | solution.py:468
  185.9 6.8 %copy-start.6 = (bf16[1280,512]{1,0:T(8,128)(2,1)S(1)}, bf16[1280,512]{1,0:T(8,128)(2,1)}, u32[]{:S(2)}) copy-start(bf16[1280,512]{1,0:T(8,128)(2,1)} %get-tuple-element.40) | copy-start | bytes 3932164
  185.9 13.7 %slice-start = ((s8[5242880]{0:T(1024)(128)(4,1)}), s8[4194304]{0:T(1024)(128)(4,1)S(1)}, s32[]{:S(2)}) async-start(s8[5242880]{0:T(1024)(128)(4,1)} %bitcast.49), calls=%async_computation.5 | async-start | bytes 8388608
  192.7 6.9 %slice-start.1 = ((s8[5242880]{0:T(1024)(128)(4,1)}), s8[1048576]{0:T(1024)(128)(4,1)S(1)}, s32[]{:S(2)}) async-start(s8[5242880]{0:T(1024)(128)(4,1)} %bitcast.49), calls=%async_computation.6 | async-start | bytes 2097152
  192.7 6.9 %copy-start.5 = (bf16[1280,512]{1,0:T(8,128)(2,1)S(1)}, bf16[1280,512]{1,0:T(8,128)(2,1)}, u32[]{:S(2)}) copy-start(bf16[1280,512]{1,0:T(8,128)(2,1)} %get-tuple-element.41) | copy-start | bytes 3932164
  259.6 30.4 %copy-start.1 = (bf16[1024,256]{1,0:T(8,128)(2,1)S(1)}, bf16[1024,256]{1,0:T(8,128)(2,1)}, u32[]{:S(2)}) copy-start(bf16[1024,256]{1,0:T(8,128)(2,1)} %attn_ref.1) | copy-start | bytes 1572868
  294.5 23.2 %all-to-all-start.3 = ((bf16[16,128,256]{2,1,0:T(8,128)(2,1)}), bf16[16,128,256]{2,1,0:T(8,128)(2,1)S(1)}, u32[]{:S(2)}, u32[]{:S(2)}) async-start(bf16[16,128,256]{2,1,0:T(8,128)(2,1)} %bitcast.13), calls=%async_computation.3 | async-start | bytes 2097152 | tf_op jit(solution)/shard_map/all_to_all | solution.py:473
Sparse Core Ops, SparseCore 0:
  259.7 30.2 all-gather.1

commit v3 on v2

--- a/solution.py
+++ b/solution.py
@@ -15,6 +15,7 @@
 CHUNKS = 16
 F32 = jnp.float32
 BF16 = jnp.bfloat16
+MESH = pl.DeviceIdType.MESH
 LAST = (((1,), (1,)), ((), ()))
 FIRST = (((0,), (0,)), ((), ()))
 PACK_EXTRA = 8
@@ -210,7 +211,20 @@
 
 
 def combine_kernel(
-    ids_ref, slot_ref, back_ref, hidden_ref, grad_ref, gain_ref, swap_ref, out_ref, total, tiles
+    ids_ref,
+    slot_ref,
+    back_ref,
+    hidden_ref,
+    grad_ref,
+    gain_ref,
+    swap_ref,
+    id_lanes,
+    slot_lanes,
+    weight_ref,
+    out_ref,
+    gate_ref,
+    total,
+    tiles,
 ):
     top_k, tokens = ids_ref.shape
 
@@ -243,22 +257,23 @@
     tiles_to_rows(
         lambda i: tiles[i * 256 : (i + 1) * 256], swap_ref[...], out_ref, tokens // 32
     )
-
-
-def gate_kernel(ids_ref, slot_ref, weight_ref, score_ref, out_ref):
-    top_k, tokens = ids_ref.shape
+    extra = back_ref[:, back_ref.shape[1] - PACK_EXTRA :, :].astype(F32)
+    score = (jnp.sum(extra, axis=1) * (1.0 / PACK_EXTRA)).astype(BF16)
+    write_gate(id_lanes[...], slot_lanes[...], weight_ref[...], score, gate_ref)
+
+
+def write_gate(ids, slot, weight, score, out_ref):
+    top_k, tokens = ids.shape
     row = lax.broadcasted_iota(jnp.int32, (LANES, tokens), 0)
-    ids = ids_ref[...]
-    slot = slot_ref[...]
     found = []
     for k in range(top_k):
         hit = jnp.where(ids[k : k + 1] == row, 1.0, 0.0).astype(BF16)
-        mine = lax.dot_general(score_ref[...], hit, FIRST, preferred_element_type=F32)
+        mine = lax.dot_general(score, hit, FIRST, preferred_element_type=F32)
         found.append(
             jnp.sum(jnp.where(slot[k : k + 1] == row, mine, 0.0), axis=0, keepdims=True)
         )
     scale = (CHUNKS * LANES) ** (-0.5)
-    value = jnp.concatenate(found, axis=0) * scale / weight_ref[...].astype(F32)
+    value = jnp.concatenate(found, axis=0) * scale / weight.astype(F32)
     out_ref[...] = value.astype(BF16)
 
 
@@ -275,22 +290,217 @@
     out_ref[0, 0] = (weights / jnp.sum(weights, axis=1, keepdims=True)).astype(BF16)
 
 
-def attention_kernel(
-    probs_ref, query_ref, key_ref, value_ref, attn_ref, grad_ref, dq_ref, dk_ref, dv_ref
+def tail_kernel(
+    sum_scale,
+    resid_hbm,
+    weight_hbm,
+    attn_hbm,
+    probs_hbm,
+    query_hbm,
+    key_hbm,
+    value_hbm,
+    dq_ref,
+    dk_ref,
+    dv_ref,
+    out_ref,
+    group,
+    weight,
+    attn,
+    probs,
+    query,
+    key,
+    value,
+    grads,
+    acc,
+    pieces,
+    arrived,
+    load_sems,
+    ring_send,
+    ring_recv,
+    side_send,
+    side_recv,
+    dp_send,
+    dp_recv,
 ):
-    probs = probs_ref[0, 0]
-    grad = grad_ref[...]
-    delta = jnp.sum(grad.astype(F32) * attn_ref[...].astype(F32), axis=1, keepdims=True)
-    prob_grad = lax.dot_general(grad, value_ref[...], LAST, preferred_element_type=F32)
-    score_grad = (probs.astype(F32) * (prob_grad - delta)).astype(BF16)
+    ep, dp = lax.axis_index("ep"), lax.axis_index("dp")
+    chips = lax.axis_size("ep") // 2
+    dp_size = lax.axis_size("dp")
+    chip, core = ep // 2, ep % 2
+    tokens, width = resid_hbm.shape
+    half = tokens // 2
+    above = ((chip + 1) % chips) * 2 + core
+    below = ((chip + chips - 1) % chips) * 2 + core
+    across = ((chip + 2) % chips) * 2 + core
+    sibling = chip * 2 + 1 - core
+
+    barrier = pltpu.get_barrier_semaphore()
+    for peer in (above, below, sibling):
+        pl.semaphore_signal(barrier, inc=1, device_id=(peer, dp), device_id_type=MESH)
+    for step in range(1, dp_size):
+        pl.semaphore_signal(
+            barrier, inc=1, device_id=(ep, (dp + step) % dp_size), device_id_type=MESH
+        )
+
+    loads = [
+        pltpu.make_async_copy(source, target, load_sems.at[number])
+        for number, (source, target) in enumerate(
+            (
+                (resid_hbm, group.at[pl.ds(pl.multiple_of(ep * tokens, tokens), tokens)]),
+                (weight_hbm, weight),
+                (attn_hbm, attn),
+                (query_hbm, query),
+                (key_hbm, key),
+                (value_hbm, value),
+                (probs_hbm, probs),
+            )
+        )
+    ]
+    for load in loads:
+        load.start()
+    loads[0].wait()
+    pl.semaphore_wait(barrier, dp_size - 1 + 3)
+
+    def part(owner, second):
+        at = pl.multiple_of(owner * tokens + second * half, half)
+        return group.at[pl.ds(at, half)]
+
+    def ring(number, owner, second, target):
+        return pltpu.make_async_remote_copy(
+            src_ref=part(owner, second),
+            dst_ref=part(owner, second),
+            send_sem=ring_send.at[number],
+            recv_sem=ring_recv.at[number],
+            device_id=(target, dp),
+            device_id_type=MESH,
+        )
+
+    def side(number, owner, second):
+        return pltpu.make_async_remote_copy(
+            src_ref=part(owner, second),
+            dst_ref=part(owner, second),
+            send_sem=side_send.at[number],
+            recv_sem=side_recv.at[number],
+            device_id=(sibling, dp),
+            device_id_type=MESH,
+        )
+
+    up = [ring(0, ep, 0, above), ring(1, ep, 1, above)]
+    down = [ring(3, ep, 0, below), ring(2, ep, 1, below)]
+    own = [side(0, ep, 0), side(1, ep, 1)]
+    for copy in (up[0], down[1], own[0], own[1], up[1], down[0]):
+        copy.start()
+
+    def matmuls(pair, last):
+        at = pl.multiple_of(pair * 2 * tokens, 2 * tokens)
+        mine = pl.ds(at, 2 * tokens)
+        grads[mine] = jnp.dot(group[mine], weight[...], preferred_element_type=F32).astype(BF16)
+
+        def add(step, carry):
+            dest = (dp + 1 + step) % dp_size
+            columns = pl.ds(pl.multiple_of(dest * tokens, tokens), tokens)
+            product = lax.dot_general(
+                group[mine, columns], attn[mine], FIRST, preferred_element_type=F32
+            )
+            if last is None:
+                acc[dest] = product
+            elif not last:
+                acc[dest] = acc[dest] + product
+            else:
+                pieces[dest] = (acc[dest] + product).astype(BF16)
+            return carry
+
+        if not last:
+            lax.fori_loop(0, dp_size, add, 0)
+        else:
+            for step in range(dp_size):
+                add(step, 0)
+                if step < dp_size - 1:
+                    send_piece(step).start()
+
+    def send_piece(step):
+        dest = (dp + 1 + step) % dp_size
+        return pltpu.make_async_remote_copy(
+            src_ref=pieces.at[dest],
+            dst_ref=arrived.at[dp],
+            send_sem=dp_send.at[step],
+            recv_sem=dp_recv.at[step],
+            device_id=(ep, dest),
+            device_id_type=MESH,
+        )
+
+    own[0].wait_recv()
+    own[1].wait_recv()
+    loads[1].wait()
+    loads[2].wait()
+    matmuls(chip, None)
+
+    up[0].wait_recv()
+    forward_up = ring(4, below, 0, above)
+    forward_up.start()
+    relay = [side(2, below, 0)]
+    relay[0].start()
+    down[1].wait_recv()
+    forward_down = ring(5, above, 1, below)
+    forward_down.start()
+    relay.append(side(3, above, 1))
+    relay[1].start()
+    up[1].wait_recv()
+    relay.append(side(4, below, 1))
+    relay[2].start()
+    down[0].wait_recv()
+    relay.append(side(5, above, 0))
+    relay[3].start()
+    for copy in relay:
+        copy.wait_recv()
+    matmuls(below // 2, False)
+    matmuls(above // 2, False)
+    forward_up.wait_recv()
+    relay.append(side(6, across, 0))
+    relay[4].start()
+    forward_down.wait_recv()
+    relay.append(side(7, across, 1))
+    relay[5].start()
+    relay[4].wait_recv()
+    relay[5].wait_recv()
+    matmuls(across // 2, True)
+
+    for load in loads[3:]:
+        load.wait()
+    heads = query.shape[1] // HEAD_DIM
     scale = HEAD_DIM ** (-0.5)
-    dq_ref[...] = (
-        jnp.dot(score_grad, key_ref[...], preferred_element_type=F32) * scale
-    ).astype(BF16)
-    dk_ref[...] = (
-        lax.dot_general(score_grad, query_ref[...], FIRST, preferred_element_type=F32) * scale
-    ).astype(BF16)
-    dv_ref[...] = lax.dot_general(probs, grad, FIRST, preferred_element_type=F32).astype(BF16)
+
+    def attend(number, carry):
+        seq, head = number // heads, number % heads
+        at = (
+            pl.ds(pl.multiple_of(seq * SEQ, SEQ), SEQ),
+            pl.ds(pl.multiple_of(head * HEAD_DIM, HEAD_DIM), HEAD_DIM),
+        )
+        grad = grads[at]
+        weights = probs[number]
+        delta = jnp.sum(grad.astype(F32) * attn[at].astype(F32), axis=1, keepdims=True)
+        prob_grad = lax.dot_general(grad, value[at], LAST, preferred_element_type=F32)
+        score_grad = (weights.astype(F32) * (prob_grad - delta)).astype(BF16)
+        dq_ref[at] = (
+            jnp.dot(score_grad, key[at], preferred_element_type=F32) * scale
+        ).astype(BF16)
+        dk_ref[at] = (
+            lax.dot_general(score_grad, query[at], FIRST, preferred_element_type=F32) * scale
+        ).astype(BF16)
+        dv_ref[at] = lax.dot_general(weights, grad, FIRST, preferred_element_type=F32).astype(BF16)
+        return carry
+
+    lax.fori_loop(0, probs.shape[0], attend, 0)
+
+    for step in range(dp_size - 1):
+        send_piece(step).wait_recv()
+    total = pieces[dp].astype(F32)
+    for step in range(1, dp_size):
+        total = total + arrived[(dp + step) % dp_size].astype(F32)
+    out_ref[...] = (total * sum_scale).astype(BF16)
+    for copy in up + down + own + relay + [forward_up, forward_down]:
+        copy.wait_send()
+    for step in range(dp_size - 1):
+        send_piece(step).wait_send()
 
 
 def per_device(
@@ -440,9 +650,12 @@
     back, grad_gate_w, grad_up_w, grad_down_w = lax.optimization_barrier(
         (back, grad_gate_w, grad_up_w, grad_down_w)
     )
-    residual_grad = call(
+    residual_grad, gate_grad = call(
         combine_kernel,
-        jax.ShapeDtypeStruct((tokens, width), BF16),
+        (
+            jax.ShapeDtypeStruct((tokens, width), BF16),
+            jax.ShapeDtypeStruct((top_k, tokens), BF16),
+        ),
         moved=8000000,
         grid_spec=pltpu.PrefetchScalarGridSpec(
             num_scalar_prefetch=2,
@@ -453,44 +666,69 @@
                 whole((tokens, CHUNKS, LANES)),
                 whole((CHUNKS, LANES)),
                 whole((256, 256)),
+                whole((top_k, tokens)),
+                whole((top_k, tokens)),
+                whole((top_k, tokens)),
             ],
-            out_specs=whole((tokens, width)),
+            out_specs=(whole((tokens, width)), whole((top_k, tokens))),
             scratch_shapes=[
                 pltpu.VMEM((tokens, CHUNKS, LANES), F32),
                 pltpu.VMEM((tokens * CHUNKS, LANES), BF16),
             ],
         ),
-    )(ids_t, slots, back, hidden3, grad3, gain2, swap)
-    gate_grad = call(gate_kernel, jax.ShapeDtypeStruct((top_k, tokens), BF16), moved=200000)(
-        ids_t, slots, weight_t, back[:, caps * 16, :]
-    ).T
-
-    group_rows = lax.all_gather(residual_grad, "ep", axis=0, tiled=True)
-    group_rows, gate_grad = lax.optimization_barrier((group_rows, gate_grad))
-    partial_w = lax.dot_general(
-        group_rows, attn_out, FIRST, preferred_element_type=F32
-    ).astype(BF16)
-    pieces = lax.all_to_all(
-        partial_w.reshape(dp_size, width // dp_size, head_cols),
-        "dp",
-        split_axis=0,
-        concat_axis=0,
-        tiled=True,
+    )(ids_t, slots, back, hidden3, grad3, gain2, swap, ids_t, slots, weight_t)
+    gate_grad = gate_grad.T
+
+    any_spec = pl.BlockSpec(memory_space=pl.ANY)
+    vmem_spec = pl.BlockSpec(memory_space=pltpu.VMEM)
+    head_shape = jax.ShapeDtypeStruct((group_len, head_cols), BF16)
+    head_vmem = pltpu.VMEM((group_len, head_cols), BF16)
+    piece_shape = (dp_size, width // dp_size, head_cols)
+    query_grad, key_grad, value_grad, out_weight_grad = pl.pallas_call(
+        functools.partial(tail_kernel, (group_len * dp_size) ** (-0.5)),
+        out_shape=(
+            head_shape,
+            head_shape,
+            head_shape,
+            jax.ShapeDtypeStruct(piece_shape[1:], BF16),
+        ),
+        in_specs=[any_spec] * 7,
+        out_specs=(vmem_spec,) * 4,
+        scratch_shapes=[
+            pltpu.VMEM((group_len, width), BF16),
+            pltpu.VMEM((width, head_cols), BF16),
+            head_vmem,
+            pltpu.VMEM((seq_count * head_count, SEQ, SEQ), BF16),
+            head_vmem,
+            head_vmem,
+            head_vmem,
+            head_vmem,
+            pltpu.VMEM(piece_shape, F32),
+            pltpu.VMEM(piece_shape, BF16),
+            pltpu.VMEM(piece_shape, BF16),
+            pltpu.SemaphoreType.DMA((7,)),
+            pltpu.SemaphoreType.DMA((6,)),
+            pltpu.SemaphoreType.DMA((6,)),
+            pltpu.SemaphoreType.DMA((8,)),
+            pltpu.SemaphoreType.DMA((8,)),
+            pltpu.SemaphoreType.DMA((dp_size - 1,)),
+            pltpu.SemaphoreType.DMA((dp_size - 1,)),
+        ],
+        compiler_params=pltpu.CompilerParams(
+            collective_id=0, has_side_effects=True, vmem_limit_bytes=VMEM_LIMIT
+        ),
+        cost_estimate=pl.CostEstimate(
+            flops=4 * 10**9, bytes_accessed=20000000, transcendentals=0
+        ),
+    )(
+        residual_grad,
+        out_weight,
+        attn_out,
+        probs.reshape(seq_count * head_count, SEQ, SEQ),
+        queries,
+        keys,
+        values,
     )
-    out_weight_grad = (
-        jnp.sum(pieces.astype(F32), axis=0) * (group_len * dp_size) ** (-0.5)
-    ).astype(BF16)
-    attn_grad = jnp.dot(group_rows, out_weight, preferred_element_type=F32).astype(BF16)
-    head_shape = jax.ShapeDtypeStruct((group_len, head_cols), BF16)
-    query_grad, key_grad, value_grad = call(
-        attention_kernel,
-        (head_shape, head_shape, head_shape),
-        flops=4 * 8 * SEQ * SEQ * HEAD_DIM,
-        moved=6000000,
-        grid=(seq_count, head_count),
-        in_specs=[probs_block] + [head_block] * 5,
-        out_specs=(head_block, head_block, head_block),
-    )(probs, queries, keys, values, attn_out, attn_grad)
     return (
         gate_grad,
         grad_gate_w,

time: 327 us -> 306 us (0.936)
  Pallas kernels: 67.9 us -> 105 us
  waiting for transfers between devices: 176 us -> 146 us
  between operations: 14.2 us -> 0.74 us
  matrix products: 26.5 us -> 17.8 us
  starting transfers between devices: 31.2 us -> 24.3 us
    pallas_call x3 -> x2, Pallas kernels: 16 us -> 53.4 us  [the longest x1 44.8 us: per_device(): pl.pallas_call(functools.partial(tail_kernel, (group_len * dp_size) ** (-...]
    all_gather x1 -> x0, waiting for transfers between devices: 24 us -> none  [per_device(): group_rows = lax.all_gather(residual_grad, 'ep', axis=0, tiled=True)]
    dot_general x2 -> x0, matrix products: 8.77 us -> none  [the longest x1 4.52 us: per_device(): lax.dot_general(group_rows, attn_out, FIRST, preferred_element_type=F32)]
    unnamed x20, local copies, waits for them, and re-layouts: 2.98 us -> 9.95 us
    all_to_all x1 -> x0, starting transfers between devices: 6.66 us -> none  [per_device(): lax.all_to_all(partial_w.reshape(dp_size, width // dp_size, head_cols), '...]
    all_to_all x1 -> x0, waiting for transfers between devices: 6.38 us -> none  [per_device(): lax.all_to_all(partial_w.reshape(dp_size, width // dp_size, head_cols), '...]
    optimization_barrier x1 -> x0, local copies, waits for them, and re-layouts: 4.07 us -> none  [per_device(): lax.optimization_barrier((back, grad_gate_w, grad_up_w, grad_down_w))]
  transfers between devices with their start and end apart: 5 -> 3, of which waited for: 5 -> 3; matrix products, arithmetic and copies ran while one was open for 9% -> 6% of each run, Pallas kernels for 10% -> 8%
where the time goes in v3:
time: 306 us; the launch traced here: 305 us
  waiting for transfers between devices  146 us (48%)
  Pallas kernels  105 us (34%)
  starting transfers between devices  24.3 us (8%)
  matrix products  17.8 us (6%)
  local copies, waits for them, and re-layouts  11 us (4%)
    all_to_all x3, waiting for transfers between devices, exchange(): return lax.all_to_all(array, both, split_axis=0, concat_axis=0, tiled=True)  146 us
    pallas_call x1, Pallas kernels, per_device(): pl.pallas_call(functools.partial(tail_kernel, (group_len * dp_size) ** (-...  44.8 us
    all_to_all x3, starting transfers between devices, exchange(): return lax.all_to_all(array, both, split_axis=0, concat_axis=0, tiled=True)  24.3 us
    pallas_call x1, Pallas kernels, per_device(): call(functools.partial(expert_down_kernel, caps), (wide_shape, narrow_sha...  18.6 us
    dot_general x3, matrix products, weight_grad(): product = lax.dot_general(left, right, FIRST, preferred_element_type=F32)  17.8 us
    pallas_call x2, Pallas kernels, send(): call(kernel, jax.ShapeDtypeStruct((rows, CHUNKS, LANES), BF16), moved=600...  14.8 us
    pallas_call x1, Pallas kernels, per_device(): call(expert_up_kernel, (wide_shape, narrow_shape, narrow_shape, narrow_sh...  11.7 us
    unnamed x20, local copies, waits for them, and re-layouts  9.95 us
  transfers between devices with their start and end apart: 3, of which 3 were waited for; matrix products, arithmetic and copies ran while one was open for 6% of the time, Pallas kernels for 8%

profile of v3, /device:TPU:1, one launch (start us, length us, event | category | flops | bytes accessed | tf_op | source)
XLA Modules:
  0.0 304.9 jit_solution(15565302998557526695)
XLA Ops:
  0.6 1.9 copy.28
  2.6 1.9 shard_map.232
  4.5 6.6 %shard_map.234 = bf16[1280,16,128]{2,1,0:T(8,128)(2,1)} custom-call(s32[128,128]{1,0:T(8,128)} %get-tuple-element.33.table_ref, bf16[128,16,128]{2,1,0:T(8,128)(2,1)} %bitcast.28, bf16[16,128]{1,0:T(8,128)(2,1)} %bitcast.37), custom_call_target="tpu_custom_call" | custom-call | bytes 6000000 | tf_op jit(solution)/shard_map/pallas_call | solution.py:552
  11.2 0.0 copy-start
  11.2 11.9 %all-to-all-start.1 = ((bf16[128,160,128]{2,1,0:T(8,128)(2,1)}), bf16[128,160,128]{2,1,0:T(8,128)(2,1)}, u32[]{:S(2)}, u32[]{:S(2)}) async-start(bf16[128,160,128]{2,1,0:T(8,128)(2,1)} %bitcast.27), calls=%async_computation.1 | async-start | bytes 10485760 | tf_op jit(solution)/shard_map/all_to_all | solution.py:549
  23.1 0.0 copy-done
  23.1 0.9 copy.27
  24.0 8.1 %shard_map.233 = bf16[1280,16,128]{2,1,0:T(8,128)(2,1)} custom-call(s32[128,128]{1,0:T(8,128)} %get-tuple-element.33.table_ref, f32[128,128]{1,0:T(8,128)} %get-tuple-element.34.scale_ref, bf16[128,16,128]{2,1,0:T(8,128)(2,1)} %bitcast.30), custom_call_target="tpu_custom_call" | custom-call | bytes 6000000 | tf_op jit(solution)/shard_map/pallas_call | solution.py:552
  32.1 53.5 %all-to-all-done.1 = bf16[128,160,128]{2,1,0:T(8,128)(2,1)} async-done(((bf16[128,160,128]{2,1,0:T(8,128)(2,1)}), bf16[128,160,128]{2,1,0:T(8,128)(2,1)}, u32[]{:S(2)}, u32[]{:S(2)}) %all-to-all-start.1) | async-done | bytes 5242912 | tf_op jit(solution)/shard_map/all_to_all | solution.py:549
  85.6 0.0 copy-start.1
  85.6 6.2 %all-to-all-start = ((bf16[128,160,128]{2,1,0:T(8,128)(2,1)}), bf16[128,160,128]{2,1,0:T(8,128)(2,1)}, u32[]{:S(2)}, u32[]{:S(2)}) async-start(bf16[128,160,128]{2,1,0:T(8,128)(2,1)} %bitcast.26), calls=%async_computation | async-start | bytes 10485760 | tf_op jit(solution)/shard_map/all_to_all | solution.py:549
  91.8 0.0 copy-done.1
  91.8 1.0 copy.26.begin_ref
  92.8 4.9 %shard_map.235 = bf16[2,2,512,512]{3,2,1,0:T(8,128)(2,1)} custom-call(bf16[1024,256]{1,0:T(8,128)(2,1)} %query_hbm.1, bf16[1024,256]{1,0:T(8,128)(2,1)} %key_hbm.1, s32[1024,1]{1,0:T(8,128)} %copy.26.begin_ref), custom_call_target="tpu_custom_call" | custom-call | flops 10000000000 | bytes 5000000 | tf_op jit(solution)/shard_map/pallas_call | solution.py:575
  97.7 11.7 %shard_map.236 = (bf16[1280,2048]{1,0:T(8,128)(2,1)}, bf16[1280,512]{1,0:T(8,128)(2,1)}, bf16[1280,512]{1,0:T(8,128)(2,1)}, bf16[1280,512]{1,0:T(8,128)(2,1)}) custom-call(bf16[20480,128]{1,0:T(8,128)(2,1)} %bitcast.6.tile_ref, bf16[256,256]{1,0:T(8,128)(2,1)} %constant.3.clone.swap_ref, bf16[1,2048,512]{2,1,0:T(8,128)(2,1)} %gate_w_ref.3, ...), custom_call_target="tpu_custom_call" | custom-call | flops 5368709120 | bytes 18000000 | tf_op jit(solution)/shard_map/pallas_call | solution.py:595
  109.4 44.9 %all-to-all-done = bf16[128,160,128]{2,1,0:T(8,128)(2,1)} async-done(((bf16[128,160,128]{2,1,0:T(8,128)(2,1)}), bf16[128,160,128]{2,1,0:T(8,128)(2,1)}, u32[]{:S(2)}, u32[]{:S(2)}) %all-to-all-start) | async-done | bytes 5242912 | tf_op jit(solution)/shard_map/all_to_all | solution.py:549
  154.3 18.6 %shard_map.237 = (bf16[1280,2048]{1,0:T(8,128)(2,1)}, bf16[1280,512]{1,0:T(8,128)(2,1)}, bf16[1280,512]{1,0:T(8,128)(2,1)}, bf16[128,168,128]{2,1,0:T(8,128)(2,1)}) custom-call(bf16[20480,128]{1,0:T(8,128)(2,1)} %bitcast.3.tile_ref, bf16[256,256]{1,0:T(8,128)(2,1)} %constant.3.clone.swap_ref, bf16[32,320]{1,0:T(8,128)(2,1)} %constant.10.clone.gather_ref, ...), custom_call_target="tpu_custom_call" | custom-call | flops 8053063680 | bytes 25000000 | tf_op jit(solution)/shard_map/pallas_call | solution.py:608
  172.9 0.0 copy-start.2
  172.9 6.2 %all-to-all-start.2 = ((bf16[128,168,128]{2,1,0:T(8,128)(2,1)}), bf16[128,168,128]{2,1,0:T(8,128)(2,1)}, u32[]{:S(2)}, u32[]{:S(2)}) async-start(bf16[128,168,128]{2,1,0:T(8,128)(2,1)} %get-tuple-element.39), calls=%async_computation.2 | async-start | bytes 11010048 | tf_op jit(solution)/shard_map/all_to_all | solution.py:549
  179.1 0.0 copy-done.2
  179.1 0.0 copy-start.4
  179.1 0.0 slice-start
  179.1 6.7 %fusion.2 = bf16[1,512,2048]{2,1,0:T(8,128)(2,1)} fusion(bf16[1280,512]{1,0:T(8,128)(2,1)S(1)} %copy-done.2, bf16[1280,2048]{1,0:T(8,128)(2,1)} %get-tuple-element.43), kind=kOutput, calls=%fused_computation.5 | convolution fusion | flops 2686451712 | bytes 8650752 | tf_op jit(solution)/shard_map/dot_general | solution.py:643
  185.9 0.0 copy-done.4
  185.9 0.0 slice-start.1
  185.9 0.0 copy-start.3
  185.9 6.9 %fusion = bf16[1,2048,512]{2,1,0:T(8,128)(2,1)} fusion(bf16[1280,2048]{1,0:T(8,128)(2,1)} %get-tuple-element.40, bf16[1280,512]{1,0:T(8,128)(2,1)S(1)} %copy-done.4), kind=kOutput, calls=%fused_computation.3 | convolution fusion | flops 2686451712 | bytes 8650752 | tf_op jit(solution)/shard_map/dot_general | solution.py:643
  192.8 0.0 slice-done
  192.8 0.0 slice-done.1
  192.8 0.0 copy-done.3
  192.8 4.1 %fusion.1 = bf16[1,2048,512]{2,1,0:T(8,128)(2,1)} fusion(bf16[1280,2048]{1,0:T(8,128)(2,1)S(1)} %bitcast.45, bf16[1280,512]{1,0:T(8,128)(2,1)S(1)} %copy-done.3), kind=kOutput, calls=%fused_computation.4 | convolution fusion | flops 2686451712 | bytes 8650752 | tf_op jit(solution)/shard_map/dot_general | solution.py:643
  196.9 47.5 %all-to-all-done.2.back_ref = bf16[128,168,128]{2,1,0:T(8,128)(2,1)} async-done(((bf16[128,168,128]{2,1,0:T(8,128)(2,1)}), bf16[128,168,128]{2,1,0:T(8,128)(2,1)}, u32[]{:S(2)}, u32[]{:S(2)}) %all-to-all-start.2) | async-done | bytes 5505056 | tf_op jit(solution)/shard_map/all_to_all | solution.py:549
  244.4 8.6 %shard_map.238 = (bf16[128,2048]{1,0:T(8,128)(2,1)}, bf16[8,128]{1,0:T(8,128)(2,1)}) custom-call(s32[8,128]{1,0:T(8,128)} %bitcast.35, s32[8,128]{1,0:T(8,128)} %get-tuple-element.32.slot_ref.slot_lanes, bf16[128,168,128]{2,1,0:T(8,128)(2,1)} %all-to-all-done.2.back_ref, bf16[128,16,128]{2,1,0:T(8,128)(2,1)} %bitcast.29, bf16[128,16,128]{2,1,0:T(8,128)(2,1)} %bitcast.31, ...), custom_call_target="tpu_custom_call" | custom-call | bytes 8000000 | tf_op jit(solution)/shard_map/pallas_call | solution.py:653
  253.0 44.8 %shard_map.239 = (bf16[1024,256]{1,0:T(8,128)(2,1)}, bf16[1024,256]{1,0:T(8,128)(2,1)}, bf16[1024,256]{1,0:T(8,128)(2,1)}, bf16[128,256]{1,0:T(8,128)(2,1)}) custom-call(bf16[128,2048]{1,0:T(8,128)(2,1)} %get-tuple-element.68.resid_hbm, bf16[2048,256]{1,0:T(8,128)(2,1)} %weight_hbm.1, bf16[1024,256]{1,0:T(8,128)(2,1)} %attn_hbm.1, ...), custom_call_target="tpu_custom_call" | custom-call | flops 4000000000 | bytes 20000000 | tf_op jit(solution)/shard_map/pallas_call | solution.py:687
  297.8 1.5 copy.33
  299.3 1.9 copy.34
  301.2 1.9 copy.35
  303.0 1.9 copy.36
  (1 shorter events, 0.0 us)
Async XLA Ops:
  11.2 11.9 %copy-start = (bf16[128,2048]{1,0:T(8,128)(2,1)S(1)}, bf16[128,2048]{1,0:T(8,128)(2,1)}, u32[]{:S(2)}) copy-start(bf16[128,2048]{1,0:T(8,128)(2,1)} %param.18) | copy-start | bytes 1572868
  11.2 74.4 %all-to-all-start.1 = ((bf16[128,160,128]{2,1,0:T(8,128)(2,1)}), bf16[128,160,128]{2,1,0:T(8,128)(2,1)}, u32[]{:S(2)}, u32[]{:S(2)}) async-start(bf16[128,160,128]{2,1,0:T(8,128)(2,1)} %bitcast.27), calls=%async_computation.1 | async-start | bytes 10485760 | tf_op jit(solution)/shard_map/all_to_all | solution.py:549
  85.6 6.2 %copy-start.1 = (s32[1024]{0:T(1024)S(1)}, s32[1024]{0:T(1024)}, u32[]{:S(2)}) copy-start(s32[1024]{0:T(1024)} %param.30) | copy-start | bytes 12292
  85.6 68.7 %all-to-all-start = ((bf16[128,160,128]{2,1,0:T(8,128)(2,1)}), bf16[128,160,128]{2,1,0:T(8,128)(2,1)}, u32[]{:S(2)}, u32[]{:S(2)}) async-start(bf16[128,160,128]{2,1,0:T(8,128)(2,1)} %bitcast.26), calls=%async_computation | async-start | bytes 10485760 | tf_op jit(solution)/shard_map/all_to_all | solution.py:549
  172.9 6.2 %copy-start.2 = (bf16[1280,512]{1,0:T(8,128)(2,1)S(1)}, bf16[1280,512]{1,0:T(8,128)(2,1)}, u32[]{:S(2)}) copy-start(bf16[1280,512]{1,0:T(8,128)(2,1)} %get-tuple-element.36.act_ref) | copy-start | bytes 3932164
  172.9 71.5 %all-to-all-start.2 = ((bf16[128,168,128]{2,1,0:T(8,128)(2,1)}), bf16[128,168,128]{2,1,0:T(8,128)(2,1)}, u32[]{:S(2)}, u32[]{:S(2)}) async-start(bf16[128,168,128]{2,1,0:T(8,128)(2,1)} %get-tuple-element.39), calls=%async_computation.2 | async-start | bytes 11010048 | tf_op jit(solution)/shard_map/all_to_all | solution.py:549
  179.1 6.8 %copy-start.4 = (bf16[1280,512]{1,0:T(8,128)(2,1)S(1)}, bf16[1280,512]{1,0:T(8,128)(2,1)}, u32[]{:S(2)}) copy-start(bf16[1280,512]{1,0:T(8,128)(2,1)} %get-tuple-element.41) | copy-start | bytes 3932164
  179.1 13.7 %slice-start = ((s8[5242880]{0:T(1024)(128)(4,1)}), s8[4194304]{0:T(1024)(128)(4,1)S(1)}, s32[]{:S(2)}) async-start(s8[5242880]{0:T(1024)(128)(4,1)} %bitcast.44), calls=%async_computation.3 | async-start | bytes 8388608
  185.9 6.9 %slice-start.1 = ((s8[5242880]{0:T(1024)(128)(4,1)}), s8[1048576]{0:T(1024)(128)(4,1)S(1)}, s32[]{:S(2)}) async-start(s8[5242880]{0:T(1024)(128)(4,1)} %bitcast.44), calls=%async_computation.4 | async-start | bytes 2097152
  185.9 6.9 %copy-start.3 = (bf16[1280,512]{1,0:T(8,128)(2,1)S(1)}, bf16[1280,512]{1,0:T(8,128)(2,1)}, u32[]{:S(2)}) copy-start(bf16[1280,512]{1,0:T(8,128)(2,1)} %get-tuple-element.42) | copy-start | bytes 3932164

commit v4 on v3

--- a/solution.py
+++ b/solution.py
@@ -54,6 +54,21 @@
             rows = turned[chunk * 16 : (chunk + 1) * 16]
             out_ref[group * 32 : group * 32 + 16, cols] = rows[:, :LANES]
             out_ref[group * 32 + 16 : group * 32 + 32, cols] = rows[:, LANES:]
+
+
+def turn_rows(rows, swap):
+    halves = [
+        jnp.concatenate(
+            [
+                rows[side * 16 : side * 16 + 16, chunk * LANES : (chunk + 1) * LANES]
+                for chunk in range(CHUNKS)
+            ],
+            axis=0,
+        )
+        for side in range(2)
+    ]
+    pair = jnp.concatenate(halves, axis=1)
+    return jnp.dot(swap, pair, preferred_element_type=F32).astype(BF16)
 
 
 def slots_kernel(caps, ids_ref, weight_ref, table_ref, scale_ref, slot_ref):
@@ -80,8 +95,8 @@
         scale = jnp.sum(jnp.where(mask, weights, 0.0), axis=1, keepdims=True)
         table = jnp.where(lane == place, token, table)
         scales = jnp.where(lane == place, scale, scales)
-    table_ref[...] = table.astype(jnp.int32)
-    scale_ref[...] = scales
+    table_ref[...] = table.T[:16].astype(jnp.int32)
+    scale_ref[...] = scales.T[:16]
     slot_ref[...] = jnp.concatenate(
         [
             jnp.sum(jnp.where(ids[k : k + 1] == row, counts, 0.0), axis=0, keepdims=True)
@@ -91,25 +106,30 @@
     ).astype(jnp.int32)
 
 
-def pack_rows_kernel(table_ref, hidden_ref, gain_ref, out_ref, normed):
-    tokens = hidden_ref.shape[0]
+def pack_rows_kernel(table_ref, hidden_ref, gain_ref, swap_ref, out_ref, normed):
+    tokens, width = hidden_ref.shape
     step = pl.program_id(0)
     caps = out_ref.shape[0] // DESTS
 
     @pl.when(step == 0)
     def _():
-        gain = gain_ref[...].astype(F32)[None]
-        for start in range(0, tokens, 16):
-            hidden = hidden_ref[start : start + 16].astype(F32)
-            mean = jnp.sum(
-                jnp.sum(hidden * hidden, axis=2, keepdims=True), axis=1, keepdims=True
-            ) * (1.0 / (CHUNKS * LANES))
-            normed[start : start + 16] = (hidden * lax.rsqrt(mean + EPS) * gain).astype(BF16)
+        gain = gain_ref[...].astype(F32)
+        swap = swap_ref[...]
+        for start in range(0, tokens, 32):
+            hidden = hidden_ref[start : start + 32].astype(F32)
+            mean = jnp.sum(hidden * hidden, axis=1, keepdims=True) * (1.0 / width)
+            low = (hidden * lax.rsqrt(mean + EPS) * gain).astype(BF16)
+            turned = turn_rows(low, swap)
+            for side in range(2):
+                for inner in range(16):
+                    normed[start + side * 16 + inner] = turned[
+                        inner * 16 : (inner + 1) * 16, side * LANES : (side + 1) * LANES
+                    ]
         normed[tokens] = jnp.zeros((CHUNKS, LANES), BF16)
 
     def fill(dest, carry):
         for place in range(caps):
-            out_ref[dest * caps + place] = normed[table_ref[step * DESTS + dest, place]]
+            out_ref[dest * caps + place] = normed[table_ref[place, step * DESTS + dest]]
         return carry
 
     lax.fori_loop(0, DESTS, fill, 0, unroll=2)
@@ -123,8 +143,8 @@
     def fill(dest, carry):
         for place in range(caps):
             at = step * DESTS + dest
-            token = jnp.minimum(table_ref[at, place], tokens - 1)
-            scale = scale_ref[at, place]
+            token = jnp.minimum(table_ref[place, at], tokens - 1)
+            scale = scale_ref[place, at]
             out_ref[dest * caps + place] = (grad_ref[token].astype(F32) * scale).astype(BF16)
         return carry
 
@@ -393,8 +413,6 @@
     def matmuls(pair, last):
         at = pl.multiple_of(pair * 2 * tokens, 2 * tokens)
         mine = pl.ds(at, 2 * tokens)
-        grads[mine] = jnp.dot(group[mine], weight[...], preferred_element_type=F32).astype(BF16)
-
         def add(step, carry):
             dest = (dp + 1 + step) % dp_size
             columns = pl.ds(pl.multiple_of(dest * tokens, tokens), tokens)
@@ -416,6 +434,7 @@
                 add(step, 0)
                 if step < dp_size - 1:
                     send_piece(step).start()
+        grads[mine] = jnp.dot(group[mine], weight[...], preferred_element_type=F32).astype(BF16)
 
     def send_piece(step):
         dest = (dp + 1 + step) % dp_size
@@ -503,6 +522,27 @@
         send_piece(step).wait_send()
 
 
+def publish_kernel(*refs):
+    count = len(refs) // 2
+    for i in range(count):
+        refs[count + i][...] = refs[i][...]
+
+
+def publish(arrays):
+    steps = 2
+    blocks = [
+        pl.BlockSpec((a.shape[0] // steps, a.shape[1]), lambda i: (i, 0)) for a in arrays
+    ]
+    return call(
+        publish_kernel,
+        tuple(jax.ShapeDtypeStruct(a.shape, a.dtype) for a in arrays),
+        moved=4000000,
+        grid=(steps,),
+        in_specs=blocks,
+        out_specs=tuple(blocks),
+    )(*arrays)
+
+
 def per_device(
     hidden_state,
     out_grad,
@@ -536,8 +576,8 @@
     table, scales, slots = call(
         functools.partial(slots_kernel, caps),
         (
-            jax.ShapeDtypeStruct((experts, LANES), jnp.int32),
-            jax.ShapeDtypeStruct((experts, LANES), F32),
+            jax.ShapeDtypeStruct((16, experts), jnp.int32),
+            jax.ShapeDtypeStruct((16, experts), F32),
             jax.ShapeDtypeStruct((top_k, tokens), jnp.int32),
         ),
         moved=300000,
@@ -564,7 +604,9 @@
         return exchange(packed.reshape(experts, caps * 16, LANES)).reshape(rows * 16, LANES)
 
     table_scratch = [pltpu.VMEM((tokens + 1, CHUNKS, LANES), BF16)]
-    got_rows = send(pack_rows_kernel, [table], [hidden3, gain2], table_scratch)
+    got_rows = send(
+        pack_rows_kernel, [table], [hidden_state, norm_gain.reshape(1, width), swap], table_scratch
+    )
     got_grads = send(pack_grads_kernel, [table, scales], [grad3], [])
 
     group_len, head_cols = queries.shape
@@ -582,7 +624,7 @@
         out_specs=probs_block,
     )(queries, keys, doc_start.reshape(group_len, 1))
 
-    got_rows, probs = lax.optimization_barrier((got_rows, probs))
+    got_rows, probs, hidden3 = lax.optimization_barrier((got_rows, probs, hidden3))
     step_rows = SOURCES * caps
     steps = rows // step_rows
     flat_tiles = pl.BlockSpec((step_rows * 16, LANES), lambda i: (i, 0))
@@ -684,7 +726,7 @@
     head_shape = jax.ShapeDtypeStruct((group_len, head_cols), BF16)
     head_vmem = pltpu.VMEM((group_len, head_cols), BF16)
     piece_shape = (dp_size, width // dp_size, head_cols)
-    query_grad, key_grad, value_grad, out_weight_grad = pl.pallas_call(
+    tail_results = pl.pallas_call(
         functools.partial(tail_kernel, (group_len * dp_size) ** (-0.5)),
         out_shape=(
             head_shape,
@@ -729,6 +771,7 @@
         keys,
         values,
     )
+    query_grad, key_grad, value_grad, out_weight_grad = publish(tail_results)
     return (
         gate_grad,
         grad_gate_w,

time: 306 us -> 299 us (0.977)
  local copies, waits for them, and re-layouts: 11 us -> 4.15 us
    unnamed x20 -> x18, local copies, waits for them, and re-layouts: 9.95 us -> 1.83 us
  transfers between devices with their start and end apart: 3 -> 3, of which waited for: 3 -> 3; matrix products, arithmetic and copies ran while one was open for 6% -> 7% of each run, Pallas kernels for 8% -> 8%
where the time goes in v4:
time: 299 us
  waiting for transfers between devices  146 us (49%)
  Pallas kernels  105 us (35%)
  starting transfers between devices  24.3 us (8%)
  matrix products  17.8 us (6%)
  local copies, waits for them, and re-layouts  4.15 us (1%)
    all_to_all x3, waiting for transfers between devices, exchange(): return lax.all_to_all(array, both, split_axis=0, concat_axis=0, tiled=True)  146 us
    pallas_call x1, Pallas kernels, per_device(): pl.pallas_call(functools.partial(tail_kernel, (group_len * dp_size) ** (-...  44.3 us
    all_to_all x3, starting transfers between devices, exchange(): return lax.all_to_all(array, both, split_axis=0, concat_axis=0, tiled=True)  24.3 us
    pallas_call x1, Pallas kernels, per_device(): call(functools.partial(expert_down_kernel, caps), (wide_shape, narrow_sha...  18.6 us
    dot_general x3, matrix products, weight_grad(): product = lax.dot_general(left, right, FIRST, preferred_element_type=F32)  17.8 us
    pallas_call x2, Pallas kernels, send(): call(kernel, jax.ShapeDtypeStruct((rows, CHUNKS, LANES), BF16), moved=600...  12.6 us
    pallas_call x1, Pallas kernels, per_device(): call(expert_up_kernel, (wide_shape, narrow_shape, narrow_shape, narrow_sh...  11.7 us
    pallas_call x1, Pallas kernels, per_device(): call(combine_kernel, (jax.ShapeDtypeStruct((tokens, width), BF16), jax.Sh...  8.58 us
  transfers between devices with their start and end apart: 3, of which 3 were waited for; matrix products, arithmetic and copies ran while one was open for 7% of the time, Pallas kernels for 8%

profile of v4, /device:TPU:1, one launch (start us, length us, event | category | flops | bytes accessed | tf_op | source)
XLA Modules:
  0.0 298.5 jit_solution(7950675191247394106)
XLA Ops:
  0.6 1.3 reshape.51.gain_ref
  1.9 1.9 shard_map.232
  3.9 6.0 %shard_map.234 = bf16[1280,16,128]{2,1,0:T(8,128)(2,1)} custom-call(s32[16,128]{1,0:T(8,128)} %get-tuple-element.38.table_ref, bf16[128,2048]{1,0:T(8,128)(2,1)} %hidden_ref.1, bf16[1,2048]{1,0:T(2,128)(2,1)} %reshape.51.gain_ref, bf16[256,256]{1,0:T(8,128)(2,1)} %constant.3.clone.swap_ref), custom_call_target="tpu_custom_call" | custom-call | bytes 6000000 | tf_op jit(solution)/shard_map/pallas_call | solution.py:592
  9.9 0.0 copy-start.1
  9.9 11.9 %all-to-all-start.1 = ((bf16[128,160,128]{2,1,0:T(8,128)(2,1)}), bf16[128,160,128]{2,1,0:T(8,128)(2,1)}, u32[]{:S(2)}, u32[]{:S(2)}) async-start(bf16[128,160,128]{2,1,0:T(8,128)(2,1)} %bitcast.27), calls=%async_computation.1 | async-start | bytes 10485760 | tf_op jit(solution)/shard_map/all_to_all | solution.py:589
  21.8 0.0 copy-done.1
  21.8 0.9 copy.27
  22.7 6.6 %shard_map.233 = bf16[1280,16,128]{2,1,0:T(8,128)(2,1)} custom-call(s32[16,128]{1,0:T(8,128)} %get-tuple-element.38.table_ref, f32[16,128]{1,0:T(8,128)} %get-tuple-element.39.scale_ref, bf16[128,16,128]{2,1,0:T(8,128)(2,1)} %bitcast.28), custom_call_target="tpu_custom_call" | custom-call | bytes 6000000 | tf_op jit(solution)/shard_map/pallas_call | solution.py:592
  29.3 55.0 %all-to-all-done.1 = bf16[128,160,128]{2,1,0:T(8,128)(2,1)} async-done(((bf16[128,160,128]{2,1,0:T(8,128)(2,1)}), bf16[128,160,128]{2,1,0:T(8,128)(2,1)}, u32[]{:S(2)}, u32[]{:S(2)}) %all-to-all-start.1) | async-done | bytes 5242912 | tf_op jit(solution)/shard_map/all_to_all | solution.py:589
  84.3 0.0 copy-start.2
  84.3 0.0 copy-start
  84.3 6.2 %all-to-all-start = ((bf16[128,160,128]{2,1,0:T(8,128)(2,1)}), bf16[128,160,128]{2,1,0:T(8,128)(2,1)}, u32[]{:S(2)}, u32[]{:S(2)}) async-start(bf16[128,160,128]{2,1,0:T(8,128)(2,1)} %bitcast.26), calls=%async_computation | async-start | bytes 10485760 | tf_op jit(solution)/shard_map/all_to_all | solution.py:589
  90.5 0.0 copy-done.2
  90.5 1.0 copy.26.begin_ref
  91.6 0.0 copy-done
  91.6 0.9 copy.28
  92.5 4.9 %shard_map.235 = bf16[2,2,512,512]{3,2,1,0:T(8,128)(2,1)} custom-call(bf16[1024,256]{1,0:T(8,128)(2,1)} %query_hbm.1, bf16[1024,256]{1,0:T(8,128)(2,1)} %key_hbm.1, s32[1024,1]{1,0:T(8,128)} %copy.26.begin_ref), custom_call_target="tpu_custom_call" | custom-call | flops 10000000000 | bytes 5000000 | tf_op jit(solution)/shard_map/pallas_call | solution.py:617
  97.4 11.7 %shard_map.236 = (bf16[1280,2048]{1,0:T(8,128)(2,1)}, bf16[1280,512]{1,0:T(8,128)(2,1)}, bf16[1280,512]{1,0:T(8,128)(2,1)}, bf16[1280,512]{1,0:T(8,128)(2,1)}) custom-call(bf16[20480,128]{1,0:T(8,128)(2,1)} %bitcast.5.tile_ref, bf16[256,256]{1,0:T(8,128)(2,1)} %constant.3.clone.swap_ref, bf16[1,2048,512]{2,1,0:T(8,128)(2,1)} %gate_w_ref.3, ...), custom_call_target="tpu_custom_call" | custom-call | flops 5368709120 | bytes 18000000 | tf_op jit(solution)/shard_map/pallas_call | solution.py:637
  109.1 43.9 %all-to-all-done = bf16[128,160,128]{2,1,0:T(8,128)(2,1)} async-done(((bf16[128,160,128]{2,1,0:T(8,128)(2,1)}), bf16[128,160,128]{2,1,0:T(8,128)(2,1)}, u32[]{:S(2)}, u32[]{:S(2)}) %all-to-all-start) | async-done | bytes 5242912 | tf_op jit(solution)/shard_map/all_to_all | solution.py:589
  153.1 18.6 %shard_map.237 = (bf16[1280,2048]{1,0:T(8,128)(2,1)}, bf16[1280,512]{1,0:T(8,128)(2,1)}, bf16[1280,512]{1,0:T(8,128)(2,1)}, bf16[128,168,128]{2,1,0:T(8,128)(2,1)}) custom-call(bf16[20480,128]{1,0:T(8,128)(2,1)} %bitcast.3.tile_ref, bf16[256,256]{1,0:T(8,128)(2,1)} %constant.3.clone.swap_ref, bf16[32,320]{1,0:T(8,128)(2,1)} %constant.10.clone.gather_ref, ...), custom_call_target="tpu_custom_call" | custom-call | flops 8053063680 | bytes 25000000 | tf_op jit(solution)/shard_map/pallas_call | solution.py:650
  171.6 0.0 copy-start.3
  171.6 6.2 %all-to-all-start.2 = ((bf16[128,168,128]{2,1,0:T(8,128)(2,1)}), bf16[128,168,128]{2,1,0:T(8,128)(2,1)}, u32[]{:S(2)}, u32[]{:S(2)}) async-start(bf16[128,168,128]{2,1,0:T(8,128)(2,1)} %get-tuple-element.44), calls=%async_computation.2 | async-start | bytes 11010048 | tf_op jit(solution)/shard_map/all_to_all | solution.py:589
  177.8 0.0 copy-done.3
  177.8 0.0 copy-start.5
  177.9 0.0 slice-start
  177.9 6.7 %fusion.2 = bf16[1,512,2048]{2,1,0:T(8,128)(2,1)} fusion(bf16[1280,512]{1,0:T(8,128)(2,1)S(1)} %copy-done.3, bf16[1280,2048]{1,0:T(8,128)(2,1)} %get-tuple-element.48), kind=kOutput, calls=%fused_computation.5 | convolution fusion | flops 2686451712 | bytes 8650752 | tf_op jit(solution)/shard_map/dot_general | solution.py:685
  184.6 0.0 copy-done.5
  184.6 0.0 slice-start.1
  184.6 0.0 copy-start.4
  184.6 6.9 %fusion = bf16[1,2048,512]{2,1,0:T(8,128)(2,1)} fusion(bf16[1280,2048]{1,0:T(8,128)(2,1)} %get-tuple-element.45, bf16[1280,512]{1,0:T(8,128)(2,1)S(1)} %copy-done.5), kind=kOutput, calls=%fused_computation.3 | convolution fusion | flops 2686451712 | bytes 8650752 | tf_op jit(solution)/shard_map/dot_general | solution.py:685
  191.5 0.0 slice-done
  191.5 0.0 slice-done.1
  191.5 0.0 copy-done.4
  191.5 4.1 %fusion.1 = bf16[1,2048,512]{2,1,0:T(8,128)(2,1)} fusion(bf16[1280,2048]{1,0:T(8,128)(2,1)S(1)} %bitcast.43, bf16[1280,512]{1,0:T(8,128)(2,1)S(1)} %copy-done.4), kind=kOutput, calls=%fused_computation.4 | convolution fusion | flops 2686451712 | bytes 8650752 | tf_op jit(solution)/shard_map/dot_general | solution.py:685
  195.7 47.5 %all-to-all-done.2.back_ref = bf16[128,168,128]{2,1,0:T(8,128)(2,1)} async-done(((bf16[128,168,128]{2,1,0:T(8,128)(2,1)}), bf16[128,168,128]{2,1,0:T(8,128)(2,1)}, u32[]{:S(2)}, u32[]{:S(2)}) %all-to-all-start.2) | async-done | bytes 5505056 | tf_op jit(solution)/shard_map/all_to_all | solution.py:589
  243.2 8.6 %shard_map.238 = (bf16[128,2048]{1,0:T(8,128)(2,1)}, bf16[8,128]{1,0:T(8,128)(2,1)}) custom-call(s32[8,128]{1,0:T(8,128)} %bitcast.34, s32[8,128]{1,0:T(8,128)} %get-tuple-element.37.slot_ref.slot_lanes, bf16[128,168,128]{2,1,0:T(8,128)(2,1)} %all-to-all-done.2.back_ref, bf16[128,16,128]{2,1,0:T(8,128)(2,1)} %bitcast.31, bf16[128,16,128]{2,1,0:T(8,128)(2,1)} %bitcast.29, ...), custom_call_target="tpu_custom_call" | custom-call | bytes 8000000 | tf_op jit(solution)/shard_map/pallas_call | solution.py:695
  251.7 44.3 %shard_map.239 = (bf16[1024,256]{1,0:T(8,128)(2,1)}, bf16[1024,256]{1,0:T(8,128)(2,1)}, bf16[1024,256]{1,0:T(8,128)(2,1)}, bf16[128,256]{1,0:T(8,128)(2,1)}) custom-call(bf16[128,2048]{1,0:T(8,128)(2,1)} %get-tuple-element.32.resid_hbm, bf16[2048,256]{1,0:T(8,128)(2,1)} %weight_hbm.1, bf16[1024,256]{1,0:T(8,128)(2,1)} %attn_hbm.1, ...), custom_call_target="tpu_custom_call" | custom-call | flops 4000000000 | bytes 20000000 | tf_op jit(solution)/shard_map/pallas_call | solution.py:729
  296.1 2.3 shard_map.240
  (1 shorter events, 0.0 us)
Async XLA Ops:
  9.9 11.9 %copy-start.1 = (bf16[128,2048]{1,0:T(8,128)(2,1)S(1)}, bf16[128,2048]{1,0:T(8,128)(2,1)}, u32[]{:S(2)}) copy-start(bf16[128,2048]{1,0:T(8,128)(2,1)} %param.18) | copy-start | bytes 1572868
  9.9 74.4 %all-to-all-start.1 = ((bf16[128,160,128]{2,1,0:T(8,128)(2,1)}), bf16[128,160,128]{2,1,0:T(8,128)(2,1)}, u32[]{:S(2)}, u32[]{:S(2)}) async-start(bf16[128,160,128]{2,1,0:T(8,128)(2,1)} %bitcast.27), calls=%async_computation.1 | async-start | bytes 10485760 | tf_op jit(solution)/shard_map/all_to_all | solution.py:589
  84.3 6.2 %copy-start.2 = (s32[1024]{0:T(1024)S(1)}, s32[1024]{0:T(1024)}, u32[]{:S(2)}) copy-start(s32[1024]{0:T(1024)} %param.30) | copy-start | bytes 12292
  84.3 7.2 %copy-start = (bf16[128,2048]{1,0:T(8,128)(2,1)S(1)}, bf16[128,2048]{1,0:T(8,128)(2,1)}, u32[]{:S(2)}) copy-start(bf16[128,2048]{1,0:T(8,128)(2,1)} %hidden_ref.1) | copy-start | bytes 1572868
  84.3 68.7 %all-to-all-start = ((bf16[128,160,128]{2,1,0:T(8,128)(2,1)}), bf16[128,160,128]{2,1,0:T(8,128)(2,1)}, u32[]{:S(2)}, u32[]{:S(2)}) async-start(bf16[128,160,128]{2,1,0:T(8,128)(2,1)} %bitcast.26), calls=%async_computation | async-start | bytes 10485760 | tf_op jit(solution)/shard_map/all_to_all | solution.py:589
  171.6 6.2 %copy-start.3 = (bf16[1280,512]{1,0:T(8,128)(2,1)S(1)}, bf16[1280,512]{1,0:T(8,128)(2,1)}, u32[]{:S(2)}) copy-start(bf16[1280,512]{1,0:T(8,128)(2,1)} %get-tuple-element.41.act_ref) | copy-start | bytes 3932164
  171.6 71.5 %all-to-all-start.2 = ((bf16[128,168,128]{2,1,0:T(8,128)(2,1)}), bf16[128,168,128]{2,1,0:T(8,128)(2,1)}, u32[]{:S(2)}, u32[]{:S(2)}) async-start(bf16[128,168,128]{2,1,0:T(8,128)(2,1)} %get-tuple-element.44), calls=%async_computation.2 | async-start | bytes 11010048 | tf_op jit(solution)/shard_map/all_to_all | solution.py:589
  177.8 6.8 %copy-start.5 = (bf16[1280,512]{1,0:T(8,128)(2,1)S(1)}, bf16[1280,512]{1,0:T(8,128)(2,1)}, u32[]{:S(2)}) copy-start(bf16[1280,512]{1,0:T(8,128)(2,1)} %get-tuple-element.46) | copy-start | bytes 3932164
  177.9 13.7 %slice-start = ((s8[5242880]{0:T(1024)(128)(4,1)}), s8[4194304]{0:T(1024)(128)(4,1)S(1)}, s32[]{:S(2)}) async-start(s8[5242880]{0:T(1024)(128)(4,1)} %bitcast.42), calls=%async_computation.3 | async-start | bytes 8388608
  184.6 6.9 %slice-start.1 = ((s8[5242880]{0:T(1024)(128)(4,1)}), s8[1048576]{0:T(1024)(128)(4,1)S(1)}, s32[]{:S(2)}) async-start(s8[5242880]{0:T(1024)(128)(4,1)} %bitcast.42), calls=%async_computation.4 | async-start | bytes 2097152
  184.6 6.9 %copy-start.4 = (bf16[1280,512]{1,0:T(8,128)(2,1)S(1)}, bf16[1280,512]{1,0:T(8,128)(2,1)}, u32[]{:S(2)}) copy-start(bf16[1280,512]{1,0:T(8,128)(2,1)} %get-tuple-element.47) | copy-start | bytes 3932164

commit v5 on v4

--- a/solution.py
+++ b/solution.py
@@ -114,6 +114,7 @@
     @pl.when(step == 0)
     def _():
         gain = gain_ref[...].astype(F32)
+        gain = jnp.concatenate([gain[chunk : chunk + 1] for chunk in range(CHUNKS)], axis=1)
         swap = swap_ref[...]
         for start in range(0, tokens, 32):
             hidden = hidden_ref[start : start + 32].astype(F32)
@@ -238,11 +239,8 @@
     grad_ref,
     gain_ref,
     swap_ref,
-    id_lanes,
-    slot_lanes,
-    weight_ref,
     out_ref,
-    gate_ref,
+    score_ref,
     total,
     tiles,
 ):
@@ -278,8 +276,7 @@
         lambda i: tiles[i * 256 : (i + 1) * 256], swap_ref[...], out_ref, tokens // 32
     )
     extra = back_ref[:, back_ref.shape[1] - PACK_EXTRA :, :].astype(F32)
-    score = (jnp.sum(extra, axis=1) * (1.0 / PACK_EXTRA)).astype(BF16)
-    write_gate(id_lanes[...], slot_lanes[...], weight_ref[...], score, gate_ref)
+    score_ref[...] = (jnp.sum(extra, axis=1) * (1.0 / PACK_EXTRA)).astype(BF16)
 
 
 def write_gate(ids, slot, weight, score, out_ref):
@@ -319,10 +316,15 @@
     query_hbm,
     key_hbm,
     value_hbm,
+    id_ref,
+    slot_ref,
+    pair_ref,
+    score_ref,
     dq_ref,
     dk_ref,
     dv_ref,
     out_ref,
+    gate_ref,
     group,
     weight,
     attn,
@@ -377,16 +379,18 @@
     ]
     for load in loads:
         load.start()
-    loads[0].wait()
     pl.semaphore_wait(barrier, dp_size - 1 + 3)
 
     def part(owner, second):
         at = pl.multiple_of(owner * tokens + second * half, half)
         return group.at[pl.ds(at, half)]
 
-    def ring(number, owner, second, target):
+    def mine_at(second):
+        return resid_hbm.at[pl.ds(second * half, half)]
+
+    def ring(number, owner, second, target, source=None):
         return pltpu.make_async_remote_copy(
-            src_ref=part(owner, second),
+            src_ref=part(owner, second) if source is None else source,
             dst_ref=part(owner, second),
             send_sem=ring_send.at[number],
             recv_sem=ring_recv.at[number],
@@ -394,9 +398,9 @@
             device_id_type=MESH,
         )
 
-    def side(number, owner, second):
+    def side(number, owner, second, source=None):
         return pltpu.make_async_remote_copy(
-            src_ref=part(owner, second),
+            src_ref=part(owner, second) if source is None else source,
             dst_ref=part(owner, second),
             send_sem=side_send.at[number],
             recv_sem=side_recv.at[number],
@@ -404,9 +408,10 @@
             device_id_type=MESH,
         )
 
-    up = [ring(0, ep, 0, above), ring(1, ep, 1, above)]
-    down = [ring(3, ep, 0, below), ring(2, ep, 1, below)]
-    own = [side(0, ep, 0), side(1, ep, 1)]
+    first, second = mine_at(0), mine_at(1)
+    up = [ring(0, ep, 0, above, first), ring(1, ep, 1, above, second)]
+    down = [ring(3, ep, 0, below, first), ring(2, ep, 1, below, second)]
+    own = [side(0, ep, 0, first), side(1, ep, 1, second)]
     for copy in (up[0], down[1], own[0], own[1], up[1], down[0]):
         copy.start()
 
@@ -447,6 +452,8 @@
             device_id_type=MESH,
         )
 
+    write_gate(id_ref[...], slot_ref[...], pair_ref[...], score_ref[...], gate_ref)
+    loads[0].wait()
     own[0].wait_recv()
     own[1].wait_recv()
     loads[1].wait()
@@ -531,7 +538,10 @@
 def publish(arrays):
     steps = 2
     blocks = [
-        pl.BlockSpec((a.shape[0] // steps, a.shape[1]), lambda i: (i, 0)) for a in arrays
+        pl.BlockSpec((a.shape[0] // steps, a.shape[1]), lambda i: (i, 0))
+        if a.shape[0] % (16 * steps) == 0
+        else whole(a.shape)
+        for a in arrays
     ]
     return call(
         publish_kernel,
@@ -605,7 +615,7 @@
 
     table_scratch = [pltpu.VMEM((tokens + 1, CHUNKS, LANES), BF16)]
     got_rows = send(
-        pack_rows_kernel, [table], [hidden_state, norm_gain.reshape(1, width), swap], table_scratch
+        pack_rows_kernel, [table], [hidden_state, gain2, swap], table_scratch
     )
     got_grads = send(pack_grads_kernel, [table, scales], [grad3], [])
 
@@ -692,11 +702,11 @@
     back, grad_gate_w, grad_up_w, grad_down_w = lax.optimization_barrier(
         (back, grad_gate_w, grad_up_w, grad_down_w)
     )
-    residual_grad, gate_grad = call(
+    residual_grad, scores = call(
         combine_kernel,
         (
             jax.ShapeDtypeStruct((tokens, width), BF16),
-            jax.ShapeDtypeStruct((top_k, tokens), BF16),
+            jax.ShapeDtypeStruct((experts, LANES), BF16),
         ),
         moved=8000000,
         grid_spec=pltpu.PrefetchScalarGridSpec(
@@ -708,19 +718,14 @@
                 whole((tokens, CHUNKS, LANES)),
                 whole((CHUNKS, LANES)),
                 whole((256, 256)),
-                whole((top_k, tokens)),
-                whole((top_k, tokens)),
-                whole((top_k, tokens)),
             ],
-            out_specs=(whole((tokens, width)), whole((top_k, tokens))),
+            out_specs=(whole((tokens, width)), whole((experts, LANES))),
             scratch_shapes=[
                 pltpu.VMEM((tokens, CHUNKS, LANES), F32),
                 pltpu.VMEM((tokens * CHUNKS, LANES), BF16),
             ],
         ),
-    )(ids_t, slots, back, hidden3, grad3, gain2, swap, ids_t, slots, weight_t)
-    gate_grad = gate_grad.T
-
+    )(ids_t, slots, back, hidden3, grad3, gain2, swap)
     any_spec = pl.BlockSpec(memory_space=pl.ANY)
     vmem_spec = pl.BlockSpec(memory_space=pltpu.VMEM)
     head_shape = jax.ShapeDtypeStruct((group_len, head_cols), BF16)
@@ -733,9 +738,10 @@
             head_shape,
             head_shape,
             jax.ShapeDtypeStruct(piece_shape[1:], BF16),
+            jax.ShapeDtypeStruct((top_k, tokens), BF16),
         ),
-        in_specs=[any_spec] * 7,
-        out_specs=(vmem_spec,) * 4,
+        in_specs=[any_spec] * 7 + [vmem_spec] * 4,
+        out_specs=(vmem_spec,) * 5,
         scratch_shapes=[
             pltpu.VMEM((group_len, width), BF16),
             pltpu.VMEM((width, head_cols), BF16),
@@ -770,10 +776,14 @@
         queries,
         keys,
         values,
+        ids_t,
+        slots,
+        weight_t,
+        scores,
     )
-    query_grad, key_grad, value_grad, out_weight_grad = publish(tail_results)
+    query_grad, key_grad, value_grad, out_weight_grad, gate_grad = publish(tail_results)
     return (
-        gate_grad,
+        gate_grad.T,
         grad_gate_w,
         grad_up_w,
         grad_down_w,

time: 299 us -> 299 us (level)
  no operation moved by 1% of the time
where the time goes in v5:
time: 299 us; the launch traced here: 298 us
  waiting for transfers between devices  146 us (49%)
  Pallas kernels  106 us (35%)
  starting transfers between devices  24.3 us (8%)
  matrix products  17.8 us (6%)
    all_to_all x3, waiting for transfers between devices, exchange(): return lax.all_to_all(array, both, split_axis=0, concat_axis=0, tiled=True)  146 us
    pallas_call x1, Pallas kernels, per_device(): pl.pallas_call(functools.partial(tail_kernel, (group_len * dp_size) ** (-...  45.3 us
    all_to_all x3, starting transfers between devices, exchange(): return lax.all_to_all(array, both, split_axis=0, concat_axis=0, tiled=True)  24.3 us
    pallas_call x1, Pallas kernels, per_device(): call(functools.partial(expert_down_kernel, caps), (wide_shape, narrow_sha...  18.6 us
    dot_general x3, matrix products, weight_grad(): product = lax.dot_general(left, right, FIRST, preferred_element_type=F32)  17.8 us
    pallas_call x2, Pallas kernels, send(): call(kernel, jax.ShapeDtypeStruct((rows, CHUNKS, LANES), BF16), moved=600...  12.7 us
    pallas_call x1, Pallas kernels, per_device(): call(expert_up_kernel, (wide_shape, narrow_shape, narrow_shape, narrow_sh...  11.7 us
    pallas_call x1, Pallas kernels, per_device(): call(combine_kernel, (jax.ShapeDtypeStruct((tokens, width), BF16), jax.Sh...  8.52 us
  transfers between devices with their start and end apart: 3, of which 3 were waited for; matrix products, arithmetic and copies ran while one was open for 7% of the time, Pallas kernels for 8%

profile of v5, /device:TPU:1, one launch (start us, length us, event | category | flops | bytes accessed | tf_op | source)
XLA Modules:
  0.0 298.3 jit_solution(15530844073614543711)
XLA Ops:
  0.6 1.9 shard_map.232
  2.6 6.1 %shard_map.234 = bf16[1280,16,128]{2,1,0:T(8,128)(2,1)} custom-call(s32[16,128]{1,0:T(8,128)} %get-tuple-element.40.table_ref, bf16[128,2048]{1,0:T(8,128)(2,1)} %hidden_ref.1, bf16[16,128]{1,0:T(8,128)(2,1)} %bitcast.33, bf16[256,256]{1,0:T(8,128)(2,1)} %constant.3.clone.swap_ref), custom_call_target="tpu_custom_call" | custom-call | bytes 6000000 | tf_op jit(solution)/shard_map/pallas_call | solution.py:602
  8.7 0.0 copy-start.1
  8.7 11.9 %all-to-all-start.1 = ((bf16[128,160,128]{2,1,0:T(8,128)(2,1)}), bf16[128,160,128]{2,1,0:T(8,128)(2,1)}, u32[]{:S(2)}, u32[]{:S(2)}) async-start(bf16[128,160,128]{2,1,0:T(8,128)(2,1)} %bitcast.27), calls=%async_computation.1 | async-start | bytes 10485760 | tf_op jit(solution)/shard_map/all_to_all | solution.py:599
  20.6 0.0 copy-done.1
  20.6 0.9 copy.27
  21.5 6.6 %shard_map.233 = bf16[1280,16,128]{2,1,0:T(8,128)(2,1)} custom-call(s32[16,128]{1,0:T(8,128)} %get-tuple-element.40.table_ref, f32[16,128]{1,0:T(8,128)} %get-tuple-element.41.scale_ref, bf16[128,16,128]{2,1,0:T(8,128)(2,1)} %bitcast.28), custom_call_target="tpu_custom_call" | custom-call | bytes 6000000 | tf_op jit(solution)/shard_map/pallas_call | solution.py:602
  28.1 55.0 %all-to-all-done.1 = bf16[128,160,128]{2,1,0:T(8,128)(2,1)} async-done(((bf16[128,160,128]{2,1,0:T(8,128)(2,1)}), bf16[128,160,128]{2,1,0:T(8,128)(2,1)}, u32[]{:S(2)}, u32[]{:S(2)}) %all-to-all-start.1) | async-done | bytes 5242912 | tf_op jit(solution)/shard_map/all_to_all | solution.py:599
  83.1 0.0 copy-start.2
  83.1 0.0 copy-start
  83.1 6.2 %all-to-all-start = ((bf16[128,160,128]{2,1,0:T(8,128)(2,1)}), bf16[128,160,128]{2,1,0:T(8,128)(2,1)}, u32[]{:S(2)}, u32[]{:S(2)}) async-start(bf16[128,160,128]{2,1,0:T(8,128)(2,1)} %bitcast.26), calls=%async_computation | async-start | bytes 10485760 | tf_op jit(solution)/shard_map/all_to_all | solution.py:599
  89.3 0.0 copy-done.2
  89.3 1.0 copy.26.begin_ref
  90.3 0.0 copy-done
  90.3 0.9 copy.28
  91.2 4.9 %shard_map.235 = bf16[2,2,512,512]{3,2,1,0:T(8,128)(2,1)} custom-call(bf16[1024,256]{1,0:T(8,128)(2,1)} %query_hbm.1, bf16[1024,256]{1,0:T(8,128)(2,1)} %key_hbm.1, s32[1024,1]{1,0:T(8,128)} %copy.26.begin_ref), custom_call_target="tpu_custom_call" | custom-call | flops 10000000000 | bytes 5000000 | tf_op jit(solution)/shard_map/pallas_call | solution.py:627
  96.1 11.7 %shard_map.236 = (bf16[1280,2048]{1,0:T(8,128)(2,1)}, bf16[1280,512]{1,0:T(8,128)(2,1)}, bf16[1280,512]{1,0:T(8,128)(2,1)}, bf16[1280,512]{1,0:T(8,128)(2,1)}) custom-call(bf16[20480,128]{1,0:T(8,128)(2,1)} %bitcast.6.tile_ref, bf16[256,256]{1,0:T(8,128)(2,1)} %constant.3.clone.swap_ref, bf16[1,2048,512]{2,1,0:T(8,128)(2,1)} %gate_w_ref.3, ...), custom_call_target="tpu_custom_call" | custom-call | flops 5368709120 | bytes 18000000 | tf_op jit(solution)/shard_map/pallas_call | solution.py:647
  107.9 43.9 %all-to-all-done = bf16[128,160,128]{2,1,0:T(8,128)(2,1)} async-done(((bf16[128,160,128]{2,1,0:T(8,128)(2,1)}), bf16[128,160,128]{2,1,0:T(8,128)(2,1)}, u32[]{:S(2)}, u32[]{:S(2)}) %all-to-all-start) | async-done | bytes 5242912 | tf_op jit(solution)/shard_map/all_to_all | solution.py:599
  151.8 18.6 %shard_map.237 = (bf16[1280,2048]{1,0:T(8,128)(2,1)}, bf16[1280,512]{1,0:T(8,128)(2,1)}, bf16[1280,512]{1,0:T(8,128)(2,1)}, bf16[128,168,128]{2,1,0:T(8,128)(2,1)}) custom-call(bf16[20480,128]{1,0:T(8,128)(2,1)} %bitcast.3.tile_ref, bf16[256,256]{1,0:T(8,128)(2,1)} %constant.3.clone.swap_ref, bf16[32,320]{1,0:T(8,128)(2,1)} %constant.10.clone.gather_ref, ...), custom_call_target="tpu_custom_call" | custom-call | flops 8053063680 | bytes 25000000 | tf_op jit(solution)/shard_map/pallas_call | solution.py:660
  170.4 0.0 copy-start.3
  170.4 6.2 %all-to-all-start.2 = ((bf16[128,168,128]{2,1,0:T(8,128)(2,1)}), bf16[128,168,128]{2,1,0:T(8,128)(2,1)}, u32[]{:S(2)}, u32[]{:S(2)}) async-start(bf16[128,168,128]{2,1,0:T(8,128)(2,1)} %get-tuple-element.46), calls=%async_computation.2 | async-start | bytes 11010048 | tf_op jit(solution)/shard_map/all_to_all | solution.py:599
  176.6 0.0 copy-done.3
  176.6 0.0 copy-start.5
  176.6 0.0 slice-start
  176.7 6.7 %fusion.2 = bf16[1,512,2048]{2,1,0:T(8,128)(2,1)} fusion(bf16[1280,512]{1,0:T(8,128)(2,1)S(1)} %copy-done.3, bf16[1280,2048]{1,0:T(8,128)(2,1)} %get-tuple-element.50), kind=kOutput, calls=%fused_computation.5 | convolution fusion | flops 2686451712 | bytes 8650752 | tf_op jit(solution)/shard_map/dot_general | solution.py:695
  183.4 0.0 copy-done.5
  183.4 0.0 slice-start.1
  183.4 0.0 copy-start.4
  183.4 6.9 %fusion = bf16[1,2048,512]{2,1,0:T(8,128)(2,1)} fusion(bf16[1280,2048]{1,0:T(8,128)(2,1)} %get-tuple-element.47, bf16[1280,512]{1,0:T(8,128)(2,1)S(1)} %copy-done.5), kind=kOutput, calls=%fused_computation.3 | convolution fusion | flops 2686451712 | bytes 8650752 | tf_op jit(solution)/shard_map/dot_general | solution.py:695
  190.3 0.0 slice-done
  190.3 0.0 slice-done.1
  190.3 0.0 copy-done.4
  190.3 4.1 %fusion.1 = bf16[1,2048,512]{2,1,0:T(8,128)(2,1)} fusion(bf16[1280,2048]{1,0:T(8,128)(2,1)S(1)} %bitcast.44, bf16[1280,512]{1,0:T(8,128)(2,1)S(1)} %copy-done.4), kind=kOutput, calls=%fused_computation.4 | convolution fusion | flops 2686451712 | bytes 8650752 | tf_op jit(solution)/shard_map/dot_general | solution.py:695
  194.4 47.5 %all-to-all-done.2.back_ref = bf16[128,168,128]{2,1,0:T(8,128)(2,1)} async-done(((bf16[128,168,128]{2,1,0:T(8,128)(2,1)}), bf16[128,168,128]{2,1,0:T(8,128)(2,1)}, u32[]{:S(2)}, u32[]{:S(2)}) %all-to-all-start.2) | async-done | bytes 5505056 | tf_op jit(solution)/shard_map/all_to_all | solution.py:599
  241.9 8.5 %shard_map.238 = (bf16[128,2048]{1,0:T(8,128)(2,1)}, bf16[128,128]{1,0:T(8,128)(2,1)}) custom-call(s32[8,128]{1,0:T(8,128)} %bitcast.36, s32[8,128]{1,0:T(8,128)} %get-tuple-element.39.slot_ref, bf16[128,168,128]{2,1,0:T(8,128)(2,1)} %all-to-all-done.2.back_ref, bf16[128,16,128]{2,1,0:T(8,128)(2,1)} %bitcast.31, bf16[128,16,128]{2,1,0:T(8,128)(2,1)} %bitcast.29, ...), custom_call_target="tpu_custom_call" | custom-call | bytes 8000000 | tf_op jit(solution)/shard_map/pallas_call | solution.py:705
  250.5 45.3 %shard_map.239 = (bf16[1024,256]{1,0:T(8,128)(2,1)}, bf16[1024,256]{1,0:T(8,128)(2,1)}, bf16[1024,256]{1,0:T(8,128)(2,1)}, bf16[128,256]{1,0:T(8,128)(2,1)}, bf16[8,128]{1,0:T(8,128)(2,1)}) custom-call(bf16[128,2048]{1,0:T(8,128)(2,1)} %get-tuple-element.34.resid_hbm, bf16[2048,256]{1,0:T(8,128)(2,1)} %weight_hbm.1, bf16[1024,256]{1,0:T(8,128)(2,1)} %attn_hbm.1, ...), custom_call_target="tpu_custom_call" | custom-call | flops 4000000000 | bytes 20000000 | tf_op jit(solution)/shard_map/pallas_call | solution.py:734
  295.8 2.3 shard_map.240
  (1 shorter events, 0.0 us)
Async XLA Ops:
  8.7 11.9 %copy-start.1 = (bf16[128,2048]{1,0:T(8,128)(2,1)S(1)}, bf16[128,2048]{1,0:T(8,128)(2,1)}, u32[]{:S(2)}) copy-start(bf16[128,2048]{1,0:T(8,128)(2,1)} %param.18) | copy-start | bytes 1572868
  8.7 74.4 %all-to-all-start.1 = ((bf16[128,160,128]{2,1,0:T(8,128)(2,1)}), bf16[128,160,128]{2,1,0:T(8,128)(2,1)}, u32[]{:S(2)}, u32[]{:S(2)}) async-start(bf16[128,160,128]{2,1,0:T(8,128)(2,1)} %bitcast.27), calls=%async_computation.1 | async-start | bytes 10485760 | tf_op jit(solution)/shard_map/all_to_all | solution.py:599
  83.1 6.2 %copy-start.2 = (s32[1024]{0:T(1024)S(1)}, s32[1024]{0:T(1024)}, u32[]{:S(2)}) copy-start(s32[1024]{0:T(1024)} %param.30) | copy-start | bytes 12292
  83.1 7.2 %copy-start = (bf16[128,2048]{1,0:T(8,128)(2,1)S(1)}, bf16[128,2048]{1,0:T(8,128)(2,1)}, u32[]{:S(2)}) copy-start(bf16[128,2048]{1,0:T(8,128)(2,1)} %hidden_ref.1) | copy-start | bytes 1572868
  83.1 68.7 %all-to-all-start = ((bf16[128,160,128]{2,1,0:T(8,128)(2,1)}), bf16[128,160,128]{2,1,0:T(8,128)(2,1)}, u32[]{:S(2)}, u32[]{:S(2)}) async-start(bf16[128,160,128]{2,1,0:T(8,128)(2,1)} %bitcast.26), calls=%async_computation | async-start | bytes 10485760 | tf_op jit(solution)/shard_map/all_to_all | solution.py:599
  170.4 6.2 %copy-start.3 = (bf16[1280,512]{1,0:T(8,128)(2,1)S(1)}, bf16[1280,512]{1,0:T(8,128)(2,1)}, u32[]{:S(2)}) copy-start(bf16[1280,512]{1,0:T(8,128)(2,1)} %get-tuple-element.43.act_ref) | copy-start | bytes 3932164
  170.4 71.5 %all-to-all-start.2 = ((bf16[128,168,128]{2,1,0:T(8,128)(2,1)}), bf16[128,168,128]{2,1,0:T(8,128)(2,1)}, u32[]{:S(2)}, u32[]{:S(2)}) async-start(bf16[128,168,128]{2,1,0:T(8,128)(2,1)} %get-tuple-element.46), calls=%async_computation.2 | async-start | bytes 11010048 | tf_op jit(solution)/shard_map/all_to_all | solution.py:599
  176.6 6.8 %copy-start.5 = (bf16[1280,512]{1,0:T(8,128)(2,1)S(1)}, bf16[1280,512]{1,0:T(8,128)(2,1)}, u32[]{:S(2)}) copy-start(bf16[1280,512]{1,0:T(8,128)(2,1)} %get-tuple-element.48) | copy-start | bytes 3932164
  176.6 13.7 %slice-start = ((s8[5242880]{0:T(1024)(128)(4,1)}), s8[4194304]{0:T(1024)(128)(4,1)S(1)}, s32[]{:S(2)}) async-start(s8[5242880]{0:T(1024)(128)(4,1)} %bitcast.43), calls=%async_computation.3 | async-start | bytes 8388608
  183.4 6.9 %slice-start.1 = ((s8[5242880]{0:T(1024)(128)(4,1)}), s8[1048576]{0:T(1024)(128)(4,1)S(1)}, s32[]{:S(2)}) async-start(s8[5242880]{0:T(1024)(128)(4,1)} %bitcast.43), calls=%async_computation.4 | async-start | bytes 2097152
  183.4 6.9 %copy-start.4 = (bf16[1280,512]{1,0:T(8,128)(2,1)S(1)}, bf16[1280,512]{1,0:T(8,128)(2,1)}, u32[]{:S(2)}) copy-start(bf16[1280,512]{1,0:T(8,128)(2,1)} %get-tuple-element.49) | copy-start | bytes 3932164

commit v6 on v5

--- a/solution.py
+++ b/solution.py
@@ -234,7 +234,7 @@
 def combine_kernel(
     ids_ref,
     slot_ref,
-    back_ref,
+    back_hbm,
     hidden_ref,
     grad_ref,
     gain_ref,
@@ -243,8 +243,23 @@
     score_ref,
     total,
     tiles,
+    back_ref,
+    load_sems,
 ):
     top_k, tokens = ids_ref.shape
+
+    count = load_sems.shape[0]
+    each = back_ref.shape[0] // count
+    loads = [
+        pltpu.make_async_copy(
+            back_hbm.at[pl.ds(i * each, each)], back_ref.at[pl.ds(i * each, each)], load_sems.at[i]
+        )
+        for i in range(count)
+    ]
+    for load in loads:
+        load.start()
+    for load in loads:
+        load.wait()
 
     def gather(token, carry):
         acc = jnp.zeros((CHUNKS, LANES), F32)
@@ -713,7 +728,7 @@
             num_scalar_prefetch=2,
             grid=(1,),
             in_specs=[
-                whole(back.shape),
+                pl.BlockSpec(memory_space=pl.ANY),
                 whole((tokens, CHUNKS, LANES)),
                 whole((tokens, CHUNKS, LANES)),
                 whole((CHUNKS, LANES)),
@@ -723,6 +738,8 @@
             scratch_shapes=[
                 pltpu.VMEM((tokens, CHUNKS, LANES), F32),
                 pltpu.VMEM((tokens * CHUNKS, LANES), BF16),
+                pltpu.VMEM(back.shape, BF16),
+                pltpu.SemaphoreType.DMA((8,)),
             ],
         ),
     )(ids_t, slots, back, hidden3, grad3, gain2, swap)

time: 299 us -> 300 us (level)
  no operation moved by 1% of the time
where the time goes in v6:
time: 300 us; the launch traced here: 299 us
  waiting for transfers between devices  146 us (49%)
  Pallas kernels  107 us (36%)
  starting transfers between devices  24.3 us (8%)
  matrix products  17.8 us (6%)
    all_to_all x3, waiting for transfers between devices, exchange(): return lax.all_to_all(array, both, split_axis=0, concat_axis=0, tiled=True)  146 us
    pallas_call x1, Pallas kernels, per_device(): pl.pallas_call(functools.partial(tail_kernel, (group_len * dp_size) ** (-...  45.4 us
    all_to_all x3, starting transfers between devices, exchange(): return lax.all_to_all(array, both, split_axis=0, concat_axis=0, tiled=True)  24.3 us
    pallas_call x1, Pallas kernels, per_device(): call(functools.partial(expert_down_kernel, caps), (wide_shape, narrow_sha...  18.6 us
    dot_general x3, matrix products, weight_grad(): product = lax.dot_general(left, right, FIRST, preferred_element_type=F32)  17.8 us
    pallas_call x2, Pallas kernels, send(): call(kernel, jax.ShapeDtypeStruct((rows, CHUNKS, LANES), BF16), moved=600...  12.7 us
    pallas_call x1, Pallas kernels, per_device(): call(expert_up_kernel, (wide_shape, narrow_shape, narrow_shape, narrow_sh...  11.7 us
    pallas_call x1, Pallas kernels, per_device(): call(combine_kernel, (jax.ShapeDtypeStruct((tokens, width), BF16), jax.Sh...  9.53 us
  transfers between devices with their start and end apart: 3, of which 3 were waited for; matrix products, arithmetic and copies ran while one was open for 7% of the time, Pallas kernels for 8%

profile of v6, /device:TPU:1, one launch (start us, length us, event | category | flops | bytes accessed | tf_op | source)
XLA Modules:
  0.0 299.4 jit_solution(14088862388676780718)
XLA Ops:
  0.6 1.9 shard_map.232
  2.6 6.1 %shard_map.234 = bf16[1280,16,128]{2,1,0:T(8,128)(2,1)} custom-call(s32[16,128]{1,0:T(8,128)} %get-tuple-element.40.table_ref, bf16[128,2048]{1,0:T(8,128)(2,1)} %hidden_ref.1, bf16[16,128]{1,0:T(8,128)(2,1)} %bitcast.33, bf16[256,256]{1,0:T(8,128)(2,1)} %constant.3.clone.swap_ref), custom_call_target="tpu_custom_call" | custom-call | bytes 6000000 | tf_op jit(solution)/shard_map/pallas_call | solution.py:617
  8.7 0.0 copy-start.1
  8.7 11.9 %all-to-all-start.1 = ((bf16[128,160,128]{2,1,0:T(8,128)(2,1)}), bf16[128,160,128]{2,1,0:T(8,128)(2,1)}, u32[]{:S(2)}, u32[]{:S(2)}) async-start(bf16[128,160,128]{2,1,0:T(8,128)(2,1)} %bitcast.27), calls=%async_computation.1 | async-start | bytes 10485760 | tf_op jit(solution)/shard_map/all_to_all | solution.py:614
  20.6 0.0 copy-done.1
  20.6 0.9 copy.27
  21.5 6.6 %shard_map.233 = bf16[1280,16,128]{2,1,0:T(8,128)(2,1)} custom-call(s32[16,128]{1,0:T(8,128)} %get-tuple-element.40.table_ref, f32[16,128]{1,0:T(8,128)} %get-tuple-element.41.scale_ref, bf16[128,16,128]{2,1,0:T(8,128)(2,1)} %bitcast.28), custom_call_target="tpu_custom_call" | custom-call | bytes 6000000 | tf_op jit(solution)/shard_map/pallas_call | solution.py:617
  28.1 55.0 %all-to-all-done.1 = bf16[128,160,128]{2,1,0:T(8,128)(2,1)} async-done(((bf16[128,160,128]{2,1,0:T(8,128)(2,1)}), bf16[128,160,128]{2,1,0:T(8,128)(2,1)}, u32[]{:S(2)}, u32[]{:S(2)}) %all-to-all-start.1) | async-done | bytes 5242912 | tf_op jit(solution)/shard_map/all_to_all | solution.py:614
  83.1 0.0 copy-start.2
  83.1 0.0 copy-start
  83.1 6.2 %all-to-all-start = ((bf16[128,160,128]{2,1,0:T(8,128)(2,1)}), bf16[128,160,128]{2,1,0:T(8,128)(2,1)}, u32[]{:S(2)}, u32[]{:S(2)}) async-start(bf16[128,160,128]{2,1,0:T(8,128)(2,1)} %bitcast.26), calls=%async_computation | async-start | bytes 10485760 | tf_op jit(solution)/shard_map/all_to_all | solution.py:614
  89.3 0.0 copy-done.2
  89.3 1.0 copy.26.begin_ref
  90.3 0.0 copy-done
  90.3 0.9 copy.28
  91.2 4.9 %shard_map.235 = bf16[2,2,512,512]{3,2,1,0:T(8,128)(2,1)} custom-call(bf16[1024,256]{1,0:T(8,128)(2,1)} %query_hbm.1, bf16[1024,256]{1,0:T(8,128)(2,1)} %key_hbm.1, s32[1024,1]{1,0:T(8,128)} %copy.26.begin_ref), custom_call_target="tpu_custom_call" | custom-call | flops 10000000000 | bytes 5000000 | tf_op jit(solution)/shard_map/pallas_call | solution.py:642
  96.1 11.7 %shard_map.236 = (bf16[1280,2048]{1,0:T(8,128)(2,1)}, bf16[1280,512]{1,0:T(8,128)(2,1)}, bf16[1280,512]{1,0:T(8,128)(2,1)}, bf16[1280,512]{1,0:T(8,128)(2,1)}) custom-call(bf16[20480,128]{1,0:T(8,128)(2,1)} %bitcast.6.tile_ref, bf16[256,256]{1,0:T(8,128)(2,1)} %constant.3.clone.swap_ref, bf16[1,2048,512]{2,1,0:T(8,128)(2,1)} %gate_w_ref.3, ...), custom_call_target="tpu_custom_call" | custom-call | flops 5368709120 | bytes 18000000 | tf_op jit(solution)/shard_map/pallas_call | solution.py:662
  107.9 43.9 %all-to-all-done = bf16[128,160,128]{2,1,0:T(8,128)(2,1)} async-done(((bf16[128,160,128]{2,1,0:T(8,128)(2,1)}), bf16[128,160,128]{2,1,0:T(8,128)(2,1)}, u32[]{:S(2)}, u32[]{:S(2)}) %all-to-all-start) | async-done | bytes 5242912 | tf_op jit(solution)/shard_map/all_to_all | solution.py:614
  151.8 18.6 %shard_map.237 = (bf16[1280,2048]{1,0:T(8,128)(2,1)}, bf16[1280,512]{1,0:T(8,128)(2,1)}, bf16[1280,512]{1,0:T(8,128)(2,1)}, bf16[128,168,128]{2,1,0:T(8,128)(2,1)}) custom-call(bf16[20480,128]{1,0:T(8,128)(2,1)} %bitcast.3.tile_ref, bf16[256,256]{1,0:T(8,128)(2,1)} %constant.3.clone.swap_ref, bf16[32,320]{1,0:T(8,128)(2,1)} %constant.10.clone.gather_ref, ...), custom_call_target="tpu_custom_call" | custom-call | flops 8053063680 | bytes 25000000 | tf_op jit(solution)/shard_map/pallas_call | solution.py:675
  170.4 0.0 copy-start.3
  170.4 6.2 %all-to-all-start.2 = ((bf16[128,168,128]{2,1,0:T(8,128)(2,1)}), bf16[128,168,128]{2,1,0:T(8,128)(2,1)}, u32[]{:S(2)}, u32[]{:S(2)}) async-start(bf16[128,168,128]{2,1,0:T(8,128)(2,1)} %get-tuple-element.46), calls=%async_computation.2 | async-start | bytes 11010048 | tf_op jit(solution)/shard_map/all_to_all | solution.py:614
  176.6 0.0 copy-done.3
  176.6 0.0 copy-start.5
  176.6 0.0 slice-start
  176.7 6.7 %fusion.2 = bf16[1,512,2048]{2,1,0:T(8,128)(2,1)} fusion(bf16[1280,512]{1,0:T(8,128)(2,1)S(1)} %copy-done.3, bf16[1280,2048]{1,0:T(8,128)(2,1)} %get-tuple-element.50), kind=kOutput, calls=%fused_computation.5 | convolution fusion | flops 2686451712 | bytes 8650752 | tf_op jit(solution)/shard_map/dot_general | solution.py:710
  183.4 0.0 copy-done.5
  183.4 0.0 slice-start.1
  183.4 0.0 copy-start.4
  183.4 6.9 %fusion = bf16[1,2048,512]{2,1,0:T(8,128)(2,1)} fusion(bf16[1280,2048]{1,0:T(8,128)(2,1)} %get-tuple-element.47, bf16[1280,512]{1,0:T(8,128)(2,1)S(1)} %copy-done.5), kind=kOutput, calls=%fused_computation.3 | convolution fusion | flops 2686451712 | bytes 8650752 | tf_op jit(solution)/shard_map/dot_general | solution.py:710
  190.3 0.0 slice-done
  190.3 0.0 slice-done.1
  190.3 0.0 copy-done.4
  190.3 4.1 %fusion.1 = bf16[1,2048,512]{2,1,0:T(8,128)(2,1)} fusion(bf16[1280,2048]{1,0:T(8,128)(2,1)S(1)} %bitcast.44, bf16[1280,512]{1,0:T(8,128)(2,1)S(1)} %copy-done.4), kind=kOutput, calls=%fused_computation.4 | convolution fusion | flops 2686451712 | bytes 8650752 | tf_op jit(solution)/shard_map/dot_general | solution.py:710
  194.4 47.5 %all-to-all-done.2.back_hbm = bf16[128,168,128]{2,1,0:T(8,128)(2,1)} async-done(((bf16[128,168,128]{2,1,0:T(8,128)(2,1)}), bf16[128,168,128]{2,1,0:T(8,128)(2,1)}, u32[]{:S(2)}, u32[]{:S(2)}) %all-to-all-start.2) | async-done | bytes 5505056 | tf_op jit(solution)/shard_map/all_to_all | solution.py:614
  241.9 9.5 %shard_map.238 = (bf16[128,2048]{1,0:T(8,128)(2,1)}, bf16[128,128]{1,0:T(8,128)(2,1)}) custom-call(s32[8,128]{1,0:T(8,128)} %bitcast.36, s32[8,128]{1,0:T(8,128)} %get-tuple-element.39.slot_ref, bf16[128,168,128]{2,1,0:T(8,128)(2,1)} %all-to-all-done.2.back_hbm, bf16[128,16,128]{2,1,0:T(8,128)(2,1)} %bitcast.31, bf16[128,16,128]{2,1,0:T(8,128)(2,1)} %bitcast.29, ...), custom_call_target="tpu_custom_call" | custom-call | bytes 8000000 | tf_op jit(solution)/shard_map/pallas_call | solution.py:720
  251.5 45.4 %shard_map.239 = (bf16[1024,256]{1,0:T(8,128)(2,1)}, bf16[1024,256]{1,0:T(8,128)(2,1)}, bf16[1024,256]{1,0:T(8,128)(2,1)}, bf16[128,256]{1,0:T(8,128)(2,1)}, bf16[8,128]{1,0:T(8,128)(2,1)}) custom-call(bf16[128,2048]{1,0:T(8,128)(2,1)} %get-tuple-element.34.resid_hbm, bf16[2048,256]{1,0:T(8,128)(2,1)} %weight_hbm.1, bf16[1024,256]{1,0:T(8,128)(2,1)} %attn_hbm.1, ...), custom_call_target="tpu_custom_call" | custom-call | flops 4000000000 | bytes 20000000 | tf_op jit(solution)/shard_map/pallas_call | solution.py:751
  296.9 2.3 shard_map.240
  (1 shorter events, 0.0 us)
Async XLA Ops:
  8.7 11.9 %copy-start.1 = (bf16[128,2048]{1,0:T(8,128)(2,1)S(1)}, bf16[128,2048]{1,0:T(8,128)(2,1)}, u32[]{:S(2)}) copy-start(bf16[128,2048]{1,0:T(8,128)(2,1)} %param.18) | copy-start | bytes 1572868
  8.7 74.4 %all-to-all-start.1 = ((bf16[128,160,128]{2,1,0:T(8,128)(2,1)}), bf16[128,160,128]{2,1,0:T(8,128)(2,1)}, u32[]{:S(2)}, u32[]{:S(2)}) async-start(bf16[128,160,128]{2,1,0:T(8,128)(2,1)} %bitcast.27), calls=%async_computation.1 | async-start | bytes 10485760 | tf_op jit(solution)/shard_map/all_to_all | solution.py:614
  83.1 6.2 %copy-start.2 = (s32[1024]{0:T(1024)S(1)}, s32[1024]{0:T(1024)}, u32[]{:S(2)}) copy-start(s32[1024]{0:T(1024)} %param.30) | copy-start | bytes 12292
  83.1 7.2 %copy-start = (bf16[128,2048]{1,0:T(8,128)(2,1)S(1)}, bf16[128,2048]{1,0:T(8,128)(2,1)}, u32[]{:S(2)}) copy-start(bf16[128,2048]{1,0:T(8,128)(2,1)} %hidden_ref.1) | copy-start | bytes 1572868
  83.1 68.7 %all-to-all-start = ((bf16[128,160,128]{2,1,0:T(8,128)(2,1)}), bf16[128,160,128]{2,1,0:T(8,128)(2,1)}, u32[]{:S(2)}, u32[]{:S(2)}) async-start(bf16[128,160,128]{2,1,0:T(8,128)(2,1)} %bitcast.26), calls=%async_computation | async-start | bytes 10485760 | tf_op jit(solution)/shard_map/all_to_all | solution.py:614
  170.4 6.2 %copy-start.3 = (bf16[1280,512]{1,0:T(8,128)(2,1)S(1)}, bf16[1280,512]{1,0:T(8,128)(2,1)}, u32[]{:S(2)}) copy-start(bf16[1280,512]{1,0:T(8,128)(2,1)} %get-tuple-element.43.act_ref) | copy-start | bytes 3932164
  170.4 71.5 %all-to-all-start.2 = ((bf16[128,168,128]{2,1,0:T(8,128)(2,1)}), bf16[128,168,128]{2,1,0:T(8,128)(2,1)}, u32[]{:S(2)}, u32[]{:S(2)}) async-start(bf16[128,168,128]{2,1,0:T(8,128)(2,1)} %get-tuple-element.46), calls=%async_computation.2 | async-start | bytes 11010048 | tf_op jit(solution)/shard_map/all_to_all | solution.py:614
  176.6 6.8 %copy-start.5 = (bf16[1280,512]{1,0:T(8,128)(2,1)S(1)}, bf16[1280,512]{1,0:T(8,128)(2,1)}, u32[]{:S(2)}) copy-start(bf16[1280,512]{1,0:T(8,128)(2,1)} %get-tuple-element.48) | copy-start | bytes 3932164
  176.6 13.7 %slice-start = ((s8[5242880]{0:T(1024)(128)(4,1)}), s8[4194304]{0:T(1024)(128)(4,1)S(1)}, s32[]{:S(2)}) async-start(s8[5242880]{0:T(1024)(128)(4,1)} %bitcast.43), calls=%async_computation.3 | async-start | bytes 8388608
  183.4 6.9 %slice-start.1 = ((s8[5242880]{0:T(1024)(128)(4,1)}), s8[1048576]{0:T(1024)(128)(4,1)S(1)}, s32[]{:S(2)}) async-start(s8[5242880]{0:T(1024)(128)(4,1)} %bitcast.43), calls=%async_computation.4 | async-start | bytes 2097152
  183.4 6.9 %copy-start.4 = (bf16[1280,512]{1,0:T(8,128)(2,1)S(1)}, bf16[1280,512]{1,0:T(8,128)(2,1)}, u32[]{:S(2)}) copy-start(bf16[1280,512]{1,0:T(8,128)(2,1)} %get-tuple-element.49) | copy-start | bytes 3932164
